TPU v7x, 32 devices: a whole 2x2x4 slice. The times are simulated.
32 devices in a mesh: stream: 2 (over x), dp: 16 (over z, y, core).
Axes of the slice: x: 2, y: 2, z: 4, core: 2. Of those that a mesh axis runs over, the one named last changes fastest.
Arguments:
- hidden: bfloat16 [2, 384, 36, 768], P('stream', 'dp'), may hold values from -6 to 6
- lengths: int32 [2, 384], P('stream', 'dp'), may hold values from 4 to 36, as said below
- task_flags: int32 [2, 384], P('stream', 'dp'), may hold values 0 or 1
- cotangent: bfloat16 [2, 384, 36, 768], P('stream', 'dp'), may hold values from -6 to 6
- cross_proj: bfloat16 [768, 2304], replicated, may hold values from -0.21875 to 0.21875
- cross_bias: float32 [3, 768], replicated, may hold values from -3 to 3
- cross_norm: float32 [2, 768], replicated, may hold values from 0.25 to 1.75
- cross_out: bfloat16 [768, 768], replicated, may hold values from -0.875 to 0.875
- self_proj: bfloat16 [2, 768, 2304], P('stream'), may hold values from -0.21875 to 0.21875
- self_bias: float32 [2, 3, 768], P('stream'), may hold values from -3 to 3
- self_norm: float32 [2, 2, 768], P('stream'), may hold values from 0.25 to 1.75
- self_out: bfloat16 [2, 768, 768], P('stream'), may hold values from -0.875 to 0.875
- ffn_up: bfloat16 [2, 768, 3072], P('stream'), may hold values from -0.21875 to 0.21875
- up_bias: float32 [2, 3072], P('stream'), may hold values from -3 to 3
- ffn_down: bfloat16 [2, 3072, 768], P('stream'), may hold values from -0.109375 to 0.109375
- down_bias: float32 [2, 768], P('stream'), may hold values from -3 to 3
- ffn_norm: float32 [2, 2, 768], P('stream'), may hold values from 0.25 to 1.75
Outputs:
- output: bfloat16 [2, 384, 36, 768], P('stream', 'dp')
- grad_hidden: bfloat16 [2, 384, 36, 768], P('stream', 'dp')
- grad_cross_proj: float32 [768, 2304], P(('stream', 'dp'))
- grad_cross_bias: float32 [3, 768], P(None, ('stream', 'dp'))
- grad_cross_norm: float32 [2, 768], P(None, ('stream', 'dp'))
- grad_cross_out: float32 [768, 768], P(('stream', 'dp'))
- grad_self_proj: float32 [2, 768, 2304], P('stream', 'dp')
- grad_self_bias: float32 [2, 3, 768], P('stream', None, 'dp')
- grad_self_norm: float32 [2, 2, 768], P('stream', None, 'dp')
- grad_self_out: float32 [2, 768, 768], P('stream', 'dp')
- grad_ffn_up: float32 [2, 768, 3072], P('stream', 'dp')
- grad_up_bias: float32 [2, 3072], P('stream', 'dp')
- grad_ffn_down: float32 [2, 3072, 768], P('stream', 'dp')
- grad_down_bias: float32 [2, 768], P('stream', 'dp')
- grad_ffn_norm: float32 [2, 2, 768], P('stream', None, 'dp')
Inputs may be any that keep to these rules, and one draw needn't show every extreme that they name: `lengths`: stream 0 (words) has 4 to 20 live slots an item and some item has exactly 20; stream 1 (regions) has 12 to 36 and some item has exactly 36.
All inputs are finite; a program needn't handle non-finite values. No bound on the sum of `task_flags` on one device may be relied on, other than what follows from the above.
Results may differ from a plain program's by a relative error of at most 0.02.
Values may be sent and summed in bfloat16 or wider, within the bound.
A program may use at most 192 MiB of HBM per device.

v0:
```python
import jax
import jax.numpy as jnp
from jax import lax
from jax.sharding import PartitionSpec as P

HEADS = 12
HEAD_DIM = 64


norm_eps = 1e-06
masked_score = -1000000000.0


def swapped(block, axis, distance):
    count = lax.axis_size(axis)
    route = []
    for low in range(count):
        high = low | 1 << distance
        if high != low and high < count:
            route += [(low, high), (high, low)]
    return lax.ppermute(block, axis, route)


def project(rows, weight):
    return jnp.dot(rows, weight, preferred_element_type=jnp.float32)


def project_back(rows, weight):
    return lax.dot_general(
        rows, weight, (((1,), (1,)), ((), ())), preferred_element_type=jnp.float32
    )


def weight_grad(inputs, grads):
    return lax.dot_general(
        inputs, grads, (((0,), (0,)), ((), ())), preferred_element_type=jnp.float32
    )


def column_sum(grads):
    return jnp.sum(grads.astype(jnp.float32), axis=0)


def norm_forward(summed, norm_gain, norm_shift):
    centred = summed - jnp.mean(summed, axis=-1, keepdims=True)
    scaled = lax.rsqrt(jnp.mean(centred * centred, axis=-1, keepdims=True) + norm_eps)
    normed = centred * scaled
    return (normed * norm_gain + norm_shift, normed, scaled)


def norm_backward(upstream, normed, scaled, norm_gain):
    inner = upstream * norm_gain
    grad_sum = scaled * (
        inner
        - jnp.mean(inner, axis=-1, keepdims=True)
        - normed * jnp.mean(inner * normed, axis=-1, keepdims=True)
    )
    return (grad_sum, jnp.sum(upstream * normed, axis=0), jnp.sum(upstream, axis=0))


def split_heads(rows, items):
    return rows.reshape(items, -1, HEADS, HEAD_DIM)


def masked_scores(queries, key_rows, key_len):
    scores = jnp.einsum(
        "bqhd,bkhd->bhqk", queries, key_rows, preferred_element_type=jnp.float32
    ) * HEAD_DIM ** (-0.5)
    slot_index = jnp.arange(key_rows.shape[1], dtype=jnp.float32)
    allowed = slot_index[None, :] < key_len.astype(jnp.float32)[:, None]
    return jnp.where(allowed[:, None, None, :], scores, masked_score)


def attend_forward(queries, key_rows, value_rows, key_len):
    items = key_len.shape[0]
    scores = masked_scores(split_heads(queries, items), split_heads(key_rows, items), key_len)
    largest = jnp.max(scores, axis=-1, keepdims=True)
    exponent = jnp.exp(scores - largest)
    total = jnp.sum(exponent, axis=-1, keepdims=True)
    context = jnp.einsum(
        "bhqk,bkhd->bqhd",
        (exponent / total).astype(jnp.bfloat16),
        split_heads(value_rows, items),
        preferred_element_type=jnp.float32,
    )
    return (context.reshape(-1, HEADS * HEAD_DIM), largest + jnp.log(total))


def attend_backward(queries, key_rows, value_rows, key_len, log_total, grad_context):
    items = key_len.shape[0]
    query_heads = split_heads(queries, items)
    key_heads = split_heads(key_rows, items)
    value_heads = split_heads(value_rows, items)
    grad_heads = split_heads(grad_context, items)
    probs = jnp.exp(masked_scores(query_heads, key_heads, key_len) - log_total)
    grad_probs = jnp.einsum(
        "bqhd,bkhd->bhqk", grad_heads, value_heads, preferred_element_type=jnp.float32
    )
    grad_scores = probs * (grad_probs - jnp.sum(probs * grad_probs, axis=-1, keepdims=True))
    rounded = grad_scores.astype(jnp.bfloat16)
    factor = HEAD_DIM ** (-0.5)
    grad_queries = (
        jnp.einsum("bhqk,bkhd->bqhd", rounded, key_heads, preferred_element_type=jnp.float32)
        * factor
    ).astype(jnp.bfloat16)
    grad_keys = (
        jnp.einsum("bhqk,bqhd->bkhd", rounded, query_heads, preferred_element_type=jnp.float32)
        * factor
    ).astype(jnp.bfloat16)
    grad_values = jnp.einsum(
        "bhqk,bqhd->bkhd",
        probs.astype(jnp.bfloat16),
        grad_heads,
        preferred_element_type=jnp.float32,
    ).astype(jnp.bfloat16)
    width = HEADS * HEAD_DIM
    return (
        grad_queries.reshape(-1, width),
        grad_keys.reshape(-1, width),
        grad_values.reshape(-1, width),
    )


def local(
    hidden,
    lengths,
    task_flags,
    cotangent,
    cross_proj,
    cross_bias,
    cross_norm,
    cross_out,
    self_proj,
    self_bias,
    self_norm,
    self_out,
    ffn_up,
    up_bias,
    ffn_down,
    down_bias,
    ffn_norm,
):
    items = hidden.shape[1]
    slots = hidden.shape[2]
    width = hidden.shape[3]
    inputs = hidden[0].reshape(items * slots, width)
    own_len = lengths[0].astype(jnp.bfloat16)
    blank_row = jnp.zeros((width,), jnp.float32)
    query_weight = cross_proj[:, :width]
    pair_weight = cross_proj[:, width:]
    pair_bias = jnp.concatenate([blank_row, cross_bias[1]])
    queries = (project(inputs, query_weight) + cross_bias[0]).astype(jnp.bfloat16)
    own_pair = (project(inputs, pair_weight) + pair_bias).astype(jnp.bfloat16)
    far_pair, far_len = swapped((own_pair, own_len), "stream", 0)
    context, cross_total = attend_forward(
        queries, far_pair[:, :width], far_pair[:, width:], far_len
    )
    context = context.astype(jnp.bfloat16)
    crossed, cross_normed, cross_scale = norm_forward(
        project(context, cross_out) + cross_bias[2] + inputs.astype(jnp.float32),
        cross_norm[0],
        cross_norm[1],
    )
    crossed_low = crossed.astype(jnp.bfloat16)
    triple = project(crossed_low, self_proj[0]) + jnp.concatenate(
        [self_bias[0, 0], blank_row, self_bias[0, 1]]
    )
    triple = triple.astype(jnp.bfloat16)
    self_context, self_total = attend_forward(
        triple[:, :width], triple[:, width : 2 * width], triple[:, 2 * width :], own_len
    )
    self_context = self_context.astype(jnp.bfloat16)
    attended, mid_normed, mid_scale = norm_forward(
        project(self_context, self_out[0]) + self_bias[0, 2] + crossed,
        self_norm[0, 0],
        self_norm[0, 1],
    )
    attended_low = attended.astype(jnp.bfloat16)
    expanded = project(attended_low, ffn_up[0]) + up_bias[0]
    activated, gelu_back = jax.vjp(
        lambda entries: jax.nn.gelu(entries, approximate=False), expanded
    )
    activated_low = activated.astype(jnp.bfloat16)
    final, last_normed, last_scale = norm_forward(
        project(activated_low, ffn_down[0]) + down_bias[0] + attended,
        ffn_norm[0, 0],
        ffn_norm[0, 1],
    )
    output = final.astype(jnp.bfloat16).reshape(1, items, slots, width)
    live_rows = (jnp.arange(slots)[None, :] < lengths[0][:, None]) & (task_flags[0][:, None] > 0)
    upstream = cotangent[0].reshape(items * slots, width).astype(jnp.float32) * live_rows.reshape(
        -1, 1
    ).astype(jnp.float32)
    grad_last, grad_ffn_gain, grad_ffn_shift = norm_backward(
        upstream, last_normed, last_scale, ffn_norm[0, 0]
    )
    grad_last_low = grad_last.astype(jnp.bfloat16)
    grad_down = weight_grad(activated_low, grad_last_low)
    grad_down_bias = column_sum(grad_last_low)
    (grad_expanded,) = gelu_back(project_back(grad_last_low, ffn_down[0]))
    grad_expanded_low = grad_expanded.astype(jnp.bfloat16)
    grad_up = weight_grad(attended_low, grad_expanded_low)
    grad_up_bias = column_sum(grad_expanded_low)
    grad_attended = grad_last + project_back(grad_expanded_low, ffn_up[0])
    ffn_norm_grad = jnp.stack([grad_ffn_gain, grad_ffn_shift], axis=1)
    grad_mid, grad_mid_gain, grad_mid_shift = norm_backward(
        grad_attended, mid_normed, mid_scale, self_norm[0, 0]
    )
    grad_mid_low = grad_mid.astype(jnp.bfloat16)
    grad_self_out = weight_grad(self_context, grad_mid_low)
    grad_self_context = project_back(grad_mid_low, self_out[0]).astype(jnp.bfloat16)
    grad_self_query, grad_self_key, grad_self_value = attend_backward(
        triple[:, :width],
        triple[:, width : 2 * width],
        triple[:, 2 * width :],
        own_len,
        self_total,
        grad_self_context,
    )
    grad_triple = jnp.concatenate([grad_self_query, grad_self_key, grad_self_value], axis=1)
    grad_self_proj = weight_grad(crossed_low, grad_triple)
    self_vector_grad = jnp.stack(
        [column_sum(grad_self_query), column_sum(grad_self_value), column_sum(grad_mid_low)], axis=1
    )
    self_norm_grad = jnp.stack([grad_mid_gain, grad_mid_shift], axis=1)
    grad_crossed = grad_mid + project_back(grad_triple, self_proj[0])
    grad_cross, grad_cross_gain, grad_cross_shift = norm_backward(
        grad_crossed, cross_normed, cross_scale, cross_norm[0]
    )
    grad_cross_low = grad_cross.astype(jnp.bfloat16)
    grad_cross_out = weight_grad(context, grad_cross_low)
    grad_context = project_back(grad_cross_low, cross_out).astype(jnp.bfloat16)
    again_pair, again_len = swapped((own_pair, own_len), "stream", 0)
    grad_queries, grad_far_keys, grad_far_values = attend_backward(
        queries, again_pair[:, :width], again_pair[:, width:], again_len, cross_total, grad_context
    )
    grad_pair = swapped(jnp.concatenate([grad_far_keys, grad_far_values], axis=1), "stream", 0)
    grad_pair_weight = weight_grad(inputs, grad_pair)
    grad_value_bias = column_sum(grad_pair[:, width:])
    grad_inputs = (
        grad_cross + project_back(grad_queries, query_weight) + project_back(grad_pair, pair_weight)
    )
    grad_hidden = grad_inputs.astype(jnp.bfloat16).reshape(1, items, slots, width)
    grad_cross_proj = jnp.concatenate([weight_grad(inputs, grad_queries), grad_pair_weight], axis=1)
    cross_vector_grad = jnp.stack(
        [column_sum(grad_queries), grad_value_bias, column_sum(grad_cross_low)], axis=1
    )
    cross_norm_grad = jnp.stack([grad_cross_gain, grad_cross_shift], axis=1)
    cross_shares = (
        lax.psum_scatter(grad_cross_proj, ("stream", "dp"), scatter_dimension=0, tiled=True),
        lax.psum_scatter(cross_vector_grad, ("stream", "dp"), scatter_dimension=0, tiled=True),
        lax.psum_scatter(cross_norm_grad, ("stream", "dp"), scatter_dimension=0, tiled=True),
        lax.psum_scatter(grad_cross_out, ("stream", "dp"), scatter_dimension=0, tiled=True),
    )
    stream_shares = (
        lax.psum_scatter(grad_up, "dp", scatter_dimension=0, tiled=True),
        lax.psum_scatter(grad_up_bias, "dp", scatter_dimension=0, tiled=True),
        lax.psum_scatter(grad_down, "dp", scatter_dimension=0, tiled=True),
        lax.psum_scatter(grad_down_bias, "dp", scatter_dimension=0, tiled=True),
        lax.psum_scatter(ffn_norm_grad, "dp", scatter_dimension=0, tiled=True),
        lax.psum_scatter(grad_self_proj, "dp", scatter_dimension=0, tiled=True),
        lax.psum_scatter(self_vector_grad, "dp", scatter_dimension=0, tiled=True),
        lax.psum_scatter(self_norm_grad, "dp", scatter_dimension=0, tiled=True),
        lax.psum_scatter(grad_self_out, "dp", scatter_dimension=0, tiled=True),
    )
    ffn_shares = stream_shares[:5]
    self_shares = stream_shares[5:]
    return (
        output,
        grad_hidden,
        cross_shares[0],
        cross_shares[1].T,
        cross_shares[2].T,
        cross_shares[3],
        self_shares[0][None],
        self_shares[1].T[None],
        self_shares[2].T[None],
        self_shares[3][None],
        ffn_shares[0][None],
        ffn_shares[1][None],
        ffn_shares[2][None],
        ffn_shares[3][None],
        ffn_shares[4].T[None],
    )


def solution(mesh):
    in_specs = (
        P("stream", "dp", None, None),
        P("stream", "dp"),
        P("stream", "dp"),
        P("stream", "dp", None, None),
        P(),
        P(),
        P(),
        P(),
        P("stream", None, None),
        P("stream", None, None),
        P("stream", None, None),
        P("stream", None, None),
        P("stream", None, None),
        P("stream", None),
        P("stream", None, None),
        P("stream", None),
        P("stream", None, None),
    )
    out_specs = (
        P("stream", "dp", None, None),
        P("stream", "dp", None, None),
        P(("stream", "dp"), None),
        P(None, ("stream", "dp")),
        P(None, ("stream", "dp")),
        P(("stream", "dp"), None),
        P("stream", "dp", None),
        P("stream", None, "dp"),
        P("stream", None, "dp"),
        P("stream", "dp", None),
        P("stream", "dp", None),
        P("stream", "dp"),
        P("stream", "dp", None),
        P("stream", "dp"),
        P("stream", None, "dp"),
    )
    return jax.shard_map(local, mesh=mesh, in_specs=in_specs, out_specs=out_specs, check_vma=False)
```

profile of v0, /device:TPU:0, one launch (start us, length us, event | category | flops | bytes accessed | tf_op | source)
XLA Modules:
  0.0 1084.7 jit_solution(14404740229683934657)
XLA Ops:
  14.6 5.9 add_convert_fusion.2
  52.2 29.1 %collective-permute-done.1 = bf16[24]{0:T(256)(128)(2,1)} collective-permute-done((bf16[24]{0:T(256)(128)(2,1)}, bf16[24]{0:T(256)(128)(2,1)}, u32[]{:S(2)}, u32[]{:S(2)}) %collective-permute-start.1) | collective-permute-done | bytes 80 | tf_op jit(solution)/shard_map/ppermute | solution.py:21
  110.4 5.5 convert_element_type.196
  156.2 5.5 convert_element_type.204
  166.6 31.2 %multiply_convert_fusion = (bf16[864,3072]{1,0:T(8,128)(2,1)S(1)}, f32[864,3072]{1,0:T(8,128)}, f32[864,3072]{1,0:T(8,128)}) fusion(f32[3072]{0:T(1024)S(1)} %bitcast.133, bf16[1,768,3072]{2,1,0:T(8,128)(2,1)} %param.29, f32[864,768]{1,0:T(8,128)S(1)} %get-tuple-element.141, f32[768]{0:T(1024)S(1)} %copy-done.33, f32[768]{0:T(1024)S(1)} %copy-done.31, ...), kind=kOutput, calls=%fused_computation.4 | convolution fusion | flops 4255358976 | bytes 33940224 | tf_op jit(solution)/shard_map/dot_general | solution.py:25
  208.1 16.0 %convert_reduce_fusion = (f32[3072]{0:T(1024)}, bf16[864,3072]{1,0:T(8,128)(2,1)}) fusion(f32[864,3072]{1,0:T(8,128)} %get-tuple-element.125, bf16[1,3072,768]{2,1,0:T(8,128)(2,1)} %param.31, f32[864,768]{1,0:T(8,128)S(1)} %get-tuple-element.119, f32[864,3072]{1,0:T(8,128)} %get-tuple-element.142, f32[3072]{0:T(1024)S(1)} %bitcast.134), kind=kOutput, calls=%fused_computation.2 | convolution fusion | flops 4122645504 | bytes 33939456 | tf_op jit(solution)/shard_map/dot_general | solution.py:29
  224.2 9.6 multiply_reduce_fusion.3
  239.1 5.5 reshape.293
  244.7 7.6 multiply_reduce_fusion.1
  252.3 6.5 convert_reduce_fusion.1
  258.9 6.2 multiply_convert_fusion.6
  282.2 16.1 %reshape.295 = bf16[864,768]{1,0:T(8,128)(2,1)} reshape(bf16[24,36,12,64]{3,2,1,0:T(8,128)(2,1)} %copy.182) | data formatting | bytes 2654208 | tf_op jit(solution)/shard_map/reshape | solution.py:119
  302.8 5.5 reshape.294
  315.3 5.5 reshape.296
  326.1 8.1 multiply_reduce_fusion.4
  357.3 10.0 fusion.100
  371.8 5.7 reshape.297
  378.7 7.8 multiply_reduce_fusion
  397.0 5.5 reshape.299
  410.5 5.7 reshape.300
  428.6 5.5 reshape.298
  437.5 41.4 %collective-permute-done.2 = bf16[864,1536]{1,0:T(8,128)(2,1)} collective-permute-done((bf16[864,1536]{1,0:T(8,128)(2,1)}, bf16[864,1536]{1,0:T(8,128)(2,1)}, u32[]{:S(2)}, u32[]{:S(2)}) %collective-permute-start.2) | collective-permute-done | bytes 2654240 | tf_op jit(solution)/shard_map/ppermute | solution.py:21
  486.8 8.1 copy.202
  495.6 10.7 fusion.97
  506.3 10.3 fusion.94
  527.6 59.6 %all-reduce.6 = (f32[3072]{0:T(1024)}, f32[768]{0:T(1024)S(1)}) all-reduce(f32[3072]{0:T(1024)} %get-tuple-element.157, f32[768]{0:T(1024)S(1)} %copy-done.42), channel_id=11, replica_groups=mesh['stream'=2,'dp'=16] {'dp'}, use_global_device_ids=true, to_apply=%region_38.39.clone | all-reduce | flops 3840 | bytes 30720
  600.5 7.4 add_convert_fusion.3
  614.4 37.6 %all-reduce.5 = (f32[768,3]{0,1:T(4,128)}, f32[768,2]{0,1:T(2,128)}) all-reduce(f32[768,3]{0,1:T(4,128)S(1)} %pad_maximum_fusion.3, f32[768,2]{0,1:T(2,128)} %pad_maximum_fusion.5), channel_id=3, replica_groups=mesh['stream'=2,'dp'=16] {'stream','dp'}, use_global_device_ids=true, to_apply=%region_22.23.clone | all-reduce | flops 3840 | bytes 30720
  654.6 66.6 %reduce-scatter.22.cloned.1.call-done = f32[48,2304]{1,0:T(8,128)} async-done(((f32[768,2304]{1,0:T(8,128)}), f32[48,2304]{1,0:T(8,128)}) %reduce-scatter.22.cloned.1.call-update) | async-done | bytes 442384 | tf_op jit(solution)/shard_map/reduce_scatter | solution.py:261
  721.3 124.9 %reduce-scatter.30.cloned.1.call-done = f32[24,2304]{1,0:T(8,128)} async-done(((f32[768,2304]{1,0:T(8,128)}), f32[24,2304]{1,0:T(8,128)}) %reduce-scatter.30.cloned.1.call-update) | async-done | bytes 221200
  846.2 115.9 %reduce-scatter.26.cloned.1.call-done = f32[48,3072]{1,0:T(8,128)} async-done(((f32[768,3072]{1,0:T(8,128)}), f32[48,3072]{1,0:T(8,128)}) %reduce-scatter.26.cloned.1.call-update) | async-done | bytes 589840 | tf_op jit(solution)/shard_map/reduce_scatter | solution.py:256
  962.1 115.8 %reduce-scatter.28.cloned.1.call-done = f32[192,768]{1,0:T(8,128)} async-done(((f32[3072,768]{1,0:T(8,128)}), f32[192,768]{1,0:T(8,128)}) %reduce-scatter.28.cloned.1.call-update) | async-done | bytes 589840 | tf_op jit(solution)/shard_map/reduce_scatter | solution.py:258
  (282 shorter events, 265.9 us)
Async XLA Ops:
  7.2 112.7 %copy-start = (bf16[1,768,2304]{2,1,0:T(8,128)(2,1)S(1)}, bf16[1,768,2304]{2,1,0:T(8,128)(2,1)}, u32[]{:S(2)}) copy-start(bf16[1,768,2304]{2,1,0:T(8,128)(2,1)} %param.25) | copy-start | bytes 10616836
  7.2 587.0 %reduce-scatter.36.cloned.1.call-start = ((), (), s32[]{:S(2)}) async-start(), calls=%async_computation.17 | async-start | bytes 417792
  14.6 9.3 copy-start.58
  20.4 61.6 %collective-permute-start = (bf16[864,1536]{1,0:T(8,128)(2,1)}, bf16[864,1536]{1,0:T(8,128)(2,1)}, u32[]{:S(2)}, u32[]{:S(2)}) collective-permute-start(bf16[864,1536]{1,0:T(8,128)(2,1)} %add_convert_fusion.2), channel_id=1, source_target_pairs={{0,16},{16,0},{1,17},{17,1},{2,18},{18,2},{3,19},{19,3},{4,20},{20... | collective-permute-start | bytes 7962632 | tf_op jit(solution)/shard_map/ppermute | solution.py:21
  23.9 57.4 %collective-permute-start.1 = (bf16[24]{0:T(256)(128)(2,1)}, bf16[24]{0:T(256)(128)(2,1)}, u32[]{:S(2)}, u32[]{:S(2)}) collective-permute-start(bf16[24]{0:T(256)(128)(2,1)} %get-tuple-element.132), channel_id=1, source_target_pairs={{0,16},{16,0},{1,17},{17,1},{2,18},{18,2},{3,19},{19,3},{4,20},{20... | collective-permute-start | bytes 152 | tf_op jit(solution)/shard_map/ppermute | solution.py:21
  49.5 112.3 %copy-start.27 = (f32[768]{0:T(1024)}, f32[768]{0:T(1024)S(1)}, u32[]{:S(2)}) copy-start(f32[768]{0:T(1024)S(1)} %get-tuple-element.112) | copy-start | bytes 9220
  49.5 112.2 %copy-start.30 = (f32[768]{0:T(1024)}, f32[768]{0:T(1024)S(1)}, u32[]{:S(2)}) copy-start(f32[768]{0:T(1024)S(1)} %get-tuple-element.113) | copy-start | bytes 9220
  119.4 42.4 %copy-start.25 = (f32[864]{0:T(1024)}, f32[864]{0:T(1024)S(1)}, u32[]{:S(2)}) copy-start(f32[864]{0:T(1024)S(1)} %broadcast_multiply_fusion.8) | copy-start | bytes 10372
  119.9 41.9 %copy-start.29 = (f32[864]{0:T(1024)}, f32[864]{0:T(1024)S(1)}, u32[]{:S(2)}) copy-start(f32[864]{0:T(1024)S(1)} %add_rsqrt_fusion.2) | copy-start | bytes 10372
  161.8 36.0 %slice-start.2 = ((s8[4718592]{0:T(1024)(128)(4,1)}), s8[4194304]{0:T(1024)(128)(4,1)S(1)}, s32[]{:S(2)}) async-start(s8[4718592]{0:T(1024)(128)(4,1)} %bitcast.127), calls=%async_computation.20 | async-start | bytes 8388608
  166.0 67.7 %copy-start.3 = (f32[864,768]{1,0:T(8,128)}, f32[864,768]{1,0:T(8,128)S(1)}, u32[]{:S(2)}) copy-start(f32[864,768]{1,0:T(8,128)S(1)} %get-tuple-element.141) | copy-start | bytes 7962628
  166.6 31.3 %copy-start.52 = (f32[768]{0:T(1024)S(1)}, f32[768]{0:T(1024)}, u32[]{:S(2)}) copy-start(f32[768]{0:T(1024)} %reduce.15) | copy-start | bytes 9220
  166.6 31.3 %slice-start.3 = ((s8[4718592]{0:T(1024)(128)(4,1)}), s8[524288]{0:T(1024)(128)(4,1)S(1)}, s32[]{:S(2)}) async-start(s8[4718592]{0:T(1024)(128)(4,1)} %bitcast.127), calls=%async_computation.21 | async-start | bytes 1048576
  208.1 16.0 %copy-start.20 = (f32[864,768]{1,0:T(8,128)}, f32[864,768]{1,0:T(8,128)S(1)}, u32[]{:S(2)}) copy-start(f32[864,768]{1,0:T(8,128)S(1)} %get-tuple-element.119) | copy-start | bytes 7962628
  275.2 320.3 %reduce-scatter.34.cloned.1.call-start = ((), (), s32[]{:S(2)}) async-start(), calls=%async_computation.16 | async-start | bytes 417792
  315.3 10.8 copy-start.26
  315.3 10.8 copy-start.28
  326.1 9.3 copy-start.46
  326.1 9.3 copy-start.47
  326.1 9.9 copy-start.41
  341.0 256.0 %reduce-scatter.32.cloned.1.call-start = ((), (), s32[]{:S(2)}) async-start(), calls=%async_computation.15 | async-start | bytes 417792
  344.0 310.7 %reduce-scatter.20.cloned.1.call-start = ((), (), s32[]{:S(2)}) async-start(), calls=%async_computation.9 | async-start | bytes 2433024 | tf_op jit(solution)/shard_map/reduce_scatter | solution.py:253
  352.2 302.5 %reduce-scatter.24.cloned.1.call-start = ((), (), s32[]{:S(2)}) async-start(), calls=%async_computation.11 | async-start | bytes 2506752 | tf_op jit(solution)/shard_map/reduce_scatter | solution.py:264
  357.3 364.0 %reduce-scatter.22.cloned.1.call-start = ((), (), s32[]{:S(2)}) async-start(), calls=%async_computation.10 | async-start | bytes 7520256 | tf_op jit(solution)/shard_map/reduce_scatter | solution.py:261
  367.3 478.8 %reduce-scatter.30.cloned.1.call-start = ((), (), s32[]{:S(2)}) async-start(), calls=%async_computation.14 | async-start | bytes 7299072
  377.4 9.1 slice-start
  419.8 59.0 %collective-permute-start.2 = (bf16[864,1536]{1,0:T(8,128)(2,1)}, bf16[864,1536]{1,0:T(8,128)(2,1)}, u32[]{:S(2)}, u32[]{:S(2)}) collective-permute-start(bf16[864,1536]{1,0:T(8,128)(2,1)} %pad_maximum_fusion.1), channel_id=1, source_target_pairs={{0,16},{16,0},{1,17},{17,1},{2,18},{18,2},{3,19},{19,3},{4,20},{20... | collective-permute-start | bytes 7962632 | tf_op jit(solution)/shard_map/ppermute | solution.py:21
  434.2 44.7 %copy-start.21 = (bf16[864,768]{1,0:T(8,128)(2,1)S(1)}, bf16[864,768]{1,0:T(8,128)(2,1)}, u32[]{:S(2)}) copy-start(bf16[864,768]{1,0:T(8,128)(2,1)} %reshape_squeeze.4) | copy-start | bytes 3981316
  494.9 467.2 %reduce-scatter.26.cloned.1.call-start = ((), (), s32[]{:S(2)}) async-start(), calls=%async_computation.12 | async-start | bytes 10027008 | tf_op jit(solution)/shard_map/reduce_scatter | solution.py:256
  506.3 571.6 %reduce-scatter.28.cloned.1.call-start = ((), (), s32[]{:S(2)}) async-start(), calls=%async_computation.13 | async-start | bytes 10027008 | tf_op jit(solution)/shard_map/reduce_scatter | solution.py:258
  516.7 8.9 copy-start.40
  516.7 10.9 %copy-start.42 = (f32[768]{0:T(1024)S(1)}, f32[768]{0:T(1024)}, u32[]{:S(2)}) copy-start(f32[768]{0:T(1024)} %get-tuple-element.118) | copy-start | bytes 9220
  (45 other events, 193.8 us)
Sparse Core Ops, SparseCore 0:
  275.3 57.1 reduce-scatter.35
  341.1 57.0 reduce-scatter.33
  401.7 54.5 reduce-scatter.31
  462.9 98.0 reduce-scatter.19
  565.2 62.0 reduce-scatter.23
  632.2 88.9 reduce-scatter.21
  727.5 118.6 reduce-scatter.29
  851.4 110.6 reduce-scatter.25
  966.8 111.0 reduce-scatter.27
where the time goes:
time: 1090 us; the launch traced here: 1080 us
  waiting for transfers between devices  494 us (45%)
  matrix products  217 us (20%)
  local copies, waits for them, and re-layouts  210 us (19%)
  blocking collectives  97.2 us (9%)
  other arithmetic  44.6 us (4%)
  between operations  16.1 us (1%)
    unnamed x13, waiting for transfers between devices  125 us
    reduce_scatter x1, waiting for transfers between devices, local(): lax.psum_scatter(grad_up, 'dp', scatter_dimension=0, tiled=True)  116 us
    reduce_scatter x1, waiting for transfers between devices, local(): lax.psum_scatter(grad_down, 'dp', scatter_dimension=0, tiled=True)  116 us
    unnamed x2, blocking collectives  97.2 us
    ppermute x3, waiting for transfers between devices, swapped(): return lax.ppermute(block, axis, route)  70.5 us
    reduce_scatter x1, waiting for transfers between devices, local(): lax.psum_scatter(grad_self_proj, 'dp', scatter_dimension=0, tiled=True)  66.6 us
    dot_general x7, matrix products, project(): return jnp.dot(rows, weight, preferred_element_type=jnp.float32)  57.1 us
    dot_general x7, matrix products, project_back(): lax.dot_general(rows, weight, (((1,), (1,)), ((), ())), preferred_element...  52.2 us
  transfers between devices with their start and end apart: 12, of which 6 were waited for; matrix products, arithmetic and copies ran while one was open for 24% of the time, Pallas kernels for 0%

commit v1 on v0

v1 whole, which is shorter than its diff:
```python
import functools

import jax
import jax.numpy as jnp
from jax import lax
from jax.experimental import pallas as pl
from jax.experimental.pallas import tpu as pltpu
from jax.sharding import PartitionSpec as P

HEADS = 12
HEAD_DIM = 64
PAIRS = HEADS // 2
LANES = 2 * HEAD_DIM

norm_eps = 1e-06
masked_score = -1000000000.0
vmem_limit = 60 * 1024 * 1024

f32 = jnp.float32
bf16 = jnp.bfloat16


def dot(left, right):
    return jnp.dot(left, right, preferred_element_type=f32)


def dot_nt(left, right):
    return lax.dot_general(left, right, (((1,), (1,)), ((), ())), preferred_element_type=f32)


def dot_tn(left, right):
    return lax.dot_general(left, right, (((0,), (0,)), ((), ())), preferred_element_type=f32)


def norm_parts(summed):
    centred = summed - jnp.mean(summed, axis=-1, keepdims=True)
    scaled = lax.rsqrt(jnp.mean(centred * centred, axis=-1, keepdims=True) + norm_eps)
    return centred * scaled, scaled


def norm_backward(upstream, normed, scaled, gain):
    inner = upstream * gain
    return scaled * (
        inner
        - jnp.mean(inner, axis=-1, keepdims=True)
        - normed * jnp.mean(inner * normed, axis=-1, keepdims=True)
    )


def row_sum(rows):
    return jnp.sum(rows, axis=0, keepdims=True)


def gelu_parts(entries):
    size = jnp.abs(entries)
    bell = jnp.exp(entries * entries * -0.5)
    t = 1.0 / (1.0 + size * (0.3275911 * 0.7071067811865476))
    poly = t * (
        0.5 * 0.254829592
        + t
        * (
            0.5 * -0.284496736
            + t * (0.5 * 1.421413741 + t * (0.5 * -1.453152027 + t * (0.5 * 1.061405429)))
        )
    )
    tail = poly * bell
    area = jnp.where(entries >= 0.0, 1.0 - tail, tail)
    return entries * area, area + entries * bell * 0.3989422804014327


def densify(dense_ref, block_ref, items, slots):
    for item in range(items):
        dense_ref[item * slots : (item + 1) * slots, :] = block_ref[0, item].astype(f32)


def pair_mask(len_ref, first, slots):
    shape = (2 * slots, 2 * slots)
    row = lax.broadcasted_iota(jnp.int32, shape, 0)
    col = lax.broadcasted_iota(jnp.int32, shape, 1)
    far_row = row >= slots
    low = jnp.where(far_row, slots, 0)
    high = jnp.where(far_row, slots + len_ref[0, first + 1], len_ref[0, first])
    allowed = (col >= low) & (col < high)
    return jnp.concatenate([allowed, allowed], axis=0)


def head_stack(rows):
    lane = lax.broadcasted_iota(jnp.int32, rows.shape, 1)
    return jnp.concatenate(
        [jnp.where(lane < HEAD_DIM, rows, 0.0), jnp.where(lane < HEAD_DIM, 0.0, rows)], axis=0
    ).astype(bf16)


def head_merge(stacked):
    count = stacked.shape[0] // 2
    lane = lax.broadcasted_iota(jnp.int32, (count, stacked.shape[1]), 1)
    return jnp.where(lane < HEAD_DIM, stacked[:count], stacked[count:])


def attend(triple_ref, context_ref, probs_ref, len_ref, first_item, items, slots):
    span = 2 * slots
    width = HEADS * HEAD_DIM

    def unit(u, carry):
        rows = pl.ds(pl.multiple_of(u * 2 * span, 2 * span), 2 * span)
        masks = [pair_mask(len_ref, first_item + 4 * u + 2 * g, slots) for g in range(2)]
        for pair in range(PAIRS):
            at = pair * LANES
            queries = triple_ref[rows, at : at + LANES].astype(f32) * HEAD_DIM**-0.5
            keys = triple_ref[rows, width + at : width + at + LANES].astype(f32)
            values = triple_ref[rows, 2 * width + at : 2 * width + at + LANES].astype(f32)
            merged = []
            for g in range(2):
                part = slice(g * span, (g + 1) * span)
                scores = dot_nt(head_stack(queries[part]), keys[part].astype(bf16))
                scores = jnp.where(masks[g], scores, masked_score)
                exponent = jnp.exp(scores - jnp.max(scores, axis=-1, keepdims=True))
                probs = exponent * (1.0 / jnp.sum(exponent, axis=-1, keepdims=True))
                probs = probs.astype(bf16)
                probs_ref[2 * u + g, pair] = probs
                merged.append(head_merge(dot(probs, values[part].astype(bf16))))
            context_ref[rows, at : at + LANES] = jnp.concatenate(merged, axis=0).astype(bf16)
        return carry

    lax.fori_loop(0, items // 4, unit, 0)


def attend_back(triple_ref, probs_ref, grad_ref, grad_triple_ref, row_base, items, slots):
    span = 2 * slots
    width = HEADS * HEAD_DIM

    def unit(u, carry):
        rows = pl.ds(pl.multiple_of(u * 2 * span, 2 * span), 2 * span)
        out_rows = pl.ds(pl.multiple_of(row_base + u * 2 * span, 2 * span), 2 * span)
        for pair in range(PAIRS):
            at = pair * LANES
            queries = triple_ref[rows, at : at + LANES].astype(f32) * HEAD_DIM**-0.5
            keys = triple_ref[rows, width + at : width + at + LANES].astype(f32)
            values = triple_ref[rows, 2 * width + at : 2 * width + at + LANES].astype(f32)
            grads = grad_ref[rows, at : at + LANES].astype(f32)
            merged = [[], [], []]
            for g in range(2):
                part = slice(g * span, (g + 1) * span)
                key_low = keys[part].astype(bf16)
                query_stack = head_stack(queries[part])
                grad_stack = head_stack(grads[part])
                probs = probs_ref[2 * u + g, pair]
                wide = probs.astype(f32)
                grad_probs = dot_nt(grad_stack, values[part].astype(bf16))
                product = wide * grad_probs
                grad_scores = product - wide * jnp.sum(product, axis=-1, keepdims=True)
                grad_scores = grad_scores.astype(bf16)
                merged[0].append(head_merge(dot(grad_scores, key_low)) * HEAD_DIM**-0.5)
                merged[1].append(dot_tn(grad_scores, query_stack))
                merged[2].append(dot_tn(probs, grad_stack))
            for part in range(3):
                grad_triple_ref[out_rows, part * width + at : part * width + at + LANES] = (
                    jnp.concatenate(merged[part], axis=0).astype(bf16)
                )
        return carry

    lax.fori_loop(0, items // 4, unit, 0)


def forward_kernel(
    items, slots,
    far_len, own_len, hidden, far, cross_proj, cross_bias, cross_norm, cross_out, self_proj, self_bias, self_norm, self_out,
    dense, far_dense, triple1, probs1, context1, normed1, scale1, triple2, probs2, context2, normed2, scale2,
    wide, far_wide,
):
    width = HEADS * HEAD_DIM
    first = pl.program_id(0) * items
    densify(wide, hidden, items, slots)
    densify(far_wide, far, items, slots)
    low = wide[...].astype(bf16)
    dense[...] = low
    far_low = far_wide[...].astype(bf16)
    far_dense[...] = far_low
    triple1[:, :width] = (dot(low, cross_proj[:, :width]) + cross_bias[0:1]).astype(bf16)
    triple1[:, width : 2 * width] = dot(far_low, cross_proj[:, width : 2 * width]).astype(bf16)
    triple1[:, 2 * width :] = (dot(far_low, cross_proj[:, 2 * width :]) + cross_bias[1:2]).astype(bf16)
    attend(triple1, context1, probs1, far_len, first, items, slots)
    normed, scale = norm_parts(dot(context1[...], cross_out[...]) + cross_bias[2:3] + wide[...])
    normed1[...] = normed
    scale1[...] = scale
    crossed = normed * cross_norm[0:1] + cross_norm[1:2]
    wide[...] = crossed
    low = crossed.astype(bf16)
    triple2[:, :width] = (dot(low, self_proj[0, :, :width]) + self_bias[0, 0:1]).astype(bf16)
    triple2[:, width : 2 * width] = dot(low, self_proj[0, :, width : 2 * width]).astype(bf16)
    triple2[:, 2 * width :] = (dot(low, self_proj[0, :, 2 * width :]) + self_bias[0, 1:2]).astype(bf16)
    attend(triple2, context2, probs2, own_len, first, items, slots)
    normed, scale = norm_parts(dot(context2[...], self_out[0]) + self_bias[0, 2:3] + wide[...])
    normed2[...] = normed
    scale2[...] = scale


def ffn_kernel(
    items, slots,
    own_len, flags, normed2, cotangent, self_norm, ffn_up, up_bias, ffn_down, down_bias, ffn_norm,
    output, grad_attended, attended_low, activated, grad_last_low, grad_expanded, up_sum, vec_sum,
    slope, wide,
):
    width = HEADS * HEAD_DIM
    chunks = ffn_up.shape[2] // width
    step = pl.program_id(0)
    first = step * items

    @pl.when(step == 0)
    def _():
        up_sum[...] = jnp.zeros_like(up_sum)
        vec_sum[...] = jnp.zeros_like(vec_sum)

    attended = normed2[...] * self_norm[0, 0:1] + self_norm[0, 1:2]
    low = attended.astype(bf16)
    attended_low[...] = low
    total = attended + down_bias[...]
    for chunk in range(chunks):
        at = slice(chunk * width, (chunk + 1) * width)
        active, rise = gelu_parts(dot(low, ffn_up[0, :, at]) + up_bias[:, at])
        active = active.astype(bf16)
        activated[:, at] = active
        slope[:, at] = rise
        total = total + dot(active, ffn_down[0, at, :])
    normed, scale = norm_parts(total)
    wide[...] = normed * ffn_norm[0, 0:1] + ffn_norm[0, 1:2]
    for item in range(items):
        output[0, item] = wide[item * slots : (item + 1) * slots, :].astype(bf16)
    slot = lax.broadcasted_iota(jnp.int32, (slots, width), 0)
    for item in range(items):
        live = jnp.where(flags[0, first + item] > 0, own_len[0, first + item], 0)
        wide[item * slots : (item + 1) * slots, :] = jnp.where(
            slot < live, cotangent[0, item].astype(f32), 0.0
        )
    upstream = wide[...]
    grad_last = norm_backward(upstream, normed, scale, ffn_norm[0, 0:1])
    grad_low = grad_last.astype(bf16)
    grad_last_low[...] = grad_low
    vec_sum[0:1] += row_sum(grad_low.astype(f32))
    vec_sum[1:2] += row_sum(upstream * normed)
    vec_sum[2:3] += row_sum(upstream)
    total = grad_last
    for chunk in range(chunks):
        at = slice(chunk * width, (chunk + 1) * width)
        grad_up = (dot_nt(grad_low, ffn_down[0, at, :]) * slope[:, at]).astype(bf16)
        grad_expanded[:, at] = grad_up
        up_sum[:, at] += row_sum(grad_up.astype(f32))
        total = total + dot_nt(grad_up, ffn_up[0, :, at])
    grad_attended[...] = total


def self_back_kernel(
    items, slots,
    grad_attended, normed2, scale2, normed1, triple2, probs2, cross_norm, self_norm, self_proj, self_out,
    grad_crossed, crossed_low, grad_mid_low, grad_triple, vec_sum,
    grad_context,
):
    width = HEADS * HEAD_DIM

    @pl.when(pl.program_id(0) == 0)
    def _():
        vec_sum[...] = jnp.zeros_like(vec_sum)

    upstream = grad_attended[...]
    normed = normed2[...]
    grad_mid = norm_backward(upstream, normed, scale2[...], self_norm[0, 0:1])
    low = grad_mid.astype(bf16)
    grad_mid_low[...] = low
    vec_sum[2:3] += row_sum(low.astype(f32))
    vec_sum[3:4] += row_sum(upstream * normed)
    vec_sum[4:5] += row_sum(upstream)
    grad_context[...] = dot_nt(low, self_out[0]).astype(bf16)
    attend_back(triple2, probs2, grad_context, grad_triple, 0, items, slots)
    vec_sum[0:1] += row_sum(grad_triple[:, :width].astype(f32))
    vec_sum[1:2] += row_sum(grad_triple[:, 2 * width :].astype(f32))
    crossed_low[...] = (normed1[...] * cross_norm[0:1] + cross_norm[1:2]).astype(bf16)
    grad_crossed[...] = grad_mid + dot_nt(grad_triple[...], self_proj[0])


def cross_back_kernel(
    items, slots,
    grad_crossed, normed1, scale1, triple1, probs1, cross_norm, cross_proj, cross_out,
    grad_own, grad_far, grad_cross_low, grad_triple, vec_sum,
    grad_context,
):
    width = HEADS * HEAD_DIM

    @pl.when(pl.program_id(0) == 0)
    def _():
        vec_sum[...] = jnp.zeros_like(vec_sum)

    upstream = grad_crossed[...]
    normed = normed1[...]
    grad_cross = norm_backward(upstream, normed, scale1[...], cross_norm[0:1])
    low = grad_cross.astype(bf16)
    grad_cross_low[...] = low
    vec_sum[2:3] += row_sum(low.astype(f32))
    vec_sum[3:4] += row_sum(upstream * normed)
    vec_sum[4:5] += row_sum(upstream)
    grad_context[...] = dot_nt(low, cross_out[...]).astype(bf16)
    attend_back(triple1, probs1, grad_context, grad_triple, 0, items, slots)
    vec_sum[0:1] += row_sum(grad_triple[:, :width].astype(f32))
    vec_sum[1:2] += row_sum(grad_triple[:, 2 * width :].astype(f32))
    grad_far[...] = dot_nt(grad_triple[:, width:], cross_proj[:, width:]).astype(bf16)
    grad_own[...] = grad_cross + dot_nt(grad_triple[:, :width], cross_proj[:, :width])


def finish_kernel(items, slots, own, far, grad_hidden, wide):
    wide[...] = own[...] + far[...].astype(f32)
    for item in range(items):
        grad_hidden[0, item] = wide[item * slots : (item + 1) * slots, :].astype(bf16)


def weight_grad_kernel(left, right, product, turned):
    @pl.when(pl.program_id(1) == 0)
    def _():
        turned[...] = left[...].T

    product[...] = dot(turned[...], right[...]).astype(bf16)


def weight_grad(left, right, at=0):
    rows, deep = left.shape
    block = HEADS * HEAD_DIM
    wide = right.shape[1] - at * block
    return pl.pallas_call(
        weight_grad_kernel,
        grid=(deep // block, wide // block),
        in_specs=[
            pl.BlockSpec((rows, block), lambda i, j: (0, i)),
            pl.BlockSpec((rows, block), lambda i, j: (0, j + at)),
        ],
        out_specs=pl.BlockSpec((block, block), lambda i, j: (i, j)),
        out_shape=jax.ShapeDtypeStruct((deep, wide), bf16),
        scratch_shapes=[pltpu.VMEM((block, rows), bf16)],
        compiler_params=pltpu.CompilerParams(vmem_limit_bytes=vmem_limit),
        cost_estimate=pl.CostEstimate(
            flops=2 * rows * deep * wide,
            bytes_accessed=2 * (rows * deep + rows * wide + deep * wide),
            transcendentals=0,
        ),
    )(left, right)


smem = pl.BlockSpec(memory_space=pltpu.SMEM)


def fixed(array):
    zeros = (0,) * array.ndim
    return pl.BlockSpec(array.shape, lambda i: zeros, pipeline_mode=pl.Buffered(1))


def rows_of(count, width):
    return pl.BlockSpec((count, width), lambda i: (i, 0))


def total_of(count, width):
    return pl.BlockSpec((count, width), lambda i: (0, 0))


def shape_of(shape, kind):
    return jax.ShapeDtypeStruct(shape, kind)


def flip(count, bit):
    return [(place, place ^ (1 << bit)) for place in range(count)]


def halve(parts, axis, bit, dim):
    mine = (lax.axis_index(axis) >> bit) & 1
    send = lax.dynamic_index_in_dim(parts, 1 - mine, dim, keepdims=False)
    keep = lax.dynamic_index_in_dim(parts, mine, dim, keepdims=False)
    return keep, lax.ppermute(send, axis, flip(lax.axis_size(axis), bit))


def scatter_sum(parts, axis, kind, other=None):
    count = lax.axis_size(axis)
    bits = count.bit_length() - 1
    stages = [(axis, bit) for bit in range(bits)]
    if other is not None:
        stages.insert(1, (other, 0))
    for number, (name, bit) in enumerate(stages):
        if name == other:
            keep, got = halve(parts, other, 0, 0)
        elif other is not None and number == 0:
            shape = parts.shape
            keep, got = halve(parts.reshape((shape[0], shape[1] // 2, 2) + shape[2:]), axis, bit, 2)
        else:
            shape = parts.shape
            keep, got = halve(parts.reshape((shape[0] // 2, 2) + shape[1:]), axis, bit, 1)
        summed = keep.astype(f32) + got.astype(f32)
        parts = summed if number == len(stages) - 1 else summed.astype(kind)
    return parts[0]


def local(
    hidden, lengths, task_flags, cotangent, cross_proj, cross_bias, cross_norm, cross_out, self_proj, self_bias,
    self_norm, self_out, ffn_up, up_bias, ffn_down, down_bias, ffn_norm,
):
    _, items, slots, width = hidden.shape
    deep = ffn_up.shape[2]
    rows = items * slots
    streams, places = lax.axis_size("stream"), lax.axis_size("dp")
    block = 8 if items % 8 == 0 else 4
    steps = items // block
    size = block * slots
    groups = items // 2
    item_spec = pl.BlockSpec((1, block, slots, width), lambda i: (0, i, 0, 0))
    probs_spec = pl.BlockSpec((block // 2, PAIRS, 4 * slots, 2 * slots), lambda i: (i, 0, 0, 0))
    row_spec = rows_of(size, width)
    scale_spec = rows_of(size, 1)
    triple_spec = rows_of(size, 3 * width)
    deep_spec = rows_of(size, deep)
    row_f32, row_bf16 = shape_of((rows, width), f32), shape_of((rows, width), bf16)
    scale_f32 = shape_of((rows, 1), f32)
    triple_bf16, deep_bf16 = shape_of((rows, 3 * width), bf16), shape_of((rows, deep), bf16)
    probs_bf16 = shape_of((groups, PAIRS, 4 * slots, 2 * slots), bf16)
    params = pltpu.CompilerParams(vmem_limit_bytes=vmem_limit)
    unit = 2 * rows * width * width

    def cost(units, count):
        return pl.CostEstimate(flops=units * unit, bytes_accessed=count, transcendentals=0)

    far, far_len = (lax.ppermute(entry, "stream", flip(streams, 0)) for entry in (hidden, lengths))

    (dense, far_dense, triple1, probs1, context1, normed1, scale1, triple2, probs2, context2, normed2, scale2) = pl.pallas_call(
        functools.partial(forward_kernel, block, slots),
        grid=(steps,),
        in_specs=[smem, smem, item_spec, item_spec]
        + [fixed(w) for w in (cross_proj, cross_bias, cross_norm, cross_out, self_proj, self_bias, self_norm, self_out)],
        out_specs=[row_spec, row_spec, triple_spec, probs_spec, row_spec, row_spec, scale_spec, triple_spec, probs_spec, row_spec, row_spec, scale_spec],
        out_shape=[row_bf16, row_bf16, triple_bf16, probs_bf16, row_bf16, row_f32, scale_f32, triple_bf16, probs_bf16, row_bf16, row_f32, scale_f32],
        scratch_shapes=[pltpu.VMEM((size, width), f32)] * 2,
        compiler_params=params,
        cost_estimate=cost(12, 30_000_000),
    )(far_len, lengths, hidden, far, cross_proj, cross_bias, cross_norm, cross_out, self_proj, self_bias, self_norm, self_out)

    output, grad_attended, attended_low, activated, grad_last_low, grad_expanded, up_sum, ffn_sum = pl.pallas_call(
        functools.partial(ffn_kernel, block, slots),
        grid=(steps,),
        in_specs=[smem, smem, row_spec, item_spec] + [fixed(w) for w in (self_norm, ffn_up, up_bias, ffn_down, down_bias, ffn_norm)],
        out_specs=[item_spec, row_spec, row_spec, deep_spec, row_spec, deep_spec, total_of(1, deep), total_of(3, width)],
        out_shape=[shape_of(hidden.shape, bf16), row_f32, row_bf16, deep_bf16, row_bf16, deep_bf16, shape_of((1, deep), f32), shape_of((3, width), f32)],
        scratch_shapes=[pltpu.VMEM((size, deep), f32), pltpu.VMEM((size, width), f32)],
        compiler_params=params,
        cost_estimate=cost(24, 30_000_000),
    )(lengths, task_flags, normed2, cotangent, self_norm, ffn_up, up_bias, ffn_down, down_bias, ffn_norm)

    grad_up = weight_grad(attended_low, grad_expanded)
    grad_down = weight_grad(activated, grad_last_low)

    grad_crossed, crossed_low, grad_mid_low, grad_triple2, self_sum = pl.pallas_call(
        functools.partial(self_back_kernel, block, slots),
        grid=(steps,),
        in_specs=[row_spec, row_spec, scale_spec, row_spec, triple_spec, probs_spec] + [fixed(w) for w in (cross_norm, self_norm, self_proj, self_out)],
        out_specs=[row_spec, row_spec, row_spec, triple_spec, total_of(5, width)],
        out_shape=[row_f32, row_bf16, row_bf16, triple_bf16, shape_of((5, width), f32)],
        scratch_shapes=[pltpu.VMEM((size, width), bf16)],
        compiler_params=params,
        cost_estimate=cost(8, 30_000_000),
    )(grad_attended, normed2, scale2, normed1, triple2, probs2, cross_norm, self_norm, self_proj, self_out)

    grad_self_proj = weight_grad(crossed_low, grad_triple2)
    grad_self_out = weight_grad(context2, grad_mid_low)

    grad_own, grad_far, grad_cross_low, grad_triple1, cross_sum = pl.pallas_call(
        functools.partial(cross_back_kernel, block, slots),
        grid=(steps,),
        in_specs=[row_spec, row_spec, scale_spec, triple_spec, probs_spec] + [fixed(w) for w in (cross_norm, cross_proj, cross_out)],
        out_specs=[row_spec, row_spec, row_spec, triple_spec, total_of(5, width)],
        out_shape=[row_f32, row_bf16, row_bf16, triple_bf16, shape_of((5, width), f32)],
        scratch_shapes=[pltpu.VMEM((size, width), bf16)],
        compiler_params=params,
        cost_estimate=cost(8, 30_000_000),
    )(grad_crossed, normed1, scale1, triple1, probs1, cross_norm, cross_proj, cross_out)

    grad_got = lax.ppermute(grad_far, "stream", flip(streams, 0))
    grad_cross_proj = jnp.concatenate([weight_grad(dense, grad_triple1[:, :width]), weight_grad(far_dense, grad_triple1, 1)], axis=1)
    grad_cross_out = weight_grad(context1, grad_cross_low)

    (grad_hidden,) = pl.pallas_call(
        functools.partial(finish_kernel, block, slots),
        grid=(steps,),
        in_specs=[row_spec, row_spec],
        out_specs=[item_spec],
        out_shape=[shape_of(hidden.shape, bf16)],
        scratch_shapes=[pltpu.VMEM((size, width), f32)],
        compiler_params=params,
        cost_estimate=cost(0, 8_000_000),
    )(grad_own, grad_got)

    def share(parts, kind=bf16):
        return scatter_sum(parts.reshape((places, parts.shape[0] // places) + parts.shape[1:]), "dp", kind)

    def share_all(parts, kind=bf16):
        return scatter_sum(
            parts.reshape((streams, places, parts.shape[0] // places // streams) + parts.shape[1:]), "dp", kind, "stream"
        )

    own_up, own_down = share(grad_up), share(grad_down)
    own_self_proj, own_self_out = share(grad_self_proj), share(grad_self_out)
    own_cross_proj, own_cross_out = share_all(grad_cross_proj), share_all(grad_cross_out)
    per = width // places
    up_rows = up_sum.reshape(places, deep // places)
    small = jnp.concatenate(
        [up_rows, ffn_sum.reshape(3, places, per).transpose(1, 0, 2).reshape(places, 3 * per),
         self_sum.reshape(5, places, per).transpose(1, 0, 2).reshape(places, 5 * per)], axis=1)
    small = share(small.reshape(places, -1), f32)[0]
    cut = deep // places
    small_up, small_vec = small[:cut], small[cut:].reshape(8, per)
    cross_small = cross_sum.reshape(5, streams * places, per // streams).transpose(1, 0, 2).reshape(streams * places, -1)
    cross_small = share_all(cross_small, f32)[0].reshape(5, per // streams)
    return (
        output,
        grad_hidden,
        own_cross_proj,
        cross_small[0:3],
        cross_small[3:5],
        own_cross_out,
        own_self_proj[None],
        small_vec[None, 3:6],
        small_vec[None, 6:8],
        own_self_out[None],
        own_up[None],
        small_up[None],
        own_down[None],
        small_vec[0][None],
        small_vec[None, 1:3],
    )


def solution(mesh):
    in_specs = (
        P("stream", "dp", None, None),
        P("stream", "dp"),
        P("stream", "dp"),
        P("stream", "dp", None, None),
        P(),
        P(),
        P(),
        P(),
        P("stream", None, None),
        P("stream", None, None),
        P("stream", None, None),
        P("stream", None, None),
        P("stream", None, None),
        P("stream", None),
        P("stream", None, None),
        P("stream", None),
        P("stream", None, None),
    )
    out_specs = (
        P("stream", "dp", None, None),
        P("stream", "dp", None, None),
        P(("stream", "dp"), None),
        P(None, ("stream", "dp")),
        P(None, ("stream", "dp")),
        P(("stream", "dp"), None),
        P("stream", "dp", None),
        P("stream", None, "dp"),
        P("stream", None, "dp"),
        P("stream", "dp", None),
        P("stream", "dp", None),
        P("stream", "dp"),
        P("stream", "dp", None),
        P("stream", "dp"),
        P("stream", None, "dp"),
    )
    return jax.shard_map(local, mesh=mesh, in_specs=in_specs, out_specs=out_specs, check_vma=False)
```

time: 1090 us -> 510 us (0.47)
  waiting for transfers between devices: 494 us -> 214 us
  matrix products: 217 us -> 0 us
  Pallas kernels: 0 us -> 188 us
  local copies, waits for them, and re-layouts: 210 us -> 40.2 us
  blocking collectives: 97.2 us -> 0 us
  starting transfers between devices: 5.05 us -> 36.5 us
  other arithmetic: 44.6 us -> 24 us
  between operations: 16.1 us -> 1.51 us
    reduce_scatter x5 -> x0, waiting for transfers between devices: 298 us -> none  [the longest x1 116 us: local(): lax.psum_scatter(grad_up, 'dp', scatter_dimension=0, tiled=True)]
    dot_general x33 -> x0, matrix products: 217 us -> none  [the longest x7 57.1 us: project(): return jnp.dot(rows, weight, preferred_element_type=jnp.float32)]
    pallas_call x0 -> x12, Pallas kernels: none -> 188 us  [the longest x7 44.7 us: weight_grad(): pl.pallas_call(weight_grad_kernel, grid=(deep // block, wide // block), i...]
    ppermute x3 -> x38, waiting for transfers between devices: 70.5 us -> 214 us  [the longest x35 189 us: halve(): return (keep, lax.ppermute(send, axis, flip(lax.axis_size(axis), bit)))]
    unnamed x13 -> x0, waiting for transfers between devices: 125 us -> none
    unnamed x2 -> x0, blocking collectives: 97.2 us -> none
    reshape x16 -> x6, local copies, waits for them, and re-layouts: 92.6 us -> 1.75 us  [the longest x1 0.84 us: local(): cross_sum.reshape(5, streams * places, per // streams).transpose(1, 0, 2)]
    convert_element_type x14 -> x0, local copies, waits for them, and re-layouts: 45.6 us -> none  [the longest x2 8.07 us: local(): self_context = self_context.astype(jnp.bfloat16)]
  transfers between devices with their start and end apart: 12 -> 38, of which waited for: 6 -> 19; matrix products, arithmetic and copies ran while one was open for 24% -> 12% of each run, Pallas kernels for 0% -> 22%
where the time goes in v1:
time: 510 us; the launch traced here: 504 us
  waiting for transfers between devices  214 us (42%)
  Pallas kernels  188 us (37%)
  local copies, waits for them, and re-layouts  40.2 us (8%)
  starting transfers between devices  36.5 us (7%)
  other arithmetic  24 us (5%)
    ppermute x35, waiting for transfers between devices, halve(): return (keep, lax.ppermute(send, axis, flip(lax.axis_size(axis), bit)))  189 us
    pallas_call x7, Pallas kernels, weight_grad(): pl.pallas_call(weight_grad_kernel, grid=(deep // block, wide // block), i...  44.7 us
    pallas_call x1, Pallas kernels, local(): pl.pallas_call(functools.partial(forward_kernel, block, slots), grid=(ste...  36.1 us
    pallas_call x1, Pallas kernels, local(): pl.pallas_call(functools.partial(self_back_kernel, block, slots), grid=(s...  36 us
    pallas_call x1, Pallas kernels, local(): pl.pallas_call(functools.partial(cross_back_kernel, block, slots), grid=(...  35.4 us
    ppermute x35, starting transfers between devices, halve(): return (keep, lax.ppermute(send, axis, flip(lax.axis_size(axis), bit)))  31.9 us
    pallas_call x1, Pallas kernels, local(): pl.pallas_call(functools.partial(ffn_kernel, block, slots), grid=(steps,)...  31.6 us
    ppermute x2, waiting for transfers between devices, local(): lax.ppermute(entry, 'stream', flip(streams, 0))  24.6 us
  transfers between devices with their start and end apart: 38, of which 19 were waited for; matrix products, arithmetic and copies ran while one was open for 12% of the time, Pallas kernels for 22%

profile of v1, /device:TPU:0, one launch (start us, length us, event | category | flops | bytes accessed | tf_op | source)
XLA Modules:
  0.0 504.3 jit_solution(3313230083297391670)
XLA Ops:
  0.7 3.0 collective-permute-start.1
  3.7 2.7 copy.63.hidden
  8.4 24.6 %collective-permute-done.1 = bf16[1,24,36,768]{3,1,2,0:T(8,128)(2,1)S(1)} collective-permute-done((bf16[1,24,36,768]{3,1,2,0:T(8,128)(2,1)}, bf16[1,24,36,768]{3,1,2,0:T(8,128)(2,1)S(1)}, u32[]{:S(2)}, u32[]{:S(2)}) %collective-permute-start.1) | collective-permute-done | bytes 1327136 | tf_op jit(solution)/shard_map/ppermute | solution.py:424
  34.9 36.1 %shard_map.280 = (bf16[864,768]{1,0:T(8,128)(2,1)}, bf16[864,768]{1,0:T(8,128)(2,1)}, bf16[864,2304]{1,0:T(8,128)(2,1)}, bf16[12,6,144,72]{3,2,1,0:T(8,128)(2,1)...) custom-call(s32[1,24]{1,0:T(1,128)} %copy-done.9, ...), custom_call_target="tpu_custom_call" | custom-call | flops 12230590464 | bytes 30000000 | tf_op jit(solution)/shard_map/pallas_call | solution.py:426
  71.0 31.6 %shard_map.281 = (bf16[1,24,36,768]{3,2,1,0:T(8,128)(2,1)}, f32[864,768]{1,0:T(8,128)}, bf16[864,768]{1,0:T(8,128)(2,1)}, bf16[864,3072]{1,0:T(8,128)(2,1)}, bf1...) custom-call(s32[1,24]{1,0:T(1,128)} %own_len.3, s32[1,24]{1,0:T(1,128)} %flags.1, ...), custom_call_target="tpu_custom_call" | custom-call | flops 24461180928 | bytes 30000000 | tf_op jit(solution)/shard_map/pallas_call | solution.py:438
  102.6 8.9 %shard_map.291 = bf16[3072,768]{1,0:T(8,128)(2,1)} custom-call(bf16[864,3072]{1,0:T(8,128)(2,1)} %get-tuple-element.73.left, bf16[864,768]{1,0:T(8,128)(2,1)} %get-tuple-element.74.right), custom_call_target="tpu_custom_call" | custom-call | flops 4076863488 | bytes 11354112 | tf_op jit(solution)/shard_map/pallas_call | solution.py:326
  111.5 3.3 dynamic-slice_bitcast_fusion
  114.8 9.2 %shard_map.290 = bf16[768,3072]{1,0:T(8,128)(2,1)} custom-call(bf16[864,768]{1,0:T(8,128)(2,1)} %get-tuple-element.71.left, bf16[864,3072]{1,0:T(8,128)(2,1)} %get-tuple-element.72.right), custom_call_target="tpu_custom_call" | custom-call | flops 4076863488 | bytes 11354112 | tf_op jit(solution)/shard_map/pallas_call | solution.py:326
  124.0 3.2 dynamic-slice_bitcast_fusion.1
  127.2 36.0 %shard_map.282 = (f32[864,768]{1,0:T(8,128)}, bf16[864,768]{1,0:T(8,128)(2,1)}, bf16[864,768]{1,0:T(8,128)(2,1)}, bf16[864,2304]{1,0:T(8,128)(2,1)}, f32[5,768]{1,0:T(8,128)}) custom-call(f32[864,768]{1,0:T(8,128)} %get-tuple-element.47.grad_attended, f32[864,768]{1,0:T(8,128)} %get-tuple-element.45.normed2, f32[864,1]{1,0:T(8,128)} %get-tuple-element.48.scale2, ...), custom_call_target="tpu_custom_call" | custom-call | flops 8153726976 | bytes 30000000 | tf_op jit(solution)/shard_map/pallas_call | solution.py:452
  163.2 4.2 shard_map.289
  172.9 7.7 %shard_map.288 = bf16[768,2304]{1,0:T(8,128)(2,1)} custom-call(bf16[864,768]{1,0:T(8,128)(2,1)} %get-tuple-element.64.left, bf16[864,2304]{1,0:T(8,128)(2,1)} %get-tuple-element.65.right), custom_call_target="tpu_custom_call" | custom-call | flops 3057647616 | bytes 8847360 | tf_op jit(solution)/shard_map/pallas_call | solution.py:326
  180.7 2.8 dynamic-slice_bitcast_fusion.2
  184.0 35.4 %shard_map.283 = (f32[864,768]{1,0:T(8,128)}, bf16[864,768]{1,0:T(8,128)(2,1)}, bf16[864,768]{1,0:T(8,128)(2,1)}, bf16[864,2304]{1,0:T(8,128)(2,1)}, f32[5,768]{1,0:T(8,128)}) custom-call(f32[864,768]{1,0:T(8,128)} %get-tuple-element.52.grad_crossed, f32[864,768]{1,0:T(8,128)} %get-tuple-element.49.normed1, f32[864,1]{1,0:T(8,128)} %get-tuple-element.53.scale1, ...), custom_call_target="tpu_custom_call" | custom-call | flops 8153726976 | bytes 30000000 | tf_op jit(solution)/shard_map/pallas_call | solution.py:466
  223.0 6.2 %shard_map.286 = bf16[768,1536]{1,0:T(8,128)(2,1)} custom-call(bf16[864,768]{1,0:T(8,128)(2,1)} %get-tuple-element.60.left, bf16[864,2304]{1,0:T(8,128)(2,1)} %get-tuple-element.59.right), custom_call_target="tpu_custom_call" | custom-call | flops 2038431744 | bytes 6340608 | tf_op jit(solution)/shard_map/pallas_call | solution.py:326
  229.2 4.2 shard_map.285
  241.2 4.2 shard_map.287
  278.9 33.3 %collective-permute-done.14 = bf16[8,24,768]{2,1,0:T(8,128)(2,1)S(1)} collective-permute-done((bf16[8,24,768]{2,1,0:T(8,128)(2,1)S(1)}, bf16[8,24,768]{2,1,0:T(8,128)(2,1)S(1)}, u32[]{:S(2)}, u32[]{:S(2)}) %collective-permute-start.14) | collective-permute-done | bytes 294944 | tf_op jit(solution)/shard_map/ppermute | solution.py:373
  312.8 8.0 %collective-permute-done.27 = bf16[4,48,768]{2,1,0:T(8,128)(2,1)S(1)} collective-permute-done((bf16[4,48,768]{2,1,0:T(8,128)(2,1)S(1)}, bf16[4,48,768]{2,1,0:T(8,128)(2,1)S(1)}, u32[]{:S(2)}, u32[]{:S(2)}) %collective-permute-start.27) | collective-permute-done | bytes 294944 | tf_op jit(solution)/shard_map/ppermute | solution.py:373
  321.4 4.5 collective-permute-done.15
  326.5 5.4 %collective-permute-done.28 = bf16[2,48,768]{2,1,0:T(8,128)(2,1)S(1)} collective-permute-done((bf16[2,48,768]{2,1,0:T(8,128)(2,1)S(1)}, bf16[2,48,768]{2,1,0:T(8,128)(2,1)S(1)}, u32[]{:S(2)}, u32[]{:S(2)}) %collective-permute-start.28) | collective-permute-done | bytes 147488 | tf_op jit(solution)/shard_map/ppermute | solution.py:373
  332.4 4.6 collective-permute-done.16
  338.7 3.7 collective-permute-done.29
  344.7 2.9 collective-permute-done.17
  348.3 4.3 shard_map.284
  369.3 13.1 %collective-permute-done.4 = bf16[8,24,2304]{2,1,0:T(8,128)(2,1)S(1)} collective-permute-done((bf16[8,24,2304]{2,1,0:T(8,128)(2,1)S(1)}, bf16[8,24,2304]{2,1,0:T(8,128)(2,1)S(1)}, u32[]{:S(2)}, u32[]{:S(2)}) %collective-permute-start.4) | collective-permute-done | bytes 884768 | tf_op jit(solution)/shard_map/ppermute | solution.py:373
  384.8 55.3 %collective-permute-done.5 = bf16[4,24,2304]{2,1,0:T(8,128)(2,1)S(1)} collective-permute-done((bf16[4,24,2304]{2,1,0:T(8,128)(2,1)S(1)}, bf16[4,24,2304]{2,1,0:T(8,128)(2,1)S(1)}, u32[]{:S(2)}, u32[]{:S(2)}) %collective-permute-start.5) | collective-permute-done | bytes 442400 | tf_op jit(solution)/shard_map/ppermute | solution.py:373
  440.7 3.0 collective-permute-start.21
  443.6 8.0 %collective-permute-done.6 = bf16[2,24,2304]{2,1,0:T(8,128)(2,1)S(1)} collective-permute-done((bf16[2,24,2304]{2,1,0:T(8,128)(2,1)S(1)}, bf16[2,24,2304]{2,1,0:T(8,128)(2,1)S(1)}, u32[]{:S(2)}, u32[]{:S(2)}) %collective-permute-start.6) | collective-permute-done | bytes 221216 | tf_op jit(solution)/shard_map/ppermute | solution.py:373
  455.8 14.4 %collective-permute-done.36 = bf16[2,192,768]{2,1,0:T(8,128)(2,1)S(1)} collective-permute-done((bf16[2,192,768]{2,1,0:T(8,128)(2,1)S(1)}, bf16[2,192,768]{2,1,0:T(8,128)(2,1)S(1)}, u32[]{:S(2)}, u32[]{:S(2)}) %collective-permute-start.36) | collective-permute-done | bytes 589856 | tf_op jit(solution)/shard_map/ppermute | solution.py:373
  471.7 16.3 %collective-permute-done.32 = bf16[2,48,3072]{2,1,0:T(8,128)(2,1)S(1)} collective-permute-done((bf16[2,48,3072]{2,1,0:T(8,128)(2,1)S(1)}, bf16[2,48,3072]{2,1,0:T(8,128)(2,1)S(1)}, u32[]{:S(2)}, u32[]{:S(2)}) %collective-permute-start.32) | collective-permute-done | bytes 589856 | tf_op jit(solution)/shard_map/ppermute | solution.py:373
  490.4 12.8 %collective-permute-done.33 = bf16[1,48,3072]{2,1,0:T(8,128)(2,1)S(1)} collective-permute-done((bf16[1,48,3072]{2,1,0:T(8,128)(2,1)S(1)}, bf16[1,48,3072]{2,1,0:T(8,128)(2,1)S(1)}, u32[]{:S(2)}, u32[]{:S(2)}) %collective-permute-start.33) | collective-permute-done | bytes 294944 | tf_op jit(solution)/shard_map/ppermute | solution.py:373
  (189 shorter events, 89.8 us)
Async XLA Ops:
  0.7 32.3 %collective-permute-start.1 = (bf16[1,24,36,768]{3,1,2,0:T(8,128)(2,1)}, bf16[1,24,36,768]{3,1,2,0:T(8,128)(2,1)S(1)}, u32[]{:S(2)}, u32[]{:S(2)}) collective-permute-start(bf16[1,24,36,768]{3,1,2,0:T(8,128)(2,1)} %param.17), channel_id=1, source_target_pairs={{0,16},{16,0},{1,17},{17,1},{2,18},{18,2},{3,19},{19,3},{4,20},{20... | collective-permute-start | bytes 3981320 | tf_op jit(solution)/shard_map/ppermute | solution.py:424
  3.7 30.7 %collective-permute-start = (s32[1,24]{1,0:T(1,128)}, s32[1,24]{1,0:T(1,128)S(1)}, u32[]{:S(2)}, u32[]{:S(2)}) collective-permute-start(s32[1,24]{1,0:T(1,128)} %own_len.3), channel_id=1, source_target_pairs={{0,16},{16,0},{1,17},{17,1},{2,18},{18,2},{3,19},{19,3},{4,20},{20... | collective-permute-start | bytes 296 | tf_op jit(solution)/shard_map/ppermute | solution.py:424
  114.8 247.3 %collective-permute-start.34 = (bf16[8,192,768]{2,1,0:T(8,128)(2,1)}, bf16[8,192,768]{2,1,0:T(8,128)(2,1)}, u32[]{:S(2)}, u32[]{:S(2)}) collective-permute-start(bf16[8,192,768]{2,1,0:T(8,128)(2,1)} %dynamic-slice_bitcast_fusion), channel_id=1, source_target_pairs={{0,1},{1,0},{2,3},{3,2},{4,5},{5,4},{6,7},{7,6},{8,9},{9,8},{10,11... | collective-permute-start | bytes 7077896 | tf_op jit(solution)/shard_map/ppermute | solution.py:373
  169.3 107.7 %collective-permute-start.26 = (bf16[8,48,768]{2,1,0:T(8,128)(2,1)}, bf16[8,48,768]{2,1,0:T(8,128)(2,1)}, u32[]{:S(2)}, u32[]{:S(2)}) collective-permute-start(bf16[8,48,768]{2,1,0:T(8,128)(2,1)} %dynamic-slice_bitcast_fusion.10), channel_id=1, source_target_pairs={{0,1},{1,0},{2,3},{3,2},{4,5},{5,4},{6,7},{7,6},{8,9},{9,8},{10,11... | collective-permute-start | bytes 1769480 | tf_op jit(solution)/shard_map/ppermute | solution.py:373
  172.9 78.7 %collective-permute-start.22 = (f32[8,1,576]{2,1,0:T(1,128)}, f32[8,1,576]{2,1,0:T(1,128)}, u32[]{:S(2)}, u32[]{:S(2)}) collective-permute-start(f32[8,1,576]{2,1,0:T(1,128)} %dynamic-slice_bitcast_fusion.20), channel_id=1, source_target_pairs={{0,1},{1,0},{2,3},{3,2},{4,5},{5,4},{6,7},{7,6},{8,9},{9,8},{10,11... | collective-permute-start | bytes 55304 | tf_op jit(solution)/shard_map/ppermute | solution.py:373
  183.5 171.8 %collective-permute-start.18 = (bf16[8,48,2304]{2,1,0:T(8,128)(2,1)}, bf16[8,48,2304]{2,1,0:T(8,128)(2,1)}, u32[]{:S(2)}, u32[]{:S(2)}) collective-permute-start(bf16[8,48,2304]{2,1,0:T(8,128)(2,1)} %dynamic-slice_bitcast_fusion.2), channel_id=1, source_target_pairs={{0,1},{1,0},{2,3},{3,2},{4,5},{5,4},{6,7},{7,6},{8,9},{9,8},{10,11... | collective-permute-start | bytes 5308424 | tf_op jit(solution)/shard_map/ppermute | solution.py:373
  220.4 15.2 %collective-permute-start.8 = (f32[2,8,1,120]{3,1,0,2:T(8,128)S(1)}, f32[2,8,1,120]{3,1,0,2:T(8,128)S(1)}, u32[]{:S(2)}, u32[]{:S(2)}) collective-permute-start(f32[2,8,1,120]{3,1,0,2:T(8,128)S(1)} %bitcast.232), channel_id=1, source_target_pairs={{0,1},{1,0},{2,3},{3,2},{4,5},{5,4},{6,7},{7,6},{8,9},{9,8},{10,11... | collective-permute-start | bytes 23048 | tf_op jit(solution)/shard_map/ppermute | solution.py:373
  239.4 6.0 %collective-permute-start.10 = (f32[4,1,120]{2,0,1:T(4,128)S(1)}, f32[4,1,120]{2,0,1:T(4,128)S(1)}, u32[]{:S(2)}, u32[]{:S(2)}) collective-permute-start(f32[4,1,120]{2,0,1:T(4,128)S(1)} %bitcast.233), channel_id=1, source_target_pairs={{0,2},{1,3},{2,0},{3,1},{4,6},{5,7},{6,4},{7,5},{8,10},{9,11},{10,... | collective-permute-start | bytes 5768 | tf_op jit(solution)/shard_map/ppermute | solution.py:373
  245.4 6.2 %collective-permute-start.11 = (f32[2,1,120]{2,1,0:T(1,128)S(1)}, f32[2,1,120]{2,1,0:T(1,128)S(1)}, u32[]{:S(2)}, u32[]{:S(2)}) collective-permute-start(f32[2,1,120]{2,1,0:T(1,128)S(1)} %fusion.33), channel_id=1, source_target_pairs={{0,4},{1,5},{2,6},{3,7},{4,0},{5,1},{6,2},{7,3},{8,12},{9,13},{10,... | collective-permute-start | bytes 2888 | tf_op jit(solution)/shard_map/ppermute | solution.py:373
  251.6 22.5 %collective-permute-start.13 = (bf16[2,8,24,768]{3,2,1,0:T(8,128)(2,1)}, bf16[2,8,24,768]{3,2,1,0:T(8,128)(2,1)}, u32[]{:S(2)}, u32[]{:S(2)}) collective-permute-start(bf16[2,8,24,768]{3,2,1,0:T(8,128)(2,1)} %dynamic-slice_bitcast_fusion.11), channel_id=1, source_target_pairs={{0,1},{1,0},{2,3},{3,2},{4,5},{5,4},{6,7},{7,6},{8,9},{9,8},{10,11... | collective-permute-start | bytes 1769480 | tf_op jit(solution)/shard_map/ppermute | solution.py:373
  270.1 88.4 %collective-permute-start.3 = (bf16[2,8,24,2304]{3,2,1,0:T(8,128)(2,1)}, bf16[2,8,24,2304]{3,2,1,0:T(8,128)(2,1)}, u32[]{:S(2)}, u32[]{:S(2)}) collective-permute-start(bf16[2,8,24,2304]{3,2,1,0:T(8,128)(2,1)} %dynamic-slice_bitcast_fusion.3), channel_id=1, source_target_pairs={{0,1},{1,0},{2,3},{3,2},{4,5},{5,4},{6,7},{7,6},{8,9},{9,8},{10,11... | collective-permute-start | bytes 5308424 | tf_op jit(solution)/shard_map/ppermute | solution.py:373
  274.1 74.2 %collective-permute-start.2 = (bf16[864,768]{1,0:T(8,128)(2,1)}, bf16[864,768]{1,0:T(8,128)(2,1)}, u32[]{:S(2)}, u32[]{:S(2)}) collective-permute-start(bf16[864,768]{1,0:T(8,128)(2,1)} %get-tuple-element.57), channel_id=1, source_target_pairs={{0,16},{16,0},{1,17},{17,1},{2,18},{18,2},{3,19},{19,3},{4,20},{20... | collective-permute-start | bytes 3981320 | tf_op jit(solution)/shard_map/ppermute | solution.py:477
  277.0 35.1 %collective-permute-start.14 = (bf16[8,24,768]{2,1,0:T(8,128)(2,1)S(1)}, bf16[8,24,768]{2,1,0:T(8,128)(2,1)S(1)}, u32[]{:S(2)}, u32[]{:S(2)}) collective-permute-start(bf16[8,24,768]{2,1,0:T(8,128)(2,1)S(1)} %dynamic-slice_bitcast_fusion.15), channel_id=1, source_target_pairs={{0,16},{16,0},{1,17},{17,1},{2,18},{18,2},{3,19},{19,3},{4,20},{20... | collective-permute-start | bytes 884744 | tf_op jit(solution)/shard_map/ppermute | solution.py:373
  312.2 8.6 %collective-permute-start.27 = (bf16[4,48,768]{2,1,0:T(8,128)(2,1)S(1)}, bf16[4,48,768]{2,1,0:T(8,128)(2,1)S(1)}, u32[]{:S(2)}, u32[]{:S(2)}) collective-permute-start(bf16[4,48,768]{2,1,0:T(8,128)(2,1)S(1)} %dynamic-slice_bitcast_fusion.14), channel_id=1, source_target_pairs={{0,2},{1,3},{2,0},{3,1},{4,6},{5,7},{6,4},{7,5},{8,10},{9,11},{10,... | collective-permute-start | bytes 884744 | tf_op jit(solution)/shard_map/ppermute | solution.py:373
  320.8 5.1 %collective-permute-start.15 = (bf16[4,24,768]{2,1,0:T(8,128)(2,1)S(1)}, bf16[4,24,768]{2,1,0:T(8,128)(2,1)S(1)}, u32[]{:S(2)}, u32[]{:S(2)}) collective-permute-start(bf16[4,24,768]{2,1,0:T(8,128)(2,1)S(1)} %dynamic-slice_bitcast_fusion.18), channel_id=1, source_target_pairs={{0,2},{1,3},{2,0},{3,1},{4,6},{5,7},{6,4},{7,5},{8,10},{9,11},{10,... | collective-permute-start | bytes 442376 | tf_op jit(solution)/shard_map/ppermute | solution.py:373
  325.9 5.9 %collective-permute-start.28 = (bf16[2,48,768]{2,1,0:T(8,128)(2,1)S(1)}, bf16[2,48,768]{2,1,0:T(8,128)(2,1)S(1)}, u32[]{:S(2)}, u32[]{:S(2)}) collective-permute-start(bf16[2,48,768]{2,1,0:T(8,128)(2,1)S(1)} %dynamic-slice_bitcast_fusion.17), channel_id=1, source_target_pairs={{0,4},{1,5},{2,6},{3,7},{4,0},{5,1},{6,2},{7,3},{8,12},{9,13},{10,... | collective-permute-start | bytes 442376 | tf_op jit(solution)/shard_map/ppermute | solution.py:373
  337.0 5.4 %collective-permute-start.29 = (bf16[1,48,768]{2,1,0:T(8,128)(2,1)S(1)}, bf16[1,48,768]{2,1,0:T(8,128)(2,1)S(1)}, u32[]{:S(2)}, u32[]{:S(2)}) collective-permute-start(bf16[1,48,768]{2,1,0:T(8,128)(2,1)S(1)} %constant_dynamic-slice_fusion.2), channel_id=1, source_target_pairs={{0,8},{1,9},{2,10},{3,11},{4,12},{5,13},{6,14},{7,15},{8,0},{9,1},... | collective-permute-start | bytes 221192 | tf_op jit(solution)/shard_map/ppermute | solution.py:373
  342.4 5.3 %collective-permute-start.17 = (bf16[1,24,768]{2,1,0:T(8,128)(2,1)S(1)}, bf16[1,24,768]{2,1,0:T(8,128)(2,1)S(1)}, u32[]{:S(2)}, u32[]{:S(2)}) collective-permute-start(bf16[1,24,768]{2,1,0:T(8,128)(2,1)S(1)} %constant_dynamic-slice_fusion.10), channel_id=1, source_target_pairs={{0,8},{1,9},{2,10},{3,11},{4,12},{5,13},{6,14},{7,15},{8,0},{9,1},... | collective-permute-start | bytes 110600 | tf_op jit(solution)/shard_map/ppermute | solution.py:373
  347.6 18.4 %collective-permute-start.30 = (bf16[8,48,3072]{2,1,0:T(8,128)(2,1)}, bf16[8,48,3072]{2,1,0:T(8,128)(2,1)}, u32[]{:S(2)}, u32[]{:S(2)}) collective-permute-start(bf16[8,48,3072]{2,1,0:T(8,128)(2,1)} %dynamic-slice_bitcast_fusion.1), channel_id=1, source_target_pairs={{0,1},{1,0},{2,3},{3,2},{4,5},{5,4},{6,7},{7,6},{8,9},{9,8},{10,11... | collective-permute-start | bytes 7077896 | tf_op jit(solution)/shard_map/ppermute | solution.py:373
  358.0 26.3 %collective-permute-start.19 = (bf16[4,48,2304]{2,1,0:T(8,128)(2,1)S(1)}, bf16[4,48,2304]{2,1,0:T(8,128)(2,1)S(1)}, u32[]{:S(2)}, u32[]{:S(2)}) collective-permute-start(bf16[4,48,2304]{2,1,0:T(8,128)(2,1)S(1)} %dynamic-slice_bitcast_fusion.6), channel_id=1, source_target_pairs={{0,2},{1,3},{2,0},{3,1},{4,6},{5,7},{6,4},{7,5},{8,10},{9,11},{10,... | collective-permute-start | bytes 2654216 | tf_op jit(solution)/shard_map/ppermute | solution.py:373
  360.5 21.9 %collective-permute-start.4 = (bf16[8,24,2304]{2,1,0:T(8,128)(2,1)S(1)}, bf16[8,24,2304]{2,1,0:T(8,128)(2,1)S(1)}, u32[]{:S(2)}, u32[]{:S(2)}) collective-permute-start(bf16[8,24,2304]{2,1,0:T(8,128)(2,1)S(1)} %dynamic-slice_bitcast_fusion.7), channel_id=1, source_target_pairs={{0,16},{16,0},{1,17},{17,1},{2,18},{18,2},{3,19},{19,3},{4,20},{20... | collective-permute-start | bytes 2654216 | tf_op jit(solution)/shard_map/ppermute | solution.py:373
  364.4 87.4 %collective-permute-start.35 = (bf16[4,192,768]{2,1,0:T(8,128)(2,1)S(1)}, bf16[4,192,768]{2,1,0:T(8,128)(2,1)S(1)}, u32[]{:S(2)}, u32[]{:S(2)}) collective-permute-start(bf16[4,192,768]{2,1,0:T(8,128)(2,1)S(1)} %dynamic-slice_bitcast_fusion.4), channel_id=1, source_target_pairs={{0,2},{1,3},{2,0},{3,1},{4,6},{5,7},{6,4},{7,5},{8,10},{9,11},{10,... | collective-permute-start | bytes 3538952 | tf_op jit(solution)/shard_map/ppermute | solution.py:373
  368.7 85.5 %collective-permute-start.31 = (bf16[4,48,3072]{2,1,0:T(8,128)(2,1)S(1)}, bf16[4,48,3072]{2,1,0:T(8,128)(2,1)S(1)}, u32[]{:S(2)}, u32[]{:S(2)}) collective-permute-start(bf16[4,48,3072]{2,1,0:T(8,128)(2,1)S(1)} %dynamic-slice_bitcast_fusion.5), channel_id=1, source_target_pairs={{0,2},{1,3},{2,0},{3,1},{4,6},{5,7},{6,4},{7,5},{8,10},{9,11},{10,... | collective-permute-start | bytes 3538952 | tf_op jit(solution)/shard_map/ppermute | solution.py:373
  382.7 57.5 %collective-permute-start.5 = (bf16[4,24,2304]{2,1,0:T(8,128)(2,1)S(1)}, bf16[4,24,2304]{2,1,0:T(8,128)(2,1)S(1)}, u32[]{:S(2)}, u32[]{:S(2)}) collective-permute-start(bf16[4,24,2304]{2,1,0:T(8,128)(2,1)S(1)} %dynamic-slice_bitcast_fusion.13), channel_id=1, source_target_pairs={{0,2},{1,3},{2,0},{3,1},{4,6},{5,7},{6,4},{7,5},{8,10},{9,11},{10,... | collective-permute-start | bytes 1327112 | tf_op jit(solution)/shard_map/ppermute | solution.py:373
  384.5 56.0 %collective-permute-start.20 = (bf16[2,48,2304]{2,1,0:T(8,128)(2,1)S(1)}, bf16[2,48,2304]{2,1,0:T(8,128)(2,1)S(1)}, u32[]{:S(2)}, u32[]{:S(2)}) collective-permute-start(bf16[2,48,2304]{2,1,0:T(8,128)(2,1)S(1)} %dynamic-slice_bitcast_fusion.12), channel_id=1, source_target_pairs={{0,4},{1,5},{2,6},{3,7},{4,0},{5,1},{6,2},{7,3},{8,12},{9,13},{10,... | collective-permute-start | bytes 1327112 | tf_op jit(solution)/shard_map/ppermute | solution.py:373
  440.3 11.4 %collective-permute-start.6 = (bf16[2,24,2304]{2,1,0:T(8,128)(2,1)S(1)}, bf16[2,24,2304]{2,1,0:T(8,128)(2,1)S(1)}, u32[]{:S(2)}, u32[]{:S(2)}) collective-permute-start(bf16[2,24,2304]{2,1,0:T(8,128)(2,1)S(1)} %dynamic-slice_bitcast_fusion.16), channel_id=1, source_target_pairs={{0,4},{1,5},{2,6},{3,7},{4,0},{5,1},{6,2},{7,3},{8,12},{9,13},{10,... | collective-permute-start | bytes 663560 | tf_op jit(solution)/shard_map/ppermute | solution.py:373
  440.7 14.3 %collective-permute-start.21 = (bf16[1,48,2304]{2,1,0:T(8,128)(2,1)S(1)}, bf16[1,48,2304]{2,1,0:T(8,128)(2,1)S(1)}, u32[]{:S(2)}, u32[]{:S(2)}) collective-permute-start(bf16[1,48,2304]{2,1,0:T(8,128)(2,1)S(1)} %constant_dynamic-slice_fusion.9), channel_id=1, source_target_pairs={{0,8},{1,9},{2,10},{3,11},{4,12},{5,13},{6,14},{7,15},{8,0},{9,1},... | collective-permute-start | bytes 663560 | tf_op jit(solution)/shard_map/ppermute | solution.py:373
  451.8 37.0 %collective-permute-start.7 = (bf16[1,24,2304]{2,1,0:T(8,128)(2,1)S(1)}, bf16[1,24,2304]{2,1,0:T(8,128)(2,1)S(1)}, u32[]{:S(2)}, u32[]{:S(2)}) collective-permute-start(bf16[1,24,2304]{2,1,0:T(8,128)(2,1)S(1)} %constant_dynamic-slice_fusion.21), channel_id=1, source_target_pairs={{0,8},{1,9},{2,10},{3,11},{4,12},{5,13},{6,14},{7,15},{8,0},{9,1},... | collective-permute-start | bytes 331784 | tf_op jit(solution)/shard_map/ppermute | solution.py:373
  452.2 18.0 %collective-permute-start.36 = (bf16[2,192,768]{2,1,0:T(8,128)(2,1)S(1)}, bf16[2,192,768]{2,1,0:T(8,128)(2,1)S(1)}, u32[]{:S(2)}, u32[]{:S(2)}) collective-permute-start(bf16[2,192,768]{2,1,0:T(8,128)(2,1)S(1)} %dynamic-slice_bitcast_fusion.8), channel_id=1, source_target_pairs={{0,4},{1,5},{2,6},{3,7},{4,0},{5,1},{6,2},{7,3},{8,12},{9,13},{10,... | collective-permute-start | bytes 1769480 | tf_op jit(solution)/shard_map/ppermute | solution.py:373
  454.7 33.3 %collective-permute-start.32 = (bf16[2,48,3072]{2,1,0:T(8,128)(2,1)S(1)}, bf16[2,48,3072]{2,1,0:T(8,128)(2,1)S(1)}, u32[]{:S(2)}, u32[]{:S(2)}) collective-permute-start(bf16[2,48,3072]{2,1,0:T(8,128)(2,1)S(1)} %dynamic-slice_bitcast_fusion.9), channel_id=1, source_target_pairs={{0,4},{1,5},{2,6},{3,7},{4,0},{5,1},{6,2},{7,3},{8,12},{9,13},{10,... | collective-permute-start | bytes 1769480 | tf_op jit(solution)/shard_map/ppermute | solution.py:373
  470.4 19.1 %collective-permute-start.37 = (bf16[1,192,768]{2,1,0:T(8,128)(2,1)S(1)}, bf16[1,192,768]{2,1,0:T(8,128)(2,1)S(1)}, u32[]{:S(2)}, u32[]{:S(2)}) collective-permute-start(bf16[1,192,768]{2,1,0:T(8,128)(2,1)S(1)} %constant_dynamic-slice_fusion), channel_id=1, source_target_pairs={{0,8},{1,9},{2,10},{3,11},{4,12},{5,13},{6,14},{7,15},{8,0},{9,1},... | collective-permute-start | bytes 884744 | tf_op jit(solution)/shard_map/ppermute | solution.py:373
  488.2 15.0 %collective-permute-start.33 = (bf16[1,48,3072]{2,1,0:T(8,128)(2,1)S(1)}, bf16[1,48,3072]{2,1,0:T(8,128)(2,1)S(1)}, u32[]{:S(2)}, u32[]{:S(2)}) collective-permute-start(bf16[1,48,3072]{2,1,0:T(8,128)(2,1)S(1)} %constant_dynamic-slice_fusion.1), channel_id=1, source_target_pairs={{0,8},{1,9},{2,10},{3,11},{4,12},{5,13},{6,14},{7,15},{8,0},{9,1},... | collective-permute-start | bytes 884744 | tf_op jit(solution)/shard_map/ppermute | solution.py:373
  (20 other events, 94.4 us)

commit v2 on v1

v2 whole, which is shorter than its diff:
```python
import functools

import jax
import jax.numpy as jnp
from jax import lax
from jax.experimental import pallas as pl
from jax.experimental.pallas import tpu as pltpu
from jax.sharding import PartitionSpec as P

HEADS = 12
HEAD_DIM = 64
PAIRS = HEADS // 2
LANES = 2 * HEAD_DIM
TILE = 8
WIDTH = HEADS * HEAD_DIM
MESH = pl.DeviceIdType.MESH

norm_eps = 1e-06
masked_score = -1000000000.0
vmem_limit = 60 * 1024 * 1024

f32 = jnp.float32
bf16 = jnp.bfloat16


def dot(left, right):
    return jnp.dot(left, right, preferred_element_type=f32)


def dot_nt(left, right):
    return lax.dot_general(left, right, (((1,), (1,)), ((), ())), preferred_element_type=f32)


def dot_tn(left, right):
    return lax.dot_general(left, right, (((0,), (0,)), ((), ())), preferred_element_type=f32)


def norm_parts(summed):
    centred = summed - jnp.mean(summed, axis=-1, keepdims=True)
    scaled = lax.rsqrt(jnp.mean(centred * centred, axis=-1, keepdims=True) + norm_eps)
    return centred * scaled, scaled


def norm_backward(upstream, normed, scaled, gain):
    inner = upstream * gain
    return scaled * (
        inner
        - jnp.mean(inner, axis=-1, keepdims=True)
        - normed * jnp.mean(inner * normed, axis=-1, keepdims=True)
    )


def row_sum(rows):
    return jnp.sum(rows, axis=0, keepdims=True)


def gelu_parts(entries):
    size = jnp.abs(entries)
    bell = jnp.exp(entries * entries * -0.5)
    t = 1.0 / (1.0 + size * (0.3275911 * 0.7071067811865476))
    poly = t * (
        0.5 * 0.254829592
        + t
        * (
            0.5 * -0.284496736
            + t * (0.5 * 1.421413741 + t * (0.5 * -1.453152027 + t * (0.5 * 1.061405429)))
        )
    )
    tail = poly * bell
    area = jnp.where(entries >= 0.0, 1.0 - tail, tail)
    return entries * area, area + entries * bell * 0.3989422804014327


def padded(slots):
    return -(-slots // TILE) * TILE


def lane_tiles(ref, at, count):
    return jnp.concatenate([ref[at + tile, :count] for tile in range(PAIRS)], axis=1)


def to_pairs(stage, ref, at, rows, slots):
    count, high = rows.shape[0], padded(slots)
    for tile in range(PAIRS):
        stage[tile, :count] = rows[:, tile * LANES : (tile + 1) * LANES]
    for group in range(TILE // 2):
        for tile in range(PAIRS):
            ref[group, :, at + tile * LANES : at + (tile + 1) * LANES] = pair_rows(stage, tile, group, high).astype(bf16)


def pair_rows(stage, tile, group, high):
    return jnp.concatenate(
        [stage[tile, pl.ds(2 * group + item, high, stride=TILE), :] for item in range(2)], axis=0)


def put_pair(stage, tile, group, rows, high):
    for item in range(2):
        stage[tile, pl.ds(2 * group + item, high, stride=TILE), :] = rows[item * high : (item + 1) * high]


def clear_padding(stage, slots):
    stage[:, slots * TILE :] = jnp.zeros((stage.shape[0], stage.shape[1] - slots * TILE, LANES), f32)


def pair_mask(len_ref, first, high):
    shape = (2 * high, 2 * high)
    row = lax.broadcasted_iota(jnp.int32, shape, 0)
    col = lax.broadcasted_iota(jnp.int32, shape, 1)
    second = row >= high
    low = jnp.where(second, high, 0)
    end = jnp.where(second, high + len_ref[pl.ds(first + 1, 1), : 2 * high], len_ref[pl.ds(first, 1), : 2 * high])
    allowed = (col >= low) & (col < end)
    return jnp.concatenate([allowed, allowed], axis=0)


def first_head(shape):
    return lax.broadcasted_iota(jnp.int32, shape, 1) < HEAD_DIM


def head_stack(rows):
    low, zero = first_head(rows.shape), jnp.zeros_like(rows)
    return jnp.concatenate([jnp.where(low, rows, zero), jnp.where(low, zero, rows)], axis=0)


def head_merge(stacked):
    count = stacked.shape[0] // 2
    return jnp.where(first_head((count, stacked.shape[1])), stacked[:count], stacked[count:])


def batches(size):
    everything = [(group, pair) for group in range(TILE // 2) for pair in range(PAIRS)]
    return [everything[at : at + size] for at in range(0, len(everything), size)]


def head_block(ref, group, part, pair):
    return ref[group, :, part * WIDTH + pair * LANES : part * WIDTH + (pair + 1) * LANES]


def attend(triple_ref, probs_ref, context_ref, stage, len_ref, first_item, slots):
    high = padded(slots)
    ones = jnp.ones((2 * high, LANES), bf16)
    masks = [pair_mask(len_ref, first_item + 2 * group, high) for group in range(TILE // 2)]
    for batch in batches(12):
        scores = [
            jnp.where(
                masks[group],
                dot_nt(head_stack(head_block(triple_ref, group, 0, pair)), head_block(triple_ref, group, 1, pair)),
                masked_score,
            )
            for group, pair in batch
        ]
        largest = [jnp.max(entry, axis=-1, keepdims=True) for entry in scores]
        weights = [jnp.exp(entry - top).astype(bf16) for entry, top in zip(scores, largest)]
        both = [
            dot(entry, jnp.concatenate([head_block(triple_ref, group, 2, pair), ones], axis=1))
            for (group, pair), entry in zip(batch, weights)
        ]
        for (group, pair), entry, sums in zip(batch, weights, both):
            inverse = 1.0 / sums[:, LANES:]
            probs_ref[group, pair] = (entry.astype(f32) * inverse[:, : 2 * high]).astype(bf16)
            context = head_merge(sums[:, :LANES] * inverse)
            context_ref[group, :, pair * LANES : (pair + 1) * LANES] = context
            put_pair(stage, pair, group, context, high)


def attend_back(triple_ref, probs_ref, context_ref, stage, out_stage, slots):
    high = padded(slots)
    ones = jnp.ones((2 * high, LANES), bf16)
    low = first_head((2 * high, LANES))
    for batch in batches(6):
        stacks, grad_probs = [], []
        for group, pair in batch:
            grads = pair_rows(stage, pair, group, high)
            delta = -grads * context_ref[group, :, pair * LANES : (pair + 1) * LANES]
            upper = delta.astype(bf16)
            lower = pltpu.roll(delta - upper.astype(f32), HEAD_DIM, 1).astype(bf16)
            deltas = jnp.concatenate([jnp.where(low, upper, lower), jnp.where(low, lower, upper)], axis=0)
            stacks.append(head_stack(grads.astype(bf16)))
            values = head_block(triple_ref, group, 2, pair)
            grad_probs.append(
                dot_nt(jnp.concatenate([stacks[-1], deltas], axis=1), jnp.concatenate([values, ones], axis=1)))
        grad_scores = [
            (probs_ref[group, pair].astype(f32) * entry).astype(bf16) for (group, pair), entry in zip(batch, grad_probs)]
        grad_queries = [dot(entry, head_block(triple_ref, group, 1, pair)) for (group, pair), entry in zip(batch, grad_scores)]
        grad_values = [dot_tn(probs_ref[group, pair], entry) for (group, pair), entry in zip(batch, stacks)]
        grad_keys = [
            dot_tn(entry, head_stack(head_block(triple_ref, group, 0, pair))) for (group, pair), entry in zip(batch, grad_scores)]
        for at, (group, pair) in enumerate(batch):
            put_pair(out_stage, pair, group, head_merge(grad_queries[at]) * HEAD_DIM**-0.5, high)
            put_pair(out_stage, PAIRS + pair, group, grad_keys[at], high)
            put_pair(out_stage, 2 * PAIRS + pair, group, grad_values[at], high)


def across(axis, bit):
    place, weight = lax.axis_index(axis), 1 << bit
    return {axis: place + weight - 2 * weight * ((place // weight) % 2)}


def greet(partners):
    barrier = pltpu.get_barrier_semaphore()
    for partner in partners:
        pl.semaphore_signal(barrier, inc=1, device_id=partner, device_id_type=MESH)
    pl.semaphore_wait(barrier, len(partners))


def forward_kernel(
    slots, steps,
    lens, whole, hidden, cross_proj, cross_bias, cross_norm, cross_out, self_proj, self_bias, self_norm, self_out,
    dense, far_dense, triple1, probs1, contexts1, context1, normed1, scale1,
    triple2, probs2, contexts2, context2, normed2, scale2,
    wide, stage, context_stage, far, far_lens, send_sem, recv_sem,
):
    count = slots * TILE
    step = pl.program_id(0)
    partner = across("stream", 0)

    def travel(part):
        if part == steps:
            source, target = lens, far_lens
        else:
            source, target = whole.at[:, pl.ds(part * TILE, TILE)], far.at[part]
        return pltpu.make_async_remote_copy(
            src_ref=source, dst_ref=target, send_sem=send_sem.at[part], recv_sem=recv_sem.at[part],
            device_id=partner, device_id_type=MESH)

    @pl.when(step == 0)
    def _():
        greet([partner])
        travel(steps).start()
        for part in range(steps):
            travel(part).start()
        clear_padding(stage, slots)

    rows = hidden[...].astype(f32).reshape(count, WIDTH)
    wide[...] = rows
    low = rows.astype(bf16)
    dense[...] = low
    queries = (dot(low, cross_proj[:, :WIDTH]) + cross_bias[0:1]).astype(bf16).astype(f32)
    to_pairs(stage, triple1, 0, queries * HEAD_DIM**-0.5, slots)

    @pl.when(step == 0)
    def _():
        travel(steps).wait()

    for part in range(steps):

        @pl.when(step == part)
        def _():
            travel(part).wait()

    far_low = far[step].astype(f32).reshape(count, WIDTH).astype(bf16)
    far_dense[...] = far_low
    to_pairs(stage, triple1, WIDTH, dot(far_low, cross_proj[:, WIDTH : 2 * WIDTH]), slots)
    to_pairs(stage, triple1, 2 * WIDTH, dot(far_low, cross_proj[:, 2 * WIDTH :]) + cross_bias[1:2], slots)
    attend(triple1, probs1, contexts1, context_stage, far_lens, step * TILE, slots)
    low = lane_tiles(context_stage, 0, count).astype(bf16)
    context1[...] = low
    normed, scale = norm_parts(dot(low, cross_out[...]) + cross_bias[2:3] + wide[...])
    normed1[...] = normed
    scale1[...] = scale
    crossed = normed * cross_norm[0:1] + cross_norm[1:2]
    wide[...] = crossed
    low = crossed.astype(bf16)
    queries = (dot(low, self_proj[0, :, :WIDTH]) + self_bias[0, 0:1]).astype(bf16).astype(f32)
    to_pairs(stage, triple2, 0, queries * HEAD_DIM**-0.5, slots)
    to_pairs(stage, triple2, WIDTH, dot(low, self_proj[0, :, WIDTH : 2 * WIDTH]), slots)
    to_pairs(stage, triple2, 2 * WIDTH, dot(low, self_proj[0, :, 2 * WIDTH :]) + self_bias[0, 1:2], slots)
    attend(triple2, probs2, contexts2, context_stage, lens, step * TILE, slots)
    low = lane_tiles(context_stage, 0, count).astype(bf16)
    context2[...] = low
    normed, scale = norm_parts(dot(low, self_out[0]) + self_bias[0, 2:3] + wide[...])
    normed2[...] = normed
    scale2[...] = scale


def ffn_kernel(
    slots,
    live, normed2, cotangent, self_norm, ffn_up, up_bias, ffn_down, down_bias, ffn_norm,
    output, grad_attended, attended_low, activated, grad_last_low, grad_expanded, up_sum, vec_sum,
    slope,
):
    width = WIDTH
    chunks = ffn_up.shape[2] // width
    step = pl.program_id(0)

    @pl.when(step == 0)
    def _():
        up_sum[...] = jnp.zeros_like(up_sum)
        vec_sum[...] = jnp.zeros_like(vec_sum)

    attended = normed2[...] * self_norm[0, 0:1] + self_norm[0, 1:2]
    low = attended.astype(bf16)
    attended_low[...] = low
    total = attended + down_bias[...]
    for chunk in range(chunks):
        at = slice(chunk * width, (chunk + 1) * width)
        active, rise = gelu_parts(dot(low, ffn_up[0, :, at]) + up_bias[:, at])
        active = active.astype(bf16)
        activated[:, at] = active
        slope[:, at] = rise
        total = total + dot(active, ffn_down[0, at, :])
    normed, scale = norm_parts(total)
    output[...] = (normed * ffn_norm[0, 0:1] + ffn_norm[0, 1:2]).reshape(slots, TILE, WIDTH).astype(bf16)
    slot = lax.broadcasted_iota(jnp.int32, (slots, TILE, WIDTH), 0)
    alive = jnp.concatenate([live[pl.ds(pl.multiple_of(step * TILE, TILE), TILE), :]] * PAIRS, axis=1)
    upstream = jnp.where(slot < alive[None], cotangent[...].astype(f32), 0.0).reshape(slots * TILE, WIDTH)
    grad_last = norm_backward(upstream, normed, scale, ffn_norm[0, 0:1])
    grad_low = grad_last.astype(bf16)
    grad_last_low[...] = grad_low
    vec_sum[0:1] += row_sum(grad_low.astype(f32))
    vec_sum[1:2] += row_sum(upstream * normed)
    vec_sum[2:3] += row_sum(upstream)
    total = grad_last
    for chunk in range(chunks):
        at = slice(chunk * width, (chunk + 1) * width)
        grad_up = (dot_nt(grad_low, ffn_down[0, at, :]) * slope[:, at]).astype(bf16)
        grad_expanded[:, at] = grad_up
        up_sum[:, at] += row_sum(grad_up.astype(f32))
        total = total + dot_nt(grad_up, ffn_up[0, :, at])
    grad_attended[...] = total


def norm_back_sums(vec_sum, upstream, normed, scale, gain):
    @pl.when(pl.program_id(0) == 0)
    def _():
        vec_sum[...] = jnp.zeros_like(vec_sum)

    grad = norm_backward(upstream, normed, scale, gain)
    low = grad.astype(bf16)
    vec_sum[2:3] += row_sum(low.astype(f32))
    vec_sum[3:4] += row_sum(upstream * normed)
    vec_sum[4:5] += row_sum(upstream)
    return grad, low


def context_back(low, out, triple, probs, contexts, grad_triple, vec_sum, stage, out_stage, slots):
    count = slots * TILE

    @pl.when(pl.program_id(0) == 0)
    def _():
        clear_padding(stage, slots)

    grads = dot_nt(low, out).astype(bf16).astype(f32)
    for tile in range(PAIRS):
        stage[tile, :count] = grads[:, tile * LANES : (tile + 1) * LANES]
    attend_back(triple, probs, contexts, stage, out_stage, slots)
    for part in range(3):
        rows = lane_tiles(out_stage, part * PAIRS, count).astype(bf16)
        grad_triple[:, part * WIDTH : (part + 1) * WIDTH] = rows
        if part != 1:
            vec_sum[part // 2 : part // 2 + 1] += row_sum(rows.astype(f32))


def self_back_kernel(
    slots,
    grad_attended, normed2, scale2, normed1, triple2, probs2, contexts2, cross_norm, self_norm, self_proj, self_out,
    grad_crossed, crossed_low, grad_mid_low, grad_triple, vec_sum,
    stage, out_stage,
):
    grad_mid, low = norm_back_sums(vec_sum, grad_attended[...], normed2[...], scale2[...], self_norm[0, 0:1])
    grad_mid_low[...] = low
    crossed_low[...] = (normed1[...] * cross_norm[0:1] + cross_norm[1:2]).astype(bf16)
    grad_crossed[...] = grad_mid
    context_back(low, self_out[0], triple2, probs2, contexts2, grad_triple, vec_sum, stage, out_stage, slots)
    grad_crossed[...] += dot_nt(grad_triple[...], self_proj[0])


def cross_back_kernel(
    slots, steps,
    grad_crossed, normed1, scale1, triple1, probs1, contexts1, cross_norm, cross_proj, cross_out,
    grad_own, grad_far, grad_got, grad_cross_low, grad_triple, vec_sum,
    stage, out_stage, outbox, send_sem, recv_sem,
):
    step = pl.program_id(0)
    partner = across("stream", 0)

    def travel(part):
        return pltpu.make_async_remote_copy(
            src_ref=outbox.at[part], dst_ref=grad_got.at[part], send_sem=send_sem.at[part], recv_sem=recv_sem.at[part],
            device_id=partner, device_id_type=MESH)

    @pl.when(step == 0)
    def _():
        greet([partner])

    grad_cross, low = norm_back_sums(vec_sum, grad_crossed[...], normed1[...], scale1[...], cross_norm[0:1])
    grad_cross_low[...] = low
    grad_own[...] = grad_cross
    context_back(low, cross_out[...], triple1, probs1, contexts1, grad_triple, vec_sum, stage, out_stage, slots)
    rows = dot_nt(grad_triple[:, WIDTH:], cross_proj[:, WIDTH:]).astype(bf16)
    grad_far[...] = rows
    for part in range(steps - 1):

        @pl.when(step == part)
        def _():
            outbox[part] = rows
            travel(part).start()

    grad_own[...] += dot_nt(grad_triple[:, :WIDTH], cross_proj[:, :WIDTH])

    @pl.when(step == steps - 1)
    def _():
        for part in range(steps - 1):
            travel(part).wait()


def place_order(digits, share):
    starts = []
    for block in range(1 << len(digits)):
        source = 0
        for number, (axis, bit, weight) in enumerate(digits):
            mine = (lax.axis_index(axis) // (1 << bit)) % 2
            other = (block >> (len(digits) - 1 - number)) & 1
            source = source + (mine + other - 2 * mine * other) * weight
        starts.append(source * share)
    return starts


def order_matrix(digits, share):
    starts = place_order(digits, share)
    block = WIDTH // len(starts)
    source = jnp.concatenate([start + jnp.arange(block) for start in starts])
    return (source[:, None] == jnp.arange(WIDTH)[None, :]).astype(bf16)


def turn(left, digits, share, order, natural, turned):
    if order is not None:
        turned[...] = dot_nt(order, left).astype(bf16)
        return
    natural[...] = left.T
    for number, start in enumerate(place_order(digits, share)):
        turned[number * share : (number + 1) * share, :] = natural[pl.ds(pl.multiple_of(start, 16), share), :]


class Products:
    def __init__(self, plan, digits, share, lefts, rights, sums, order, natural, turned, outbox, inbox, small_out, small_in, sems):
        self.plan, self.digits, self.share = plan, digits, share
        self.lefts, self.rights, self.sums, self.order = lefts, rights, sums, order
        self.natural, self.turned, self.sems = natural, turned, sems
        self.boxes = (outbox, inbox, small_out, small_in)
        self.half = WIDTH // 2
        self.count = len(plan)
        self.total = self.count + (1 if sums else 0)

    def travel(self, at):
        outbox, inbox, small_out, small_in = self.boxes
        source, target = (outbox.at[at], inbox.at[at]) if at < self.count else (small_out, small_in)
        return pltpu.make_async_remote_copy(
            src_ref=source, dst_ref=target, send_sem=self.sems[0].at[at], recv_sem=self.sems[1].at[at],
            device_id=across("dp", 0), device_id_type=MESH)

    def block(self, at, rows):
        if at == self.count:
            return dot_nt(self.order()[rows, :], sum(ref[...] for ref in self.sums).astype(bf16))
        left, right = self.plan[at]
        return dot(self.turned[left, rows, :], self.rights[right]())

    def send(self):
        ready = set()
        for at in range(self.total):
            if at < self.count and self.plan[at][0] not in ready:
                left = self.plan[at][0]
                ready.add(left)
                order = self.order() if self.natural is None else None
                turn(self.lefts[left](), self.digits, self.share, order, self.natural, self.turned.at[left])
            product = self.block(at, slice(self.half, 2 * self.half)).astype(bf16)
            if at < self.count:
                self.boxes[0][at] = product
            else:
                self.boxes[2][...] = product
            self.travel(at).start()

    def keep(self, store):
        for at in range(self.total):
            product = self.block(at, slice(0, self.half))
            self.travel(at).wait()
            store(at, product + (self.boxes[1][at] if at < self.count else self.boxes[3][...]).astype(f32))


class Loads:
    def __init__(self, pairs, sem):
        self.copies = [pltpu.make_async_copy(source, target, sem.at[at]) for at, (source, target) in enumerate(pairs)]
        self.targets = [target for _, target in pairs]
        self.waited = set()
        for copy in self.copies:
            copy.start()

    def __getitem__(self, at):
        def read():
            if at not in self.waited:
                self.waited.add(at)
                self.copies[at].wait()
            return self.targets[at][...]

        return read


def weight_grad_kernel(plan, digits, share, stacked, sources, orders, lefts_count, sums_count, *refs):
    refs = list(refs)

    def take(count):
        out = refs[:count]
        del refs[:count]
        return out

    order = take(orders)
    operands = take(len({name for name, _ in sources}))
    sums = take(sums_count)
    kept, sent = take(2)
    natural = take(1)[0] if share % 16 == 0 else None
    turned, outbox, inbox, small_out, small_in, loaded, order_at, load_sem, send_sem, recv_sem = refs
    quarter = WIDTH // 4
    greet([across("dp", 0)])
    pairs = [(order[0], order_at)] if orders else []
    for at, (name, column) in enumerate(sources):
        pairs.append((operands[name].at[:, pl.ds(column * WIDTH, WIDTH)], loaded.at[at]))
    loads = Loads(pairs, load_sem)
    skip = len(pairs) - len(sources)
    products = Products(
        plan, digits, share, [loads[skip + at] for at in range(lefts_count)],
        [loads[skip + at] for at in range(lefts_count, len(sources))], sums, loads[0] if orders else None, natural, turned,
        outbox, inbox, small_out, small_in, (send_sem, recv_sem))

    def store(at, product):
        wide = product.shape[1]
        place = (slice(at * quarter, (at + 1) * quarter), slice(0, wide)) if stacked else (slice(0, quarter), slice(at * WIDTH, at * WIDTH + wide))
        kept[place] = product[:quarter].astype(bf16)
        sent[place] = product[quarter:].astype(bf16)

    products.send()
    products.keep(store)


def weight_grad(operands, sources, lefts_count, plan, digits, share, identity, sums=(), stacked=False, order=None):
    rows = operands[0].shape[0]
    half, quarter, count = WIDTH // 2, WIDTH // 4, len(plan)
    columns = WIDTH if stacked else count * WIDTH + (LANES if sums else 0)
    turn_rows = share % 16 == 0
    orders = [order] if sums or not turn_rows else []
    total = count + (1 if sums else 0)
    return pl.pallas_call(
        functools.partial(weight_grad_kernel, plan, digits, share, stacked, sources, len(orders), lefts_count, len(sums)),
        in_specs=[pl.BlockSpec(memory_space=pl.ANY)] * (len(orders) + len(operands)) + [pl.BlockSpec(memory_space=pltpu.VMEM)] * len(sums),
        out_specs=[pl.BlockSpec(memory_space=pltpu.VMEM)] * 2,
        out_shape=[jax.ShapeDtypeStruct((quarter * (count if stacked else 1), columns), bf16)] * 2,
        scratch_shapes=([pltpu.VMEM((WIDTH, rows), bf16)] if turn_rows else []) + [
            pltpu.VMEM((lefts_count, WIDTH, rows), bf16),
            pltpu.VMEM((count, half, WIDTH), bf16),
            pltpu.VMEM((count, half, WIDTH), bf16),
            pltpu.VMEM((half, LANES), bf16),
            pltpu.VMEM((half, LANES), bf16),
            pltpu.VMEM((len(sources), rows, WIDTH), bf16),
            pltpu.VMEM((WIDTH, WIDTH) if orders else (16, LANES), bf16),
            pltpu.SemaphoreType.DMA((len(sources) + len(orders),)),
            pltpu.SemaphoreType.DMA((total,)),
            pltpu.SemaphoreType.DMA((total,)),
        ],
        compiler_params=pltpu.CompilerParams(vmem_limit_bytes=vmem_limit, collective_id=identity, has_side_effects=True),
        cost_estimate=pl.CostEstimate(
            flops=2 * rows * WIDTH * WIDTH * (count + lefts_count),
            bytes_accessed=2 * (rows * WIDTH * len(sources) + WIDTH * columns),
            transcendentals=0,
        ),
    )(*orders, *operands, *sums)


def cross_finish_kernel(
    plan, digits, share, steps,
    order, dense, far_dense, context1, grad_triple, grad_cross_low, grad_own, grad_far, grad_got, sums,
    grad_hidden, result,
    turned, outbox, inbox, small_out, small_in, loaded, order_at, own, got, last, total, box1, box2, box3,
    load_sem, send_sem, recv_sem, send_last, recv_last, send_part, recv_part,
):
    links = [across("stream", 0), across("dp", 1), across("dp", 2)]
    greet(links + [across("dp", 0)])
    size = grad_own.shape[0] // steps
    slots = size // TILE
    columns = [grad_triple.at[:, pl.ds(part * WIDTH, WIDTH)] for part in range(3)]
    sources = [dense, columns[0], far_dense, columns[1], columns[2], context1, grad_cross_low]
    pairs = [(order, order_at)] + [(source, loaded.at[at]) for at, source in enumerate(sources)] + [(grad_own, own), (grad_got, got)]
    loads = Loads(pairs, load_sem)
    final = pltpu.make_async_remote_copy(
        src_ref=grad_far.at[pl.ds((steps - 1) * size, size)], dst_ref=last, send_sem=send_last, recv_sem=recv_last,
        device_id=links[0], device_id_type=MESH)
    final.start()
    products = Products(
        plan, digits, share, [loads[1], loads[3], loads[6]], [loads[2], loads[4], loads[5], loads[7]], [sums], loads[0], None,
        turned, outbox, inbox, small_out, small_in, (send_sem, recv_sem))
    cut = 4 * WIDTH // 3
    bounds = [(0, cut), (cut, 2 * cut), (2 * cut, total.shape[-1])]
    routes = [(0, 1, 2), (1, 2, 0), (2, 0, 1)]
    boxes = [box1, box2, box3]

    def view(part, stage, sent):
        spot = [slice(None)] * 3
        for axis in routes[part][:stage]:
            spot[axis] = 0
        spot[routes[part][stage]] = sent
        return tuple(spot) + (slice(None), slice(*bounds[part]))

    def travel(part, stage):
        wide = bounds[part][1] - bounds[part][0]
        at = 3 * part + stage
        box = boxes[stage].at[part]
        target = box.at[(slice(None),) * (3 - stage) + (slice(0, wide),)]
        return pltpu.make_async_remote_copy(
            src_ref=total.at[view(part, stage, 1)], dst_ref=target, send_sem=send_part.at[at], recv_sem=recv_part.at[at],
            device_id=links[routes[part][stage]], device_id_type=MESH)

    def store(at, product):
        wide = product.shape[1]
        rows = product.reshape(2, 2, 2, product.shape[0] // 8, wide).astype(bf16)
        total[:, :, :, :, at * WIDTH : at * WIDTH + wide] = rows
        for part in range(3):
            if at == min(part + 1, len(plan)) and part < 2 or part == 2 and at == len(plan):
                travel(part, 0).start()

    products.send()
    products.keep(store)

    def put(part, rows):
        value = own[part * size : (part + 1) * size, :] + rows.astype(f32)
        grad_hidden[:, part * TILE : (part + 1) * TILE, :] = value.reshape(slots, TILE, WIDTH).astype(bf16)

    loads[len(pairs) - 2]()
    loads[len(pairs) - 1]()
    for part in range(steps - 1):
        put(part, got[part])
    final.wait()
    put(steps - 1, last[...])
    for stage in range(3):
        for part in range(3):
            travel(part, stage).wait()
            wide = bounds[part][1] - bounds[part][0]
            spot = view(part, stage, 0)
            came = boxes[stage][(part,) + (slice(None),) * (3 - stage) + (slice(0, wide),)]
            total[spot] = (total[spot].astype(f32) + came.astype(f32)).astype(bf16)
            if stage < 2:
                travel(part, stage + 1).start()
    result[...] = total[0, 0, 0]


smem = pl.BlockSpec(memory_space=pltpu.SMEM)


def fixed(array):
    zeros = (0,) * array.ndim
    return pl.BlockSpec(array.shape, lambda i: zeros, pipeline_mode=pl.Buffered(1))


def rows_of(count, width):
    return pl.BlockSpec((count, width), lambda i: (i, 0))


def total_of(count, width):
    return pl.BlockSpec((count, width), lambda i: (0, 0))


def shape_of(shape, kind):
    return jax.ShapeDtypeStruct(shape, kind)


def flip(count, bit):
    return [(place, place ^ (1 << bit)) for place in range(count)]


def send(parts, axis, bit):
    return lax.ppermute(parts, axis, flip(lax.axis_size(axis), bit))


def add(kept, got):
    return (kept.astype(f32) + got.astype(f32)).astype(bf16)


def halve(kept, got):
    half = kept.shape[0] // 2
    return add(kept[:half], got[:half]), add(kept[half:], got[half:])


def halve_at(kept, got, axis, bit):
    mine = (lax.axis_index(axis) >> bit) & 1
    shape = (kept.shape[0] // 2, 2) + kept.shape[1:]
    kept, got = kept.reshape(shape), got.reshape(shape)

    def part(at):
        return add(lax.dynamic_index_in_dim(kept, at, 1, keepdims=False), lax.dynamic_index_in_dim(got, at, 1, keepdims=False))

    return part(mine), part(1 - mine)


def after(value, *earlier):
    return lax.optimization_barrier((value,) + earlier)


def local(
    hidden, lengths, task_flags, cotangent, cross_proj, cross_bias, cross_norm, cross_out, self_proj, self_bias,
    self_norm, self_out, ffn_up, up_bias, ffn_down, down_bias, ffn_norm,
):
    _, items, slots, width = hidden.shape
    deep = ffn_up.shape[2]
    rows = items * slots
    streams, places = lax.axis_size("stream"), lax.axis_size("dp")
    bits = places.bit_length() - 1
    steps = items // TILE
    size = TILE * slots
    high = padded(slots)
    groups = items // 2
    item_spec = pl.BlockSpec((slots, TILE, width), lambda i: (0, i, 0))
    row_spec = rows_of(size, width)
    scale_spec = rows_of(size, 1)
    wide_spec = rows_of(size, 3 * width)
    deep_spec = rows_of(size, deep)
    triple_spec = pl.BlockSpec((TILE // 2, 2 * high, 3 * width), lambda i: (i, 0, 0))
    pair_spec = pl.BlockSpec((TILE // 2, 2 * high, width), lambda i: (i, 0, 0))
    probs_spec = pl.BlockSpec((TILE // 2, PAIRS, 4 * high, 2 * high), lambda i: (i, 0, 0, 0))
    any_spec = pl.BlockSpec(memory_space=pl.ANY)
    row_f32, row_bf16 = shape_of((rows, width), f32), shape_of((rows, width), bf16)
    scale_f32 = shape_of((rows, 1), f32)
    wide_bf16, deep_bf16 = shape_of((rows, 3 * width), bf16), shape_of((rows, deep), bf16)
    triple_bf16 = shape_of((groups, 2 * high, 3 * width), bf16)
    pair_f32 = shape_of((groups, 2 * high, width), f32)
    probs_bf16 = shape_of((groups, PAIRS, 4 * high, 2 * high), bf16)
    sum_spec, sum_f32 = total_of(LANES, width), shape_of((LANES, width), f32)
    params = pltpu.CompilerParams(vmem_limit_bytes=vmem_limit)
    unit = 2 * rows * width * width
    stage = pltpu.VMEM((PAIRS, TILE * high, LANES), f32)
    out_stage = pltpu.VMEM((3 * PAIRS, TILE * high, LANES), f32)

    def remote(identity):
        return pltpu.CompilerParams(vmem_limit_bytes=vmem_limit, collective_id=identity, has_side_effects=True)

    def cost(units, count):
        return pl.CostEstimate(flops=units * unit, bytes_accessed=count, transcendentals=0)

    chunk_bits = (width * places // deep).bit_length() - 1
    share, cross_share = width // places, width // places // streams
    digits = [("dp", bit, 1 << bit) for bit in range(bits)]
    z_digits = [digits[0], digits[2], digits[1]] + digits[3:]
    cross_digits = [digits[0], ("stream", 0, places)] + digits[1:]
    order, cross_order = order_matrix(digits, share), order_matrix(cross_digits, cross_share)
    z_order = order_matrix(z_digits, share) if share % 16 else None
    lens = jnp.broadcast_to(lengths[0][:, None], (items, LANES))
    live = jnp.broadcast_to(jnp.where(task_flags[0] > 0, lengths[0], 0)[:, None], (items, LANES))
    slot_rows = jnp.transpose(hidden[0], (1, 0, 2))
    slot_cotangent = jnp.transpose(cotangent[0], (1, 0, 2))

    def down_halve(kept, got, bit):
        if bit >= chunk_bits:
            return halve_at(kept, got, "dp", bit)
        half = kept.shape[1] // 2
        return add(kept[:, :half], got[:, :half]), add(kept[:, half:], got[:, half:])

    (dense, far_dense, triple1, probs1, contexts1, context1, normed1, scale1,
     triple2, probs2, contexts2, context2, normed2, scale2) = pl.pallas_call(
        functools.partial(forward_kernel, slots, steps),
        grid=(steps,),
        in_specs=[fixed(lens), any_spec, item_spec]
        + [fixed(w) for w in (cross_proj, cross_bias, cross_norm, cross_out, self_proj, self_bias, self_norm, self_out)],
        out_specs=[row_spec, row_spec] + [triple_spec, probs_spec, pair_spec, row_spec, row_spec, scale_spec] * 2,
        out_shape=[row_bf16, row_bf16] + [triple_bf16, probs_bf16, pair_f32, row_bf16, row_f32, scale_f32] * 2,
        scratch_shapes=[
            pltpu.VMEM((size, width), f32), stage, stage,
            pltpu.VMEM((steps, slots, TILE, width), bf16),
            pltpu.VMEM((items, LANES), jnp.int32),
            pltpu.SemaphoreType.DMA((steps + 1,)),
            pltpu.SemaphoreType.DMA((steps + 1,)),
        ],
        compiler_params=remote(0),
        cost_estimate=cost(12, 40_000_000),
    )(lens, slot_rows, slot_rows, cross_proj, cross_bias, cross_norm, cross_out, self_proj, self_bias, self_norm, self_out)

    output, grad_attended, attended_low, activated, grad_last_low, grad_expanded, up_sum, ffn_sum = pl.pallas_call(
        functools.partial(ffn_kernel, slots),
        grid=(steps,),
        in_specs=[fixed(live), row_spec, item_spec] + [fixed(w) for w in (self_norm, ffn_up, up_bias, ffn_down, down_bias, ffn_norm)],
        out_specs=[item_spec, row_spec, row_spec, deep_spec, row_spec, deep_spec, total_of(1, deep), total_of(3, width)],
        out_shape=[shape_of((slots, items, width), bf16), row_f32, row_bf16, deep_bf16, row_bf16, deep_bf16, shape_of((1, deep), f32), shape_of((3, width), f32)],
        scratch_shapes=[pltpu.VMEM((size, deep), f32)],
        compiler_params=params,
        cost_estimate=cost(24, 30_000_000),
    )(live, normed2, slot_cotangent, self_norm, ffn_up, up_bias, ffn_down, down_bias, ffn_norm)

    chunks = deep // width
    down_kept, down_sent = weight_grad(
        [activated, grad_last_low], [(0, at) for at in range(chunks)] + [(1, 0)], chunks, [(at, 0) for at in range(chunks)],
        digits[:chunk_bits], deep // places, 1, stacked=True)
    attended_low, down_sent = after(attended_low, down_sent)
    up_kept, up_sent = weight_grad(
        [attended_low, grad_expanded], [(0, 0)] + [(1, at) for at in range(chunks)], 1, [(0, at) for at in range(chunks)],
        z_digits, share, 2, order=z_order)
    grad_attended, down_sent, up_sent = after(grad_attended, down_sent, up_sent)
    down_got, up_got = send(down_sent, "dp", 1), send(up_sent, "dp", 2)

    grad_crossed, crossed_low, grad_mid_low, grad_triple2, self_sum = pl.pallas_call(
        functools.partial(self_back_kernel, slots),
        grid=(steps,),
        in_specs=[row_spec, row_spec, scale_spec, row_spec, triple_spec, probs_spec, pair_spec]
        + [fixed(w) for w in (cross_norm, self_norm, self_proj, self_out)],
        out_specs=[row_spec, row_spec, row_spec, wide_spec, sum_spec],
        out_shape=[row_f32, row_bf16, row_bf16, wide_bf16, sum_f32],
        scratch_shapes=[stage, out_stage],
        compiler_params=params,
        cost_estimate=cost(8, 30_000_000),
    )(grad_attended, normed2, scale2, normed1, triple2, probs2, contexts2, cross_norm, self_norm, self_proj, self_out)

    up_small = up_sum.reshape(places, chunks, share).transpose(1, 0, 2).reshape(chunks, width)
    small = jnp.concatenate([ffn_sum, up_small], axis=0)
    small = jnp.pad(small, ((8, LANES - 8 - small.shape[0]), (0, 0)))
    rest = 1 << chunk_bits
    stack = (places // rest, rest // 4, deep // places, width)
    down_kept, down_got = down_kept.reshape(stack), down_got.reshape(stack)
    down_kept, down_sent = down_halve(down_kept, down_got, 2)
    up_kept, up_sent = halve(up_kept, up_got)
    crossed_low, down_sent, up_sent = after(crossed_low, down_sent, up_sent)
    down_got, up_got = send(down_sent, "dp", 2), send(up_sent, "dp", 1)
    self_kept, self_sent = weight_grad(
        [crossed_low, context2, grad_triple2, grad_mid_low], [(0, 0), (1, 0), (2, 0), (2, 1), (2, 2), (3, 0)], 2,
        [(0, 0), (0, 1), (0, 2), (1, 3)], digits, share, 3, (self_sum, small), order=order)
    down_kept, down_sent = down_halve(down_kept, down_got, 3)
    up_kept, up_sent = halve(up_kept, up_got)
    grad_crossed, down_sent, up_sent, self_sent = after(grad_crossed, down_sent, up_sent, self_sent)
    down_got, up_got, self_got = send(down_sent, "dp", 3), send(up_sent, "dp", 3), send(self_sent, "dp", 1)

    grad_own, grad_far, grad_got, grad_cross_low, grad_triple1, cross_sum = pl.pallas_call(
        functools.partial(cross_back_kernel, slots, steps),
        grid=(steps,),
        in_specs=[row_spec, row_spec, scale_spec, triple_spec, probs_spec, pair_spec]
        + [fixed(w) for w in (cross_norm, cross_proj, cross_out)],
        out_specs=[row_spec, row_spec, any_spec, row_spec, wide_spec, sum_spec],
        out_shape=[row_f32, row_bf16, shape_of((steps - 1, size, width), bf16), row_bf16, wide_bf16, sum_f32],
        scratch_shapes=[
            stage, out_stage,
            pltpu.VMEM((steps - 1, size, width), bf16),
            pltpu.SemaphoreType.DMA((steps - 1,)),
            pltpu.SemaphoreType.DMA((steps - 1,)),
        ],
        compiler_params=remote(5),
        cost_estimate=cost(8, 30_000_000),
    )(grad_crossed, normed1, scale1, triple1, probs1, contexts1, cross_norm, cross_proj, cross_out)

    self_kept, self_sent = halve(self_kept, self_got)
    grad_cross_low, self_sent = after(grad_cross_low, self_sent)
    self_got = send(self_sent, "dp", 2)
    half, left, parts = width // 2, width // 16, 4
    wide = 4 * width + LANES
    box = wide - 2 * (4 * width // 3)
    grad_hidden, cross_rest = pl.pallas_call(
        functools.partial(cross_finish_kernel, [(0, 0), (1, 1), (1, 2), (2, 3)], cross_digits, cross_share, steps),
        in_specs=[any_spec] * 9 + [pl.BlockSpec(memory_space=pltpu.VMEM)],
        out_specs=[pl.BlockSpec(memory_space=pltpu.VMEM)] * 2,
        out_shape=[shape_of((slots, items, width), bf16), shape_of((left, wide), bf16)],
        scratch_shapes=[
            pltpu.VMEM((3, width, rows), bf16),
            pltpu.VMEM((parts, half, width), bf16),
            pltpu.VMEM((parts, half, width), bf16),
            pltpu.VMEM((half, LANES), bf16),
            pltpu.VMEM((half, LANES), bf16),
            pltpu.VMEM((7, rows, width), bf16),
            pltpu.VMEM((width, width), bf16),
            pltpu.VMEM((rows, width), f32),
            pltpu.VMEM((steps - 1, size, width), bf16),
            pltpu.VMEM((size, width), bf16),
            pltpu.VMEM((2, 2, 2, left, wide), bf16),
            pltpu.VMEM((3, 2, 2, left, box), bf16),
            pltpu.VMEM((3, 2, left, box), bf16),
            pltpu.VMEM((3, left, box), bf16),
            pltpu.SemaphoreType.DMA((10,)),
            pltpu.SemaphoreType.DMA((parts + 1,)),
            pltpu.SemaphoreType.DMA((parts + 1,)),
            pltpu.SemaphoreType.DMA,
            pltpu.SemaphoreType.DMA,
            pltpu.SemaphoreType.DMA((9,)),
            pltpu.SemaphoreType.DMA((9,)),
        ],
        compiler_params=remote(4),
        cost_estimate=cost(7, 30_000_000),
    )(cross_order, dense, far_dense, context1, grad_triple1, grad_cross_low, grad_own, grad_far, grad_got, cross_sum)

    output, grad_hidden = (jnp.transpose(entry, (1, 0, 2))[None] for entry in (output, grad_hidden))
    self_kept, self_sent = halve(self_kept, self_got)
    cross_kept, cross_sent = cross_rest[: left // 2], cross_rest[left // 2 :]
    self_got, cross_got = send(self_sent, "dp", 3), send(cross_sent, "dp", 3)
    for bit in range(4, bits):
        up_kept, up_sent = halve(up_kept, up_got)
        up_got = send(up_sent, "dp", bit)
        self_kept, self_sent = halve(self_kept, self_got)
        self_got = send(self_sent, "dp", bit)
        cross_kept, cross_sent = halve(cross_kept, cross_got)
        cross_got = send(cross_sent, "dp", bit)
        down_kept, down_sent = down_halve(down_kept, down_got, bit)
        down_got = send(down_sent, "dp", bit)
    own_cross = cross_kept.astype(f32) + cross_got.astype(f32)
    own_up = up_kept.astype(f32) + up_got.astype(f32)
    own_down = (down_kept.astype(f32) + down_got.astype(f32)).reshape(deep // places, width)
    own_self = self_kept.astype(f32) + self_got.astype(f32)
    own_self_proj, own_self_out, self_small = own_self[:, : 3 * width], own_self[:, 3 * width : 4 * width], own_self[:, 4 * width :]
    own_cross_proj, own_cross_out, cross_small = own_cross[:, : 3 * width], own_cross[:, 3 * width : 4 * width], own_cross[:, 4 * width :]
    cross_small = cross_small[:, :5].T
    ffn_small = self_small[:, 8:11].T
    small_up = self_small[:, 11 : 11 + deep // width].T.reshape(-1)
    self_small = self_small[:, :5].T
    return (
        output,
        grad_hidden,
        own_cross_proj,
        cross_small[0:3],
        cross_small[3:5],
        own_cross_out,
        own_self_proj[None],
        self_small[None, 0:3],
        self_small[None, 3:5],
        own_self_out[None],
        own_up[None],
        small_up[None],
        own_down[None],
        ffn_small[0][None],
        ffn_small[None, 1:3],
    )


def solution(mesh):
    in_specs = (
        P("stream", "dp", None, None),
        P("stream", "dp"),
        P("stream", "dp"),
        P("stream", "dp", None, None),
        P(),
        P(),
        P(),
        P(),
        P("stream", None, None),
        P("stream", None, None),
        P("stream", None, None),
        P("stream", None, None),
        P("stream", None, None),
        P("stream", None),
        P("stream", None, None),
        P("stream", None),
        P("stream", None, None),
    )
    out_specs = (
        P("stream", "dp", None, None),
        P("stream", "dp", None, None),
        P(("stream", "dp"), None),
        P(None, ("stream", "dp")),
        P(None, ("stream", "dp")),
        P(("stream", "dp"), None),
        P("stream", "dp", None),
        P("stream", None, "dp"),
        P("stream", None, "dp"),
        P("stream", "dp", None),
        P("stream", "dp", None),
        P("stream", "dp"),
        P("stream", "dp", None),
        P("stream", "dp"),
        P("stream", None, "dp"),
    )
    return jax.shard_map(local, mesh=mesh, in_specs=in_specs, out_specs=out_specs, check_vma=False)
```

time: 510 us -> 272 us (0.53)
  waiting for transfers between devices: 214 us -> 13.1 us
  local copies, waits for them, and re-layouts: 40.2 us -> 14.4 us
  Pallas kernels: 188 us -> 212 us
  starting transfers between devices: 36.5 us -> 13.6 us
  other arithmetic: 24 us -> 12 us
    ppermute x38 -> x10, waiting for transfers between devices: 214 us -> 13.1 us  [send(): return lax.ppermute(parts, axis, flip(lax.axis_size(axis), bit))]
    pallas_call x12 -> x8, Pallas kernels: 188 us -> 212 us  [the longest x1 45.5 us: local(): pl.pallas_call(functools.partial(forward_kernel, slots, steps), grid=(ste...]
    ppermute x38 -> x10, starting transfers between devices: 36.5 us -> 13.6 us  [send(): return lax.ppermute(parts, axis, flip(lax.axis_size(axis), bit))]
    squeeze x33 -> x0, local copies, waits for them, and re-layouts: 15.9 us -> none  [halve(): send = lax.dynamic_index_in_dim(parts, 1 - mine, dim, keepdims=False)]
    convert_element_type x20 -> x9, other arithmetic: 13.8 us -> 6.64 us  [the longest x7 4.01 us: add(): return (kept.astype(f32) + got.astype(f32)).astype(bf16)]
    unnamed x33 -> x24, local copies, waits for them, and re-layouts: 11.8 us -> 5.36 us
    add x13 -> x26, other arithmetic: 5.86 us -> 0.23 us  [the longest x1 0.11 us: local(): own_self = self_kept.astype(f32) + self_got.astype(f32)]
  transfers between devices with their start and end apart: 38 -> 10, of which waited for: 19 -> 2; matrix products, arithmetic and copies ran while one was open for 12% -> 5% of each run, Pallas kernels for 22% -> 41%
where the time goes in v2:
time: 272 us; the launch traced here: 266 us
  Pallas kernels  212 us (78%)
  local copies, waits for them, and re-layouts  14.4 us (5%)
  starting transfers between devices  13.6 us (5%)
  waiting for transfers between devices  13.1 us (5%)
  other arithmetic  12 us (4%)
    pallas_call x1, Pallas kernels, local(): pl.pallas_call(functools.partial(forward_kernel, slots, steps), grid=(ste...  45.5 us
    pallas_call x1, Pallas kernels, local(): pl.pallas_call(functools.partial(cross_finish_kernel, [(0, 0), (1, 1), (1...  40.8 us
    pallas_call x3, Pallas kernels, weight_grad(): pl.pallas_call(functools.partial(weight_grad_kernel, plan, digits, share,...  40.7 us
    pallas_call x1, Pallas kernels, local(): pl.pallas_call(functools.partial(cross_back_kernel, slots, steps), grid=(...  32.5 us
    pallas_call x1, Pallas kernels, local(): pl.pallas_call(functools.partial(ffn_kernel, slots), grid=(steps,), in_sp...  31.4 us
    pallas_call x1, Pallas kernels, local(): pl.pallas_call(functools.partial(self_back_kernel, slots), grid=(steps,),...  21 us
    ppermute x10, starting transfers between devices, send(): return lax.ppermute(parts, axis, flip(lax.axis_size(axis), bit))  13.6 us
    ppermute x10, waiting for transfers between devices, send(): return lax.ppermute(parts, axis, flip(lax.axis_size(axis), bit))  13.1 us
  transfers between devices with their start and end apart: 10, of which 2 were waited for; matrix products, arithmetic and copies ran while one was open for 5% of the time, Pallas kernels for 41%

profile of v2, /device:TPU:0, one launch (start us, length us, event | category | flops | bytes accessed | tf_op | source)
XLA Modules:
  0.0 266.4 jit_solution(3796607113442576234)
XLA Ops:
  0.6 1.3 copy.44.self_bias
  2.6 1.3 broadcast_in_dim.42.lens
  3.9 45.5 %shard_map.280 = (bf16[864,768]{1,0:T(8,128)(2,1)}, bf16[864,768]{1,0:T(8,128)(2,1)}, bf16[12,80,2304]{2,1,0:T(8,128)(2,1)}, bf16[12,6,160,80]{3,2,1,0:T(8,128)(...) custom-call(s32[24,128]{1,0:T(8,128)} %broadcast_in_dim.42.lens, ...), custom_call_target="tpu_custom_call" | custom-call | flops 12230590464 | bytes 40000000 | tf_op jit(solution)/shard_map/pallas_call | solution.py:754
  50.1 31.4 %shard_map.281 = (bf16[36,24,768]{2,1,0:T(8,128)(2,1)}, f32[864,768]{1,0:T(8,128)}, bf16[864,768]{1,0:T(8,128)(2,1)}, bf16[864,3072]{1,0:T(8,128)(2,1)}, bf16[86...) custom-call(s32[24,128]{1,0:T(8,128)} %broadcast_in_dim.41.live, ...), custom_call_target="tpu_custom_call" | custom-call | flops 24461180928 | bytes 30000000 | tf_op jit(solution)/shard_map/pallas_call | solution.py:772
  81.5 13.9 %shard_map.282 = (bf16[768,768]{1,0:T(8,128)(2,1)}, bf16[768,768]{1,0:T(8,128)(2,1)}) custom-call(bf16[864,3072]{1,0:T(8,128)(2,1)} %get-tuple-element.77.refs_0_, bf16[864,768]{1,0:T(8,128)(2,1)} %get-tuple-element.78.refs_1_), custom_call_target="tpu_custom_call" | custom-call | flops 8153726976 | bytes 7815168 | tf_op jit(solution)/shard_map/pallas_call | solution.py:541
  95.4 12.2 %shard_map.283 = (bf16[192,3072]{1,0:T(8,128)(2,1)}, bf16[192,3072]{1,0:T(8,128)(2,1)}) custom-call(bf16[864,768]{1,0:T(8,128)(2,1)} %get-tuple-element.81.refs_0_, bf16[864,3072]{1,0:T(8,128)(2,1)} %get-tuple-element.82.refs_1_), custom_call_target="tpu_custom_call" | custom-call | flops 5096079360 | bytes 11354112 | tf_op jit(solution)/shard_map/pallas_call | solution.py:541
  107.6 1.8 collective-permute-start
  109.5 1.6 collective-permute-start.1
  111.3 1.3 fusion.order
  113.1 0.7 reduce.3
  114.1 0.8 select_maximum_fusion.refs_6_
  114.9 1.3 fusion.1.refs_0_
  116.3 21.0 %shard_map.284 = (f32[864,768]{1,0:T(8,128)}, bf16[864,768]{1,0:T(8,128)(2,1)}, bf16[864,768]{1,0:T(8,128)(2,1)}, bf16[864,2304]{1,0:T(8,128)(2,1)}, f32[128,768]{1,0:T(8,128)}) custom-call(f32[864,768]{1,0:T(8,128)} %get-tuple-element.84.grad_attended, f32[864,768]{1,0:T(8,128)} %get-tuple-element.70.normed2, f32[864,1]{1,0:T(8,128)} %get-tuple-element.85.scale2, ...), custom_call_target="tpu_custom_call" | custom-call | flops 8153726976 | bytes 30000000 | tf_op jit(solution)/shard_map/pallas_call | solution.py:794
  137.3 1.0 fusion.2
  138.8 1.2 add_convert_fusion.2
  140.4 0.9 collective-permute-start.3
  141.5 14.7 %shard_map.285 = (bf16[192,3200]{1,0:T(8,128)(2,1)}, bf16[192,3200]{1,0:T(8,128)(2,1)}) custom-call(bf16[768,768]{1,0:T(8,128)(2,1)} %fusion.1.refs_0_, bf16[864,768]{1,0:T(8,128)(2,1)} %get-tuple-element.98.refs_1_, bf16[864,768]{1,0:T(8,128)(2,1)} %get-tuple-element.99.refs_2_, bf16[864,2304]{1,0:T(8,128)(2,1)} %get-tuple-element.100.refs_3_, ...), custom_call_target="tpu_custom_call" | custom-call | flops 6115295232 | bytes 12877824 | tf_op jit(solution)/shard_map/pallas_call | solution.py:541
  156.3 1.2 fusion.4
  157.5 1.1 collective-permute-start.4
  158.7 2.6 collective-permute-start.8
  161.6 32.5 %shard_map.286 = (f32[864,768]{1,0:T(8,128)}, bf16[864,768]{1,0:T(8,128)(2,1)}, bf16[2,288,768]{2,1,0:T(8,128)(2,1)}, bf16[864,768]{1,0:T(8,128)(2,1)}, bf16[864,2304]{1,0:T(8,128)(2,1)}, /*index=5*/f32[128,768]{1,0:T(8,128)}) custom-call(f32[864,768]{1,0:T(8,128)} %get-tuple-element.106.grad_crossed, f32[864,768]{1,0:T(8,128)} %get-tuple-element.86.normed1, ...), custom_call_target="tpu_custom_call" | custom-call | flops 8153726976 | bytes 30000000 | tf_op jit(solution)/shard_map/pallas_call | solution.py:824
  194.1 2.1 add_bitcast_fusion
  196.2 0.9 add_bitcast_fusion.1
  197.4 1.7 collective-permute-start.6
  199.1 40.8 %shard_map.287 = (bf16[36,24,768]{2,1,0:T(8,128)(2,1)}, bf16[48,3200]{1,0:T(8,128)(2,1)}) custom-call(bf16[768,768]{1,0:T(8,128)(2,1)} %fusion.order, bf16[864,768]{1,0:T(8,128)(2,1)} %get-tuple-element.72.dense, bf16[864,768]{1,0:T(8,128)(2,1)} %get-tuple-element.73.far_dense, bf16[864,768]{1,0:T(8,128)(2,1)} %get-tuple-element.74.context1, ...), custom_call_target="tpu_custom_call" | custom-call | flops 7134511104 | bytes 30000000 | tf_op jit(solution)/shard_map/pallas_call | solution.py:847
  239.9 1.0 slice.111
  240.9 2.6 collective-permute-start.5
  244.0 11.5 %collective-permute-done.5 = bf16[24,3200]{1,0:T(8,128)(2,1)S(1)} collective-permute-done((bf16[24,3200]{1,0:T(8,128)(2,1)S(1)}, bf16[24,3200]{1,0:T(8,128)(2,1)S(1)}, u32[]{:S(2)}, u32[]{:S(2)}) %collective-permute-start.5) | collective-permute-done | bytes 153632 | tf_op jit(solution)/shard_map/ppermute | solution.py:668
  255.5 0.7 slice.139
  258.2 1.6 collective-permute-done.7
  260.0 0.8 slice_bitcast_fusion
  265.0 1.1 copy.62
  (85 shorter events, 10.9 us)
Async XLA Ops:
  107.6 5.5 %copy-start.8 = (f32[1,3072]{1,0:T(1,128)S(1)}, f32[1,3072]{1,0:T(1,128)}, u32[]{:S(2)}) copy-start(f32[1,3072]{1,0:T(1,128)} %get-tuple-element.104) | copy-start | bytes 36868
  107.6 6.4 %copy-start.7 = (f32[3,768]{1,0:T(4,128)S(1)}, f32[3,768]{1,0:T(4,128)}, u32[]{:S(2)}) copy-start(f32[3,768]{1,0:T(4,128)} %get-tuple-element.103) | copy-start | bytes 27652
  107.6 29.7 %collective-permute-start = (bf16[768,768]{1,0:T(8,128)(2,1)}, bf16[768,768]{1,0:T(8,128)(2,1)S(1)}, u32[]{:S(2)}, u32[]{:S(2)}) collective-permute-start(bf16[768,768]{1,0:T(8,128)(2,1)} %get-tuple-element.92), channel_id=1, source_target_pairs={{0,2},{1,3},{2,0},{3,1},{4,6},{5,7},{6,4},{7,5},{8,10},{9,11},{10,... | collective-permute-start | bytes 3538952 | tf_op jit(solution)/shard_map/ppermute | solution.py:668
  109.5 28.9 %collective-permute-start.1 = (bf16[192,3072]{1,0:T(8,128)(2,1)}, bf16[192,3072]{1,0:T(8,128)(2,1)S(1)}, u32[]{:S(2)}, u32[]{:S(2)}) collective-permute-start(bf16[192,3072]{1,0:T(8,128)(2,1)} %get-tuple-element.95), channel_id=1, source_target_pairs={{0,4},{1,5},{2,6},{3,7},{4,0},{5,1},{6,2},{7,3},{8,12},{9,13},{10,... | collective-permute-start | bytes 3538952 | tf_op jit(solution)/shard_map/ppermute | solution.py:668
  116.3 21.0 %copy-start.3 = (bf16[768,768]{1,0:T(8,128)(2,1)S(1)}, bf16[768,768]{1,0:T(8,128)(2,1)}, u32[]{:S(2)}) copy-start(bf16[768,768]{1,0:T(8,128)(2,1)} %get-tuple-element.91) | copy-start | bytes 3538948
  137.3 1.5 copy-start.2
  140.0 16.3 %collective-permute-start.2 = (bf16[2,1,192,768]{3,2,1,0:T(8,128)(2,1)}, bf16[2,1,192,768]{3,2,1,0:T(8,128)(2,1)}, u32[]{:S(2)}, u32[]{:S(2)}) collective-permute-start(bf16[2,1,192,768]{3,2,1,0:T(8,128)(2,1)} %fusion.2), channel_id=1, source_target_pairs={{0,4},{1,5},{2,6},{3,7},{4,0},{5,1},{6,2},{7,3},{8,12},{9,13},{10,... | collective-permute-start | bytes 1769480 | tf_op jit(solution)/shard_map/ppermute | solution.py:668
  140.4 15.8 %collective-permute-start.3 = (bf16[96,3072]{1,0:T(8,128)(2,1)}, bf16[96,3072]{1,0:T(8,128)(2,1)S(1)}, u32[]{:S(2)}, u32[]{:S(2)}) collective-permute-start(bf16[96,3072]{1,0:T(8,128)(2,1)} %get-tuple-element.97), channel_id=1, source_target_pairs={{0,2},{1,3},{2,0},{3,1},{4,6},{5,7},{6,4},{7,5},{8,10},{9,11},{10,... | collective-permute-start | bytes 1769480 | tf_op jit(solution)/shard_map/ppermute | solution.py:668
  156.2 1.3 copy-start.4
  157.5 39.6 %collective-permute-start.4 = (bf16[192,3200]{1,0:T(8,128)(2,1)}, bf16[192,3200]{1,0:T(8,128)(2,1)S(1)}, u32[]{:S(2)}, u32[]{:S(2)}) collective-permute-start(bf16[192,3200]{1,0:T(8,128)(2,1)} %get-tuple-element.114), channel_id=1, source_target_pairs={{0,2},{1,3},{2,0},{3,1},{4,6},{5,7},{6,4},{7,5},{8,10},{9,11},{10,... | collective-permute-start | bytes 3686408 | tf_op jit(solution)/shard_map/ppermute | solution.py:668
  158.7 37.5 %collective-permute-start.8 = (bf16[48,3072]{1,0:T(8,128)(2,1)S(1)}, bf16[48,3072]{1,0:T(8,128)(2,1)S(1)}, u32[]{:S(2)}, u32[]{:S(2)}) collective-permute-start(bf16[48,3072]{1,0:T(8,128)(2,1)S(1)} %add_convert_fusion.9), channel_id=1, source_target_pairs={{0,8},{1,9},{2,10},{3,11},{4,12},{5,13},{6,14},{7,15},{8,0},{9,1},... | collective-permute-start | bytes 884744 | tf_op jit(solution)/shard_map/ppermute | solution.py:668
  161.3 32.8 %collective-permute-start.9 = (bf16[1,1,192,768]{3,2,1,0:T(8,128)(2,1)S(1)}, bf16[1,1,192,768]{3,2,1,0:T(8,128)(2,1)}, u32[]{:S(2)}, u32[]{:S(2)}) collective-permute-start(bf16[1,1,192,768]{3,2,1,0:T(8,128)(2,1)S(1)} %fusion.4), channel_id=1, source_target_pairs={{0,8},{1,9},{2,10},{3,11},{4,12},{5,13},{6,14},{7,15},{8,0},{9,1},... | collective-permute-start | bytes 884744 | tf_op jit(solution)/shard_map/ppermute | solution.py:668
  161.6 34.6 %copy-start.5 = (bf16[96,3072]{1,0:T(8,128)(2,1)S(1)}, bf16[96,3072]{1,0:T(8,128)(2,1)}, u32[]{:S(2)}) copy-start(bf16[96,3072]{1,0:T(8,128)(2,1)} %copy-done.4) | copy-start | bytes 1769476
  194.1 3.0 %copy-start.1 = (bf16[192,3200]{1,0:T(8,128)(2,1)S(1)}, bf16[192,3200]{1,0:T(8,128)(2,1)}, u32[]{:S(2)}) copy-start(bf16[192,3200]{1,0:T(8,128)(2,1)} %get-tuple-element.113) | copy-start | bytes 3686404
  197.4 46.1 %collective-permute-start.6 = (bf16[96,3200]{1,0:T(8,128)(2,1)S(1)}, bf16[96,3200]{1,0:T(8,128)(2,1)S(1)}, u32[]{:S(2)}, u32[]{:S(2)}) collective-permute-start(bf16[96,3200]{1,0:T(8,128)(2,1)S(1)} %get-tuple-element.122), channel_id=1, source_target_pairs={{0,4},{1,5},{2,6},{3,7},{4,0},{5,1},{6,2},{7,3},{8,12},{9,13},{10,... | collective-permute-start | bytes 1843208 | tf_op jit(solution)/shard_map/ppermute | solution.py:668
  239.9 15.6 %copy-start.6 = (bf16[48,3200]{1,0:T(8,128)(2,1)S(1)}, bf16[48,3200]{1,0:T(8,128)(2,1)}, u32[]{:S(2)}) copy-start(bf16[48,3200]{1,0:T(8,128)(2,1)} %get-tuple-element.121) | copy-start | bytes 921604
  240.9 14.6 %collective-permute-start.5 = (bf16[24,3200]{1,0:T(8,128)(2,1)S(1)}, bf16[24,3200]{1,0:T(8,128)(2,1)S(1)}, u32[]{:S(2)}, u32[]{:S(2)}) collective-permute-start(bf16[24,3200]{1,0:T(8,128)(2,1)S(1)} %slice.111), channel_id=1, source_target_pairs={{0,8},{1,9},{2,10},{3,11},{4,12},{5,13},{6,14},{7,15},{8,0},{9,1},... | collective-permute-start | bytes 460808 | tf_op jit(solution)/shard_map/ppermute | solution.py:668
  243.6 16.2 %collective-permute-start.7 = (bf16[48,3200]{1,0:T(8,128)(2,1)S(1)}, bf16[48,3200]{1,0:T(8,128)(2,1)S(1)}, u32[]{:S(2)}, u32[]{:S(2)}) collective-permute-start(bf16[48,3200]{1,0:T(8,128)(2,1)S(1)} %add_convert_fusion.6), channel_id=1, source_target_pairs={{0,8},{1,9},{2,10},{3,11},{4,12},{5,13},{6,14},{7,15},{8,0},{9,1},... | collective-permute-start | bytes 921608 | tf_op jit(solution)/shard_map/ppermute | solution.py:668
  258.2 6.7 %copy-start = (bf16[36,24,768]{2,1,0:T(8,128)(2,1)S(1)}, bf16[36,24,768]{2,1,0:T(8,128)(2,1)}, u32[]{:S(2)}) copy-start(bf16[36,24,768]{2,1,0:T(8,128)(2,1)} %get-tuple-element.120) | copy-start | bytes 3981316

commit v3 on v2

v3 whole, which is shorter than its diff:
```python
import functools

import jax
import jax.numpy as jnp
from jax import lax
from jax.experimental import pallas as pl
from jax.experimental.pallas import tpu as pltpu
from jax.sharding import PartitionSpec as P

HEADS = 12
HEAD_DIM = 64
PAIRS = HEADS // 2
LANES = 2 * HEAD_DIM
TILE = 8
WIDTH = HEADS * HEAD_DIM
MESH = pl.DeviceIdType.MESH

norm_eps = 1e-06
masked_score = -1000000000.0
vmem_limit = 63 * 1024 * 1024

f32 = jnp.float32
bf16 = jnp.bfloat16


def dot(left, right):
    return jnp.dot(left, right, preferred_element_type=f32)


def dot_nt(left, right):
    return lax.dot_general(left, right, (((1,), (1,)), ((), ())), preferred_element_type=f32)


def dot_tn(left, right):
    return lax.dot_general(left, right, (((0,), (0,)), ((), ())), preferred_element_type=f32)


def norm_parts(summed):
    centred = summed - jnp.mean(summed, axis=-1, keepdims=True)
    scaled = lax.rsqrt(jnp.mean(centred * centred, axis=-1, keepdims=True) + norm_eps)
    return centred * scaled, scaled


def norm_backward(upstream, normed, scaled, gain):
    inner = upstream * gain
    return scaled * (
        inner
        - jnp.mean(inner, axis=-1, keepdims=True)
        - normed * jnp.mean(inner * normed, axis=-1, keepdims=True)
    )


def row_sum(rows):
    return jnp.sum(rows, axis=0, keepdims=True)


def gelu_parts(entries):
    size = jnp.abs(entries)
    bell = jnp.exp(entries * entries * -0.5)
    t = 1.0 / (1.0 + size * (0.3275911 * 0.7071067811865476))
    poly = t * (
        0.5 * 0.254829592
        + t
        * (
            0.5 * -0.284496736
            + t * (0.5 * 1.421413741 + t * (0.5 * -1.453152027 + t * (0.5 * 1.061405429)))
        )
    )
    tail = poly * bell
    area = jnp.where(entries >= 0.0, 1.0 - tail, tail)
    return entries * area, area + entries * bell * 0.3989422804014327


def padded(slots):
    return -(-slots // TILE) * TILE


def lane_tiles(ref, at, count):
    return jnp.concatenate([ref[at + tile, :count] for tile in range(PAIRS)], axis=1)


def to_pairs(stage, ref, at, rows, slots):
    count, high = rows.shape[0], padded(slots)
    for tile in range(PAIRS):
        stage[tile, :count] = rows[:, tile * LANES : (tile + 1) * LANES]
    for group in range(TILE // 2):
        for tile in range(PAIRS):
            ref[group, :, at + tile * LANES : at + (tile + 1) * LANES] = pair_rows(stage, tile, group, high).astype(bf16)


def pair_rows(stage, tile, group, high):
    return jnp.concatenate(
        [stage[tile, pl.ds(2 * group + item, high, stride=TILE), :] for item in range(2)], axis=0)


def put_pair(stage, tile, group, rows, high):
    for item in range(2):
        stage[tile, pl.ds(2 * group + item, high, stride=TILE), :] = rows[item * high : (item + 1) * high]


def clear_padding(stage, slots):
    stage[:, slots * TILE :] = jnp.zeros((stage.shape[0], stage.shape[1] - slots * TILE, LANES), f32)


def pair_mask(len_ref, first, high):
    shape = (2 * high, 2 * high)
    row = lax.broadcasted_iota(jnp.int32, shape, 0)
    col = lax.broadcasted_iota(jnp.int32, shape, 1)
    second = row >= high
    low = jnp.where(second, high, 0)
    end = jnp.where(second, high + len_ref[pl.ds(first + 1, 1), : 2 * high], len_ref[pl.ds(first, 1), : 2 * high])
    allowed = (col >= low) & (col < end)
    return jnp.concatenate([allowed, allowed], axis=0)


def first_head(shape):
    return lax.broadcasted_iota(jnp.int32, shape, 1) < HEAD_DIM


def head_stack(rows):
    low, zero = first_head(rows.shape), jnp.zeros_like(rows)
    return jnp.concatenate([jnp.where(low, rows, zero), jnp.where(low, zero, rows)], axis=0)


def head_merge(stacked):
    count = stacked.shape[0] // 2
    return jnp.where(first_head((count, stacked.shape[1])), stacked[:count], stacked[count:])


def batches(size):
    everything = [(group, pair) for group in range(TILE // 2) for pair in range(PAIRS)]
    return [everything[at : at + size] for at in range(0, len(everything), size)]


def head_block(ref, group, part, pair):
    return ref[group, :, part * WIDTH + pair * LANES : part * WIDTH + (pair + 1) * LANES]


def attend(triple_ref, probs_ref, context_ref, stage, len_ref, first_item, slots):
    high = padded(slots)
    ones = jnp.ones((2 * high, LANES), bf16)
    masks = [pair_mask(len_ref, first_item + 2 * group, high) for group in range(TILE // 2)]
    for batch in batches(12):
        scores = [
            jnp.where(
                masks[group],
                dot_nt(head_stack(head_block(triple_ref, group, 0, pair)), head_block(triple_ref, group, 1, pair)),
                masked_score,
            )
            for group, pair in batch
        ]
        largest = [jnp.max(entry, axis=-1, keepdims=True) for entry in scores]
        weights = [jnp.exp(entry - top).astype(bf16) for entry, top in zip(scores, largest)]
        both = [
            dot(entry, jnp.concatenate([head_block(triple_ref, group, 2, pair), ones], axis=1))
            for (group, pair), entry in zip(batch, weights)
        ]
        for (group, pair), entry, sums in zip(batch, weights, both):
            inverse = 1.0 / sums[:, LANES:]
            probs_ref[group, pair] = (entry.astype(f32) * inverse[:, : 2 * high]).astype(bf16)
            context = head_merge(sums[:, :LANES] * inverse)
            context_ref[group, :, pair * LANES : (pair + 1) * LANES] = context
            put_pair(stage, pair, group, context, high)


def attend_back(triple_ref, probs_ref, context_ref, stage, out_stage, slots):
    high = padded(slots)
    ones = jnp.ones((2 * high, LANES), bf16)
    low = first_head((2 * high, LANES))
    for batch in batches(6):
        stacks, grad_probs = [], []
        for group, pair in batch:
            grads = pair_rows(stage, pair, group, high)
            delta = -grads * context_ref[group, :, pair * LANES : (pair + 1) * LANES]
            upper = delta.astype(bf16)
            lower = pltpu.roll(delta - upper.astype(f32), HEAD_DIM, 1).astype(bf16)
            deltas = jnp.concatenate([jnp.where(low, upper, lower), jnp.where(low, lower, upper)], axis=0)
            stacks.append(head_stack(grads.astype(bf16)))
            values = head_block(triple_ref, group, 2, pair)
            grad_probs.append(
                dot_nt(jnp.concatenate([stacks[-1], deltas], axis=1), jnp.concatenate([values, ones], axis=1)))
        grad_scores = [
            (probs_ref[group, pair].astype(f32) * entry).astype(bf16) for (group, pair), entry in zip(batch, grad_probs)]
        grad_queries = [dot(entry, head_block(triple_ref, group, 1, pair)) for (group, pair), entry in zip(batch, grad_scores)]
        grad_values = [dot_tn(probs_ref[group, pair], entry) for (group, pair), entry in zip(batch, stacks)]
        grad_keys = [
            dot_tn(entry, head_stack(head_block(triple_ref, group, 0, pair))) for (group, pair), entry in zip(batch, grad_scores)]
        for at, (group, pair) in enumerate(batch):
            put_pair(out_stage, pair, group, head_merge(grad_queries[at]) * HEAD_DIM**-0.5, high)
            put_pair(out_stage, PAIRS + pair, group, grad_keys[at], high)
            put_pair(out_stage, 2 * PAIRS + pair, group, grad_values[at], high)


def across(axis, bit):
    place, weight = lax.axis_index(axis), 1 << bit
    return {axis: place + weight - 2 * weight * ((place // weight) % 2)}


def own_bit(axis, bit):
    return (lax.axis_index(axis) // (1 << bit)) % 2


def greet(partners):
    barrier = pltpu.get_barrier_semaphore()
    for partner in partners:
        pl.semaphore_signal(barrier, inc=1, device_id=partner, device_id_type=MESH)
    pl.semaphore_wait(barrier, len(partners))


def remote_copy(source, target, sems, at, partner):
    return pltpu.make_async_remote_copy(
        src_ref=source, dst_ref=target, send_sem=sems[0].at[at], recv_sem=sems[1].at[at],
        device_id=partner, device_id_type=MESH)


def row_slices(slots):
    step = 6 if slots % 6 == 0 else slots
    return [slice(at * TILE, (at + step) * TILE) for at in range(0, slots, step)]


def fold(rows):
    return jnp.sum(rows.reshape(rows.shape[0] // TILE, TILE, rows.shape[1]), axis=0)


def norm_rows(wide, normed_ref, scale_ref, gain, shift, low, slots):
    for rows in row_slices(slots):
        normed, scale = norm_parts(wide[rows])
        normed_ref[rows] = normed
        scale_ref[rows] = scale
        result = normed * gain + shift
        wide[rows] = result
        if low is not None:
            low[rows] = result.astype(bf16)


def norm_back_rows(upstream_ref, normed_ref, scale_ref, gain, grad_ref, low_ref, vec_sum, slots):
    sums = [0.0, 0.0, 0.0]
    for rows in row_slices(slots):
        upstream, normed = upstream_ref[rows], normed_ref[rows]
        grad = norm_backward(upstream, normed, scale_ref[rows], gain)
        low = grad.astype(bf16)
        grad_ref[rows] = grad
        low_ref[rows] = low
        sums = [total + fold(part) for total, part in zip(sums, (low.astype(f32), upstream * normed, upstream))]
    for at, total in enumerate(sums):
        vec_sum[2 + at : 3 + at] += row_sum(total)


def forward_kernel(
    slots, steps,
    lengths, whole, hidden, cross_proj_at, cross_out_at, self_proj_at, self_out_at, cross_bias, cross_norm, self_bias, self_norm,
    dense, far_dense, triple1, probs1, contexts1, context1, normed1, scale1,
    triple2, probs2, contexts2, context2, normed2, scale2,
    wide, low, stage, context_stage, far, lens, far_lens, cross_proj, cross_out, self_proj, self_out, send_sem, recv_sem, load_sem,
):
    count = slots * TILE
    step = pl.program_id(0)
    partner = across("stream", 0)
    sources = [cross_proj_at, cross_out_at, self_proj_at.at[0], self_out_at.at[0]]
    loads = [
        pltpu.make_async_copy(source, target, load_sem.at[at])
        for at, (source, target) in enumerate(zip(sources, [cross_proj, cross_out, self_proj, self_out]))
    ]

    def travel(part):
        if part == steps:
            source, target = lens, far_lens
        else:
            source, target = whole.at[:, pl.ds(part * TILE, TILE)], far.at[part]
        return remote_copy(source, target, (send_sem, recv_sem), part, partner)

    @pl.when(step == 0)
    def _():
        loads[0].start()
        for item in range(lens.shape[0]):
            lens[item : item + 1] = jnp.full((1, LANES), lengths[0, item], jnp.int32)
        greet([partner])
        travel(steps).start()
        for part in range(steps):
            travel(part).start()
        for load in loads[1:]:
            load.start()
        clear_padding(stage, slots)
        loads[0].wait()

    rows = hidden[...].astype(f32).reshape(count, WIDTH)
    wide[...] = rows
    dense[...] = rows.astype(bf16)
    queries = (dot(dense[...], cross_proj[:, :WIDTH]) + cross_bias[0:1]).astype(bf16).astype(f32)
    to_pairs(stage, triple1, 0, queries * HEAD_DIM**-0.5, slots)

    @pl.when(step == 0)
    def _():
        travel(steps).wait()
        for load in loads[1:]:
            load.wait()

    for part in range(steps):

        @pl.when(step == part)
        def _():
            travel(part).wait()

    far_dense[...] = far[step].astype(f32).reshape(count, WIDTH).astype(bf16)
    to_pairs(stage, triple1, WIDTH, dot(far_dense[...], cross_proj[:, WIDTH : 2 * WIDTH]), slots)
    to_pairs(stage, triple1, 2 * WIDTH, dot(far_dense[...], cross_proj[:, 2 * WIDTH :]) + cross_bias[1:2], slots)
    attend(triple1, probs1, contexts1, context_stage, far_lens, step * TILE, slots)
    context1[...] = lane_tiles(context_stage, 0, count).astype(bf16)
    wide[...] += dot(context1[...], cross_out[...]) + cross_bias[2:3]
    norm_rows(wide, normed1, scale1, cross_norm[0:1], cross_norm[1:2], low, slots)
    queries = (dot(low[...], self_proj[:, :WIDTH]) + self_bias[0, 0:1]).astype(bf16).astype(f32)
    to_pairs(stage, triple2, 0, queries * HEAD_DIM**-0.5, slots)
    to_pairs(stage, triple2, WIDTH, dot(low[...], self_proj[:, WIDTH : 2 * WIDTH]), slots)
    to_pairs(stage, triple2, 2 * WIDTH, dot(low[...], self_proj[:, 2 * WIDTH :]) + self_bias[0, 1:2], slots)
    attend(triple2, probs2, contexts2, context_stage, lens, step * TILE, slots)
    context2[...] = lane_tiles(context_stage, 0, count).astype(bf16)
    wide[...] += dot(context2[...], self_out[...]) + self_bias[0, 2:3]
    for rows in row_slices(slots):
        normed, scale = norm_parts(wide[rows])
        normed2[rows] = normed
        scale2[rows] = scale


def order_rows(digits, share):
    shape = (WIDTH, WIDTH)
    row, col = (lax.broadcasted_iota(jnp.int32, shape, dim) for dim in range(2))
    block, spot = col // share, 0
    for axis, bit, weight in digits:
        mine, other = own_bit(axis, bit), (block // weight) % 2
        spot = 2 * spot + mine + other - 2 * mine * other
    return jnp.where(row == spot * share + col % share, 1.0, 0.0).astype(bf16)


def own_first(digits, block):
    spot = 0
    for axis, bit, weight in digits:
        mine, other = own_bit(axis, bit), (block // weight) % 2
        spot = 2 * spot + mine + other - 2 * mine * other
    return spot


class Products:
    def __init__(self, share, both, inbox, sems, wide=None, order=None):
        self.share, self.both, self.inbox, self.sems, self.wide, self.order = share, both, inbox, sems, wide, order
        self.half = WIDTH // 2
        self.small = self.share % (TILE if wide is not None else 2 * TILE) != 0

    def travel(self, at):
        return remote_copy(self.both.at[at, pl.ds(self.half, self.half)], self.inbox.at[at], self.sems, at, across("dp", 0))

    def put(self, at, product, digits):
        columns = slice(0, product.shape[1])
        if self.small:
            self.both[at, :, columns] = dot(order_rows(digits, self.share), product.astype(bf16)).astype(bf16)
        elif self.wide is not None:
            for block in range(WIDTH // self.share):
                spot = pl.multiple_of(own_first(digits, block) * self.share, TILE)
                self.wide[pl.ds(spot, self.share), columns] = product[block * self.share : (block + 1) * self.share]
            self.both[at, :, columns] = self.wide[:, columns].astype(bf16)
        else:
            for block in range(WIDTH // self.share):
                spot = pl.multiple_of(own_first(digits, block) * self.share, 2 * TILE)
                self.both[at, pl.ds(spot, self.share), columns] = product[block * self.share : (block + 1) * self.share].astype(bf16)
        self.travel(at).start()

    def send(self, at, left, right, digits):
        self.put(at, dot_tn(left, right), digits)

    def send_sums(self, at, sums, digits):
        self.put(at, sums.T, digits)

    def keep(self, at, wide=WIDTH):
        self.travel(at).wait()
        return self.both[at, : self.half, :wide].astype(f32) + self.inbox[at, :, :wide].astype(f32)


class Halving:
    def __init__(self, now, boxes, sems, base, partners, first=None):
        self.now, self.boxes, self.sems, self.base, self.partners, self.first = now, boxes, sems, base, partners, first

    def travel(self, stage):
        box = self.boxes[stage]
        source = self.first
        if stage > 0 or source is None:
            source = self.now.at[pl.ds(box.shape[0], box.shape[0])]
        return remote_copy(source, box, self.sems, self.base + stage, self.partners[stage])

    def start(self, stage):
        self.travel(stage).start()

    def total(self, stage):
        self.travel(stage).wait()
        box = self.boxes[stage]
        return self.now[: box.shape[0]].astype(f32) + box[...].astype(f32)

    def finish(self, stage):
        self.now[: self.boxes[stage].shape[0]] = self.total(stage).astype(bf16)


def ffn_rows(
    slots, step, live, normed2, cotangent, self_norm, ffn_up, up_bias, ffn_down, down_bias, ffn_norm, down_load,
    output, grad_attended, attended_low, activated, grad_last_low, grad_expanded, up_sum, vec_sum, slope, wide,
):
    count = slots * TILE
    here = pl.ds(pl.multiple_of(step * count, count), count)
    chunks = ffn_up.shape[1] // WIDTH
    attended = normed2[...] * self_norm[0, 0:1] + self_norm[0, 1:2]
    attended_low[here] = attended.astype(bf16)
    wide[...] = attended + down_bias[...]
    parts = [slice(chunk * WIDTH, (chunk + 1) * WIDTH) for chunk in range(chunks)]

    def rise(part):
        return dot(attended_low[here], ffn_up[:, part]) + up_bias[:, part]

    entries = rise(parts[0])
    for number, part in enumerate(parts):
        later = rise(parts[number + 1]) if number + 1 < chunks else None
        active, steep = gelu_parts(entries)
        activated[here, part] = active.astype(bf16)
        slope[:, part] = steep
        if number == 0:

            @pl.when(step == 0)
            def _():
                down_load.wait()

        wide[...] += dot(activated[here, part], ffn_down[part, :])
        entries = later
    each = slots // len(row_slices(slots))
    sums = [0.0, 0.0, 0.0]
    alive = jnp.concatenate([live[...]] * PAIRS, axis=1)
    for number, rows in enumerate(row_slices(slots)):
        spots = slice(number * each, (number + 1) * each)
        shape = (each, TILE, WIDTH)
        normed, scale = norm_parts(wide[rows])
        output[spots] = (normed * ffn_norm[0, 0:1] + ffn_norm[0, 1:2]).reshape(shape).astype(bf16)
        slot = lax.broadcasted_iota(jnp.int32, shape, 0) + number * each
        upstream = jnp.where(slot < alive[None], cotangent[spots].astype(f32), 0.0).reshape(each * TILE, WIDTH)
        grad = norm_backward(upstream, normed, scale, ffn_norm[0, 0:1])
        low = grad.astype(bf16)
        wide[rows] = grad
        grad_last_low[pl.ds(pl.multiple_of(step * count + number * each * TILE, each * TILE), each * TILE)] = low
        sums = [total + fold(part) for total, part in zip(sums, (low.astype(f32), upstream * normed, upstream))]
    for at, total in enumerate(sums):
        vec_sum[at : at + 1] += row_sum(total)
    grad_low = grad_last_low[here]
    total = wide[...]
    for part in parts:
        grad_up = (dot_nt(grad_low, ffn_down[part, :]) * slope[:, part]).astype(bf16)
        grad_expanded[here, part] = grad_up
        up_sum[:, part] += row_sum(grad_up.astype(f32))
        total = total + dot_nt(grad_up, ffn_up[:, part])
    grad_attended[...] = total


def ffn_kernel(
    slots, steps, down_digits, down_share, up_digits, up_share, chunk_digits,
    lengths, flags, normed2, cotangent, ffn_up_at, ffn_down_at, self_norm, up_bias, down_bias, ffn_norm,
    output, grad_attended, up_sum, vec_sum, down_kept, down_sent, up_kept, up_sent,
    ffn_up, ffn_down, attended_low, activated, grad_last_low, grad_expanded, slope, wide, live,
    down_both, down_in, up_both, up_in, load_sem, down_send, down_recv, up_send, up_recv,
):
    step = pl.program_id(0)
    chunks = ffn_up.shape[1] // WIDTH
    loads = [
        pltpu.make_async_copy(ffn_up_at.at[0], ffn_up, load_sem.at[0]),
        pltpu.make_async_copy(ffn_down_at.at[0], ffn_down, load_sem.at[1]),
    ]

    @pl.when(step == 0)
    def _():
        for load in loads:
            load.start()
        greet([across("dp", 0)])
        up_sum[...] = jnp.zeros_like(up_sum)
        vec_sum[...] = jnp.zeros_like(vec_sum)
        loads[0].wait()

    @pl.when(step < steps)
    def _():
        for item in range(TILE):
            count = jnp.where(flags[0, step * TILE + item] > 0, lengths[0, step * TILE + item], 0)
            live[item : item + 1] = jnp.full((1, LANES), count, jnp.int32)
        ffn_rows(
            slots, step, live, normed2, cotangent, self_norm, ffn_up, up_bias, ffn_down, down_bias, ffn_norm, loads[1],
            output, grad_attended, attended_low, activated, grad_last_low, grad_expanded, up_sum, vec_sum, slope, wide)

    @pl.when(step == steps)
    def _():
        quarter = WIDTH // 4
        down = Products(down_share, down_both, down_in, (down_send, down_recv))
        up = Products(up_share, up_both, up_in, (up_send, up_recv))
        inner = quarter // down_share

        def keep_down(chunk):
            product = down.keep(chunk).astype(bf16)
            place = own_first(chunk_digits, chunk)
            for piece in range(inner):
                spot = pl.ds(pl.multiple_of((piece * chunks + place) * down_share, 16), down_share)
                from_own = slice(piece * down_share, (piece + 1) * down_share)
                from_other = slice(quarter + piece * down_share, quarter + (piece + 1) * down_share)
                down_kept[spot, :] = product[from_own]
                down_sent[spot, :] = product[from_other]

        def keep_up(chunk):
            product = up.keep(chunk).astype(bf16)
            at = slice(chunk * WIDTH, (chunk + 1) * WIDTH)
            up_kept[:, at] = product[:quarter]
            up_sent[:, at] = product[quarter:]

        for chunk in range(chunks):
            down.send(chunk, activated[:, chunk * WIDTH : (chunk + 1) * WIDTH], grad_last_low[...], down_digits)
            if chunk > 1:
                keep_down(chunk - 2)
        for chunk in range(chunks):
            up.send(chunk, attended_low[...], grad_expanded[:, chunk * WIDTH : (chunk + 1) * WIDTH], up_digits)
            if chunk < 2:
                keep_down(chunks - 2 + chunk)
            else:
                keep_up(chunk - 2)
        keep_up(chunks - 2)
        keep_up(chunks - 1)


def context_back(low, out, triple, probs, contexts, grad_triple, here, vec_sum, stage, out_stage, slots):
    count = slots * TILE
    grads = dot_nt(low, out).astype(bf16).astype(f32)
    for tile in range(PAIRS):
        stage[tile, :count] = grads[:, tile * LANES : (tile + 1) * LANES]
    attend_back(triple, probs, contexts, stage, out_stage, slots)
    for part in range(3):
        rows = lane_tiles(out_stage, part * PAIRS, count).astype(bf16)
        grad_triple[here, part * WIDTH : (part + 1) * WIDTH] = rows
        if part != 1:
            vec_sum[part // 2 : part // 2 + 1] += row_sum(rows.astype(f32))


def self_kernel(
    slots, steps, digits, z_digits, share,
    grad_attended, normed2, scale2, normed1, triple2, probs2, contexts2,
    cross_norm, self_norm, ffn_sum, up_sum, self_proj_at, self_out_at, context_at,
    down_kept, down_sent, up_kept, up_sent,
    grad_crossed, down_half, up_half, self_kept, self_sent,
    stage, out_stage, self_proj, self_out, context, crossed_low, grad_mid_low, grad_triple, vec_sum,
    both, inbox,
    down_now, down_box1, down_box2, up_now, up_box1, up_box2, load_sem, send_sem, recv_sem, sum_send, sum_recv,
):
    step = pl.program_id(0)
    count = slots * TILE
    here = pl.ds(pl.multiple_of(step * count, count), count)
    near, next_one = across("dp", 1), across("dp", 2)
    sums = (sum_send, sum_recv)
    early, late = [], []
    for number, (now, boxes, route, sent) in enumerate((
        (down_now, (down_box1, down_box2), [near, next_one], down_sent), (up_now, (up_box1, up_box2), [next_one, near], up_sent),
    )):
        cut = now.shape[1] // 2
        for place, group in enumerate((early, late)):
            columns = pl.ds(place * cut, cut)
            group.append(Halving(
                now.at[:, columns], [box.at[:, columns] for box in boxes], sums, 4 * number + 2 * place, route, sent.at[:, columns]))
    pairs = [
        (self_out_at.at[0], self_out), (self_proj_at.at[0], self_proj), (down_kept, down_now), (up_kept, up_now),
        (context_at, context),
    ]
    loads = [pltpu.make_async_copy(source, target, load_sem.at[at]) for at, (source, target) in enumerate(pairs)]

    @pl.when(step == 0)
    def _():
        loads[0].start()
        greet([across("dp", 0), near, next_one])
        for part in early:
            part.start(0)
        for load in loads[1:]:
            load.start()
        vec_sum[...] = jnp.zeros_like(vec_sum)
        clear_padding(stage, slots)
        loads[0].wait()
        loads[1].wait()

    @pl.when(step < steps)
    def _():
        norm_back_rows(grad_attended, normed2, scale2, self_norm[0, 0:1], grad_crossed, grad_mid_low.at[here], vec_sum, slots)
        crossed_low[here] = (normed1[...] * cross_norm[0:1] + cross_norm[1:2]).astype(bf16)
        context_back(grad_mid_low[here], self_out[...], triple2, probs2, contexts2, grad_triple, here, vec_sum, stage, out_stage, slots)
        grad_crossed[...] += dot_nt(grad_triple[here], self_proj[...])

    @pl.when(step == 0)
    def _():
        for part in late:
            part.start(0)

    @pl.when(step == steps - 2)
    def _():
        loads[2].wait()
        loads[3].wait()
        for part in early:
            part.finish(0)
            part.start(1)

    @pl.when(step == steps)
    def _():
        loads[4].wait()
        vec_sum[8:11] = ffn_sum[...]
        chunks = up_sum.shape[1] // WIDTH
        for chunk in range(chunks):
            vec_sum[16 + chunk : 17 + chunk] = up_sum[:, chunk * WIDTH : (chunk + 1) * WIDTH]
        quarter = WIDTH // 4
        products = Products(share, both, inbox, (send_sem, recv_sem))
        orders = [digits, digits, digits, z_digits, z_digits]

        def keep(at, wide=WIDTH):
            product = products.keep(at, wide).astype(bf16)
            columns = slice(at * WIDTH, at * WIDTH + wide)
            self_kept[:, columns] = product[:quarter]
            self_sent[:, columns] = product[quarter:]

        for part in range(3):
            products.send(part, crossed_low[...], grad_triple[:, part * WIDTH : (part + 1) * WIDTH], orders[part])
            if part > 0:
                keep(part - 1)
        products.send(3, context[...], grad_mid_low[...], orders[3])
        keep(2)
        turned = vec_sum[...].T
        lane = lax.broadcasted_iota(jnp.int32, (share, LANES), 1)
        wide = [jnp.broadcast_to(turned[:, 16 + chunk : 17 + chunk], (WIDTH, LANES)) for chunk in range(chunks)]
        pieces = []
        for place in range(WIDTH // share):
            piece = turned[place * share : (place + 1) * share]
            for column in range(chunks):
                source = (place * chunks + column) * share
                rows = wide[source // WIDTH][source % WIDTH : source % WIDTH + share]
                piece = jnp.where(lane == 11 + column, rows, piece)
            pieces.append(piece)
        products.put(4, jnp.concatenate(pieces, axis=0), orders[4])
        keep(3)
        keep(4, LANES)
        for part in late:
            part.finish(0)
        for part in early:
            part.finish(1)
        down_half[...] = down_now[...]
        up_half[...] = up_now[...]


def cross_kernel(
    slots, steps, digits, share, finish,
    grad_crossed, normed1, scale1, triple1, probs1, contexts1,
    cross_norm, cross_proj_at, cross_out_at, dense_at, far_at, context_at,
    down_at, up_at, self_kept, self_sent,
    grad_hidden, own_down, own_up, self_result, cross_result,
    stage, out_stage, cross_proj, cross_out, lefts, grad_cross_low, grad_triple, grad_own, vec_sum,
    dx_out, dx_in, both, inbox, wide, total, box1, box2, box3, last_out, last_in,
    down_now, down_box1, down_box2, up_now, up_box1, up_box2, self_now, self_box1, self_box2, self_box3,
    load_sem, send_sem, recv_sem, dx_send, dx_recv, sum_send, sum_recv, part_send, part_recv, out_sem,
):
    step = pl.program_id(0)
    count = slots * TILE
    here = pl.ds(pl.multiple_of(step * count, count), count)
    links = [across("stream", 0), across("dp", 1), across("dp", 2)]
    sums = (sum_send, sum_recv)
    last = across("dp", 3)
    early, late = [], []
    for number, (now, boxes, route) in enumerate((
        (down_now, (down_box1, down_box2), [links[2], last]), (up_now, (up_box1, up_box2), [links[1], last]),
    )):
        cut = now.shape[1] // 2
        high = now.shape[0] // 2
        early.append(Halving(
            now.at[pl.ds(0, high), pl.ds(0, cut)], [boxes[1].at[:, pl.ds(0, cut)]], sums, 8 + number, route[1:]))
        columns = pl.ds(cut, cut)
        late.append(Halving(now.at[:, columns], [box.at[:, columns] for box in boxes], sums, 10 + 2 * number, route))
    middle = 3 * WIDTH
    own = []
    for number, (columns, route) in enumerate((
        (pl.ds(0, middle), [links[1], links[2], last]), (pl.ds(middle, self_now.shape[1] - middle), [links[2], links[1], last]),
    )):
        boxes = [box.at[:, columns] for box in (self_box1, self_box2, self_box3)]
        own.append(Halving(self_now.at[:, columns], boxes, sums, 3 * number, route, self_sent.at[:, columns]))
    pairs = [
        (cross_out_at, cross_out), (cross_proj_at, cross_proj), (down_at, down_now), (up_at, up_now), (self_kept, self_now),
        (dense_at, lefts.at[0]), (far_at, lefts.at[1]), (context_at, lefts.at[0]),
    ]
    loads = [pltpu.make_async_copy(source, target, load_sem.at[at]) for at, (source, target) in enumerate(pairs)]

    def travel(part):
        return remote_copy(dx_out.at[part], dx_in.at[part], (dx_send, dx_recv), part, links[0])

    @pl.when(step == 0)
    def _():
        for at in (0, 2, 3, 1, 4):
            loads[at].start()
        greet(links + [last, across("dp", 0)])
        loads[2].wait()
        loads[3].wait()
        for part in early + late + own:
            part.start(0)
        for at in (5, 6):
            loads[at].start()
        vec_sum[...] = jnp.zeros_like(vec_sum)
        clear_padding(stage, slots)
        loads[0].wait()
        loads[1].wait()

    @pl.when(step < steps)
    def _():
        norm_back_rows(grad_crossed, normed1, scale1, cross_norm[0:1], grad_own.at[here], grad_cross_low.at[here], vec_sum, slots)
        context_back(grad_cross_low[here], cross_out[...], triple1, probs1, contexts1, grad_triple, here, vec_sum, stage, out_stage, slots)
        dx_out[step] = dot_nt(grad_triple[here, WIDTH:], cross_proj[:, WIDTH:]).reshape(slots, TILE, WIDTH).astype(bf16)
        travel(step).start()
        grad_own[here] += dot_nt(grad_triple[here, :WIDTH], cross_proj[:, :WIDTH])

    @pl.when(step == steps - 2)
    def _():
        for part in late:
            part.finish(0)
            part.start(1)

    @pl.when(step == steps)
    def _():
        for at in range(4, len(loads) - 1):
            loads[at].wait()
        for part in own:
            part.finish(0)
            part.start(1)
        products = Products(share, both, inbox, (send_sem, recv_sem), wide)
        cut = 4 * WIDTH // 3
        bounds = [(0, cut), (cut, 2 * cut), (2 * cut, total.shape[-1])]
        routes = [(0, 1, 2), (1, 0, 2), (0, 1, 2)]
        boxes = [box1, box2, box3]

        def view(part, stage, sent):
            spot = [slice(None)] * 3
            for axis in routes[part][:stage]:
                spot[axis] = 0
            spot[routes[part][stage]] = sent
            return tuple(spot) + (slice(None), slice(*bounds[part]))

        def box_view(part, stage):
            wide = bounds[part][1] - bounds[part][0]
            return (part,) + (slice(None),) * (3 - stage) + (slice(0, wide),)

        def hop(part, stage):
            return remote_copy(
                total.at[view(part, stage, 1)], boxes[stage].at[box_view(part, stage)], (part_send, part_recv),
                3 * part + stage, links[routes[part][stage]])

        def keep(at, wide=WIDTH):
            product = products.keep(at, wide)
            total[:, :, :, :, at * WIDTH : at * WIDTH + wide] = product.reshape(2, 2, 2, product.shape[0] // 8, wide).astype(bf16)

        products.send(0, lefts[0], grad_triple[:, :WIDTH], digits)
        loads[7].start()
        products.send(1, lefts[1], grad_triple[:, WIDTH : 2 * WIDTH], digits)
        keep(0)
        products.send(2, lefts[1], grad_triple[:, 2 * WIDTH :], digits)
        keep(1)
        hop(0, 0).start()
        loads[7].wait()
        products.send(3, lefts[0], grad_cross_low[...], digits)
        keep(2)
        hop(1, 0).start()
        products.send_sums(4, vec_sum[...], digits)
        keep(3)
        keep(4, LANES)
        hop(2, 0).start()
        for part in own:
            part.finish(1)
            part.start(2)
        def leave(part):
            return pltpu.make_async_copy(dx_out.at[part], grad_hidden.at[:, pl.ds(part * TILE, TILE)], out_sem.at[part])

        def write(part):
            travel(part).wait()
            value = grad_own[part * count : (part + 1) * count].reshape(slots, TILE, WIDTH) + dx_in[part].astype(f32)
            dx_out[part] = value.astype(bf16)
            leave(part).start()

        for part in range(steps):
            write(part)
        last_rows = total.shape[3] // 2

        def last_hop(part):
            columns = pl.ds(bounds[part][0], bounds[part][1] - bounds[part][0])
            return remote_copy(last_out.at[:, columns], last_in.at[:, columns], (part_send, part_recv), 9 + part, last)

        kept = []
        for stage_at in range(3):
            for part in range(3):
                hop(part, stage_at).wait()
                spot = view(part, stage_at, 0)
                summed = total[spot].astype(f32) + boxes[stage_at][box_view(part, stage_at)].astype(f32)
                if stage_at < 2:
                    total[spot] = summed.astype(bf16)
                    hop(part, stage_at + 1).start()
                elif not finish:
                    cross_result[:, slice(*bounds[part])] = summed
                else:
                    kept.append(summed[:last_rows])
                    gap = jnp.zeros((last_out.shape[0] - last_rows, summed.shape[1]), f32)
                    last_out[:, slice(*bounds[part])] = jnp.concatenate([summed[last_rows:], gap], axis=0).astype(bf16)
                    last_hop(part).start()
        for first, second, result in zip(early, late, (own_down, own_up)):
            cut = result.shape[1] // 2
            result[:, :cut] = first.total(0)
            result[:, cut:] = second.total(1)
        self_result[...] = jnp.concatenate([part.total(2) for part in own], axis=1)
        if finish:
            for part in range(3):
                last_hop(part).wait()
            cross_result[...] = jnp.concatenate(kept, axis=1) + last_in[...].astype(f32)[:last_rows]
        for part in range(steps):
            leave(part).wait()


def unpack_kernel(
    output, grad_hidden, own_down, own_up, own_self, own_cross,
    output_to, grad_hidden_to, own_down_to, own_up_to, self_proj, self_out, self_bias, self_norm, down_bias, ffn_norm, up_bias,
    cross_proj, cross_out, cross_bias, cross_norm,
):
    for source, target in zip((output, grad_hidden, own_down, own_up), (output_to, grad_hidden_to, own_down_to, own_up_to)):
        target[...] = source[...]
    for source, wide, narrow in ((own_self, self_proj, self_out), (own_cross, cross_proj, cross_out)):
        wide[...] = source[:, : 3 * WIDTH]
        narrow[...] = source[:, 3 * WIDTH : 4 * WIDTH]
    small = own_self[:, 4 * WIDTH :].T
    self_bias[...] = small[0:3]
    self_norm[...] = small[3:5]
    down_bias[...] = small[8:9]
    ffn_norm[...] = small[9:11]
    chunks = up_bias.shape[1] // small.shape[1]
    up_bias[...] = jnp.concatenate([small[11 + chunk : 12 + chunk] for chunk in range(chunks)], axis=1)
    small = own_cross[:, 4 * WIDTH :].T
    cross_bias[...] = small[0:3]
    cross_norm[...] = small[3:5]


smem = pl.BlockSpec(memory_space=pltpu.SMEM)


def fixed(array):
    zeros = (0,) * array.ndim
    return pl.BlockSpec(array.shape, lambda i: zeros, pipeline_mode=pl.Buffered(1))


def rows_of(count, width):
    return pl.BlockSpec((count, width), lambda i: (i, 0))


def total_of(count, width):
    return pl.BlockSpec((count, width), lambda i: (0, 0))


def shape_of(shape, kind):
    return jax.ShapeDtypeStruct(shape, kind)


def flip(count, bit):
    return [(place, place ^ (1 << bit)) for place in range(count)]


def send(parts, axis, bit):
    return lax.ppermute(parts, axis, flip(lax.axis_size(axis), bit))


def local(
    hidden, lengths, task_flags, cotangent, cross_proj, cross_bias, cross_norm, cross_out, self_proj, self_bias,
    self_norm, self_out, ffn_up, up_bias, ffn_down, down_bias, ffn_norm,
):
    _, items, slots, width = hidden.shape
    deep = ffn_up.shape[2]
    rows = items * slots
    streams, places = lax.axis_size("stream"), lax.axis_size("dp")
    bits = places.bit_length() - 1
    steps = items // TILE
    size = TILE * slots
    high = padded(slots)
    groups = items // 2
    item_spec = pl.BlockSpec((slots, TILE, width), lambda i: (0, i, 0))
    row_spec = rows_of(size, width)
    scale_spec = rows_of(size, 1)
    wide_spec = rows_of(size, 3 * width)
    deep_spec = rows_of(size, deep)
    triple_spec = pl.BlockSpec((TILE // 2, 2 * high, 3 * width), lambda i: (i, 0, 0))
    pair_spec = pl.BlockSpec((TILE // 2, 2 * high, width), lambda i: (i, 0, 0))
    probs_spec = pl.BlockSpec((TILE // 2, PAIRS, 4 * high, 2 * high), lambda i: (i, 0, 0, 0))
    any_spec = pl.BlockSpec(memory_space=pl.ANY)
    row_f32, row_bf16 = shape_of((rows, width), f32), shape_of((rows, width), bf16)
    scale_f32 = shape_of((rows, 1), f32)
    wide_bf16, deep_bf16 = shape_of((rows, 3 * width), bf16), shape_of((rows, deep), bf16)
    triple_bf16 = shape_of((groups, 2 * high, 3 * width), bf16)
    pair_f32 = shape_of((groups, 2 * high, width), f32)
    probs_bf16 = shape_of((groups, PAIRS, 4 * high, 2 * high), bf16)
    sum_spec, sum_f32 = total_of(LANES, width), shape_of((LANES, width), f32)
    params = pltpu.CompilerParams(vmem_limit_bytes=vmem_limit)
    unit = 2 * rows * width * width
    stage = pltpu.VMEM((PAIRS, TILE * high, LANES), f32)
    out_stage = pltpu.VMEM((3 * PAIRS, TILE * high, LANES), f32)

    def remote(identity):
        return pltpu.CompilerParams(vmem_limit_bytes=vmem_limit, collective_id=identity, has_side_effects=True)

    def cost(units, count):
        return pl.CostEstimate(flops=units * unit, bytes_accessed=count, transcendentals=0)

    def scratch(*shape, kind=bf16):
        return pltpu.VMEM(shape, kind)

    def semaphores(count):
        return [pltpu.SemaphoreType.DMA((count,))] * 2

    vmem_spec = pl.BlockSpec(memory_space=pltpu.VMEM)

    def held(spec):
        return pl.BlockSpec(spec.block_shape, lambda i: spec.index_map(jnp.minimum(i, steps - 1)))

    def kept_out(*shape):
        zeros = (0,) * len(shape)
        return pl.BlockSpec(shape, lambda i: zeros)

    chunk_bits = (width * places // deep).bit_length() - 1
    share, cross_share = width // places, width // places // streams
    digits = [("dp", bit, 1 << bit) for bit in range(bits)]
    z_digits = [digits[0], digits[2], digits[1]] + digits[3:]
    cross_digits = [digits[0], ("stream", 0, places)] + digits[1:]
    slot_rows = jnp.transpose(hidden[0], (1, 0, 2))
    slot_cotangent = jnp.transpose(cotangent[0], (1, 0, 2))

    (dense, far_dense, triple1, probs1, contexts1, context1, normed1, scale1,
     triple2, probs2, contexts2, context2, normed2, scale2) = pl.pallas_call(
        functools.partial(forward_kernel, slots, steps),
        grid=(steps,),
        in_specs=[smem, any_spec, item_spec] + [any_spec] * 4 + [fixed(w) for w in (cross_bias, cross_norm, self_bias, self_norm)],
        out_specs=[row_spec, row_spec] + [triple_spec, probs_spec, pair_spec, row_spec, row_spec, scale_spec] * 2,
        out_shape=[row_bf16, row_bf16] + [triple_bf16, probs_bf16, pair_f32, row_bf16, row_f32, scale_f32] * 2,
        scratch_shapes=[
            scratch(size, width, kind=f32), scratch(size, width), stage, stage,
            scratch(steps, slots, TILE, width), *[scratch(items, LANES, kind=jnp.int32)] * 2,
            scratch(width, 3 * width), scratch(width, width), scratch(width, 3 * width), scratch(width, width),
            *semaphores(steps + 1), pltpu.SemaphoreType.DMA((4,)),
        ],
        compiler_params=remote(0),
        cost_estimate=cost(12, 40_000_000),
    )(lengths, slot_rows, slot_rows, cross_proj, cross_out, self_proj, self_out, cross_bias, cross_norm, self_bias, self_norm)

    chunks = deep // width
    half, quarter = width // 2, width // 4
    total = 4 * width + LANES
    (output, grad_attended, up_sum, ffn_sum, down_kept, down_sent, up_kept, up_sent) = pl.pallas_call(
        functools.partial(
            ffn_kernel, slots, steps, digits[:chunk_bits], deep // places, z_digits, share, [(axis, bit, 1 << number) for number, (axis, bit, _) in enumerate(digits[chunk_bits:])]),
        grid=(steps + 1,),
        in_specs=[smem, smem, held(row_spec), held(item_spec), any_spec, any_spec]
        + [fixed(w) for w in (self_norm, up_bias, down_bias, ffn_norm)],
        out_specs=[held(item_spec), held(row_spec), total_of(1, deep), total_of(3, width)]
        + [kept_out(chunks * quarter, width)] * 2 + [kept_out(quarter, deep)] * 2,
        out_shape=[shape_of((slots, items, width), bf16), row_f32, shape_of((1, deep), f32), shape_of((3, width), f32)]
        + [shape_of((chunks * quarter, width), bf16)] * 2 + [shape_of((quarter, deep), bf16)] * 2,
        scratch_shapes=[
            scratch(width, deep), scratch(deep, width), scratch(rows, width), scratch(rows, deep), scratch(rows, width),
            scratch(rows, deep), scratch(size, deep, kind=f32), scratch(size, width, kind=f32), scratch(TILE, LANES, kind=jnp.int32),
            *[scratch(chunks, width, width), scratch(chunks, half, width)] * 2,
            pltpu.SemaphoreType.DMA((2,)), *semaphores(chunks), *semaphores(chunks),
        ],
        compiler_params=remote(1),
        cost_estimate=cost(36, 40_000_000),
    )(lengths, task_flags, normed2, slot_cotangent, ffn_up, ffn_down, self_norm, up_bias, down_bias, ffn_norm)

    grad_crossed, down_half, up_half, self_kept, self_sent = pl.pallas_call(
        functools.partial(self_kernel, slots, steps, digits, z_digits, share),
        grid=(steps + 1,),
        in_specs=[held(spec) for spec in (row_spec, row_spec, scale_spec, row_spec, triple_spec, probs_spec, pair_spec)]
        + [fixed(w) for w in (cross_norm, self_norm, ffn_sum, up_sum)] + [any_spec] * 7,
        out_specs=[held(row_spec), kept_out(chunks * quarter, width), kept_out(quarter, deep)] + [kept_out(quarter, total)] * 2,
        out_shape=[row_f32, shape_of((chunks * quarter, width), bf16), shape_of((quarter, deep), bf16)]
        + [shape_of((quarter, total), bf16)] * 2,
        scratch_shapes=[
            stage, out_stage, scratch(width, 3 * width), scratch(width, width), scratch(rows, width),
            scratch(rows, width), scratch(rows, width), scratch(rows, 3 * width), scratch(LANES, width, kind=f32),
            scratch(5, width, width), scratch(5, half, width),
            scratch(chunks * quarter, width), scratch(chunks * quarter, width), scratch(chunks * quarter // 2, width),
            scratch(quarter, deep), scratch(quarter, deep), scratch(quarter // 2, deep),
            pltpu.SemaphoreType.DMA((5,)), *semaphores(5), *semaphores(8),
        ],
        compiler_params=remote(2),
        cost_estimate=cost(18, 40_000_000),
    )(grad_attended, normed2, scale2, normed1, triple2, probs2, contexts2, cross_norm, self_norm, ffn_sum, up_sum,
      self_proj, self_out, context2, down_kept, down_sent, up_kept, up_sent)

    left = width // 16
    finish = bits == 4
    cross_left = left // 2 if finish else left
    box = total - 2 * (4 * width // 3)
    rest_rows = chunks * quarter // 4
    tails = [(left, total), (cross_left, total)]
    grad_hidden, own_down, own_up, own_self, own_cross = pl.pallas_call(
        functools.partial(cross_kernel, slots, steps, cross_digits, cross_share, finish),
        grid=(steps + 1,),
        in_specs=[held(spec) for spec in (row_spec, row_spec, scale_spec, triple_spec, probs_spec, pair_spec)]
        + [fixed(cross_norm)] + [any_spec] * 9,
        out_specs=[any_spec, kept_out(rest_rows, width), kept_out(left, deep)] + [kept_out(*shape) for shape in tails],
        out_shape=[shape_of((slots, items, width), bf16), shape_of((rest_rows, width), f32), shape_of((left, deep), f32)]
        + [shape_of(shape, f32) for shape in tails],
        scratch_shapes=[
            stage, out_stage, scratch(width, 3 * width), scratch(width, width), scratch(2, rows, width),
            scratch(rows, width), scratch(rows, 3 * width), scratch(rows, width, kind=f32), scratch(LANES, width, kind=f32),
            scratch(steps, slots, TILE, width), scratch(steps, slots, TILE, width), scratch(5, width, width), scratch(5, half, width),
            scratch(width, width, kind=f32),
            scratch(2, 2, 2, left, total), scratch(3, 2, 2, left, box), scratch(3, 2, left, box), scratch(3, left, box),
            scratch(32, total), scratch(32, total),
            scratch(4 * rest_rows, width), scratch(2 * rest_rows, width), scratch(rest_rows, width),
            scratch(4 * left, deep), scratch(2 * left, deep), scratch(left, deep),
            scratch(quarter, total), scratch(quarter, total), scratch(quarter // 2, total), scratch(left, total),
            pltpu.SemaphoreType.DMA((8,)), *semaphores(5), *semaphores(steps), *semaphores(14), *semaphores(12),
            pltpu.SemaphoreType.DMA((steps,)),
        ],
        compiler_params=remote(3),
        cost_estimate=cost(18, 40_000_000),
    )(grad_crossed, normed1, scale1, triple1, probs1, contexts1, cross_norm, cross_proj, cross_out, dense, far_dense, context1,
      down_half, up_half, self_kept, self_sent)

    def sum_rest(total, first):
        for bit in range(first, bits):
            half = total.shape[0] // 2
            total = total[:half].astype(f32) + send(total[half:].astype(bf16), "dp", bit).astype(f32)
        return total

    own_down, own_up = sum_rest(own_down, 4), sum_rest(own_up, 4)
    own_self = sum_rest(own_self, 4)
    own_cross = sum_rest(own_cross, 4 if finish else 3)
    share, cross_share = own_self.shape[0], own_cross.shape[0]
    shapes = [
        (slots, items, width), (slots, items, width), own_down.shape, own_up.shape, (share, 3 * width), (share, width), (3, share), (2, share),
        (1, share), (2, share), (1, deep // places), (cross_share, 3 * width), (cross_share, width), (3, cross_share), (2, cross_share),
    ]
    (output, grad_hidden, own_down, own_up, own_self_proj, own_self_out, self_vectors, self_norms, down_vector, ffn_norms, small_up,
     own_cross_proj, own_cross_out, cross_vectors, cross_norms) = pl.pallas_call(
        unpack_kernel,
        in_specs=[vmem_spec] * 6,
        out_specs=[vmem_spec] * len(shapes),
        out_shape=[shape_of(shape, bf16 if at < 2 else f32) for at, shape in enumerate(shapes)],
        compiler_params=params,
        cost_estimate=cost(0, 10_000_000),
    )(output, grad_hidden, own_down, own_up, own_self, own_cross)
    output, grad_hidden = (jnp.transpose(entry, (1, 0, 2))[None] for entry in (output, grad_hidden))
    return (
        output,
        grad_hidden,
        own_cross_proj,
        cross_vectors,
        cross_norms,
        own_cross_out,
        own_self_proj[None],
        self_vectors[None],
        self_norms[None],
        own_self_out[None],
        own_up[None],
        small_up,
        own_down[None],
        down_vector,
        ffn_norms[None],
    )


def solution(mesh):
    in_specs = (
        P("stream", "dp", None, None),
        P("stream", "dp"),
        P("stream", "dp"),
        P("stream", "dp", None, None),
        P(),
        P(),
        P(),
        P(),
        P("stream", None, None),
        P("stream", None, None),
        P("stream", None, None),
        P("stream", None, None),
        P("stream", None, None),
        P("stream", None),
        P("stream", None, None),
        P("stream", None),
        P("stream", None, None),
    )
    out_specs = (
        P("stream", "dp", None, None),
        P("stream", "dp", None, None),
        P(("stream", "dp"), None),
        P(None, ("stream", "dp")),
        P(None, ("stream", "dp")),
        P(("stream", "dp"), None),
        P("stream", "dp", None),
        P("stream", None, "dp"),
        P("stream", None, "dp"),
        P("stream", "dp", None),
        P("stream", "dp", None),
        P("stream", "dp"),
        P("stream", "dp", None),
        P("stream", "dp"),
        P("stream", None, "dp"),
    )
    return jax.shard_map(local, mesh=mesh, in_specs=in_specs, out_specs=out_specs, check_vma=False)
```

time: 272 us -> 238 us (0.88); the launches traced: 266 us -> 240 us
  Pallas kernels: 212 us -> 236 us
  starting transfers between devices: 13.6 us -> 0 us
  waiting for transfers between devices: 13.1 us -> 0 us
  other arithmetic: 12 us -> 0 us
  local copies, waits for them, and re-layouts: 14.4 us -> 2.53 us
    pallas_call x7 -> x4, Pallas kernels: 166 us -> 194 us  [the longest x1 80.1 us: local(): pl.pallas_call(functools.partial(cross_kernel, slots, steps, cross_digits...]
    ppermute x10 -> x0, starting transfers between devices: 13.6 us -> none  [send(): return lax.ppermute(parts, axis, flip(lax.axis_size(axis), bit))]
    ppermute x10 -> x0, waiting for transfers between devices: 13.1 us -> none  [send(): return lax.ppermute(parts, axis, flip(lax.axis_size(axis), bit))]
    convert_element_type x9 -> x0, other arithmetic: 6.64 us -> none  [the longest x7 4.01 us: add(): return (kept.astype(f32) + got.astype(f32)).astype(bf16)]
    slice x8 -> x0, local copies, waits for them, and re-layouts: 3.82 us -> none  [the longest x1 0.99 us: local(): cross_kept, cross_sent = (cross_rest[:left // 2], cross_rest[left // 2:])]
    broadcast_in_dim x5 -> x0, local copies, waits for them, and re-layouts: 3.47 us -> none  [the longest x1 1.32 us: local(): lens = jnp.broadcast_to(lengths[0][:, None], (items, LANES))]
    unnamed x24 -> x2, local copies, waits for them, and re-layouts: 5.36 us -> 2.53 us
    pallas_call x1, Pallas kernels: 45.5 us -> 42.7 us  [local(): pl.pallas_call(functools.partial(forward_kernel, slots, steps), grid=(ste...]
  transfers between devices with their start and end apart: 10 -> 0, of which waited for: 2 -> 0; matrix products, arithmetic and copies ran while one was open for 5% -> 0% of each run, Pallas kernels for 41% -> 0%
where the time goes in v3:
time: 238 us; the launch traced here: 240 us
  Pallas kernels  236 us (99%)
  local copies, waits for them, and re-layouts  2.53 us (1%)
    pallas_call x1, Pallas kernels, local(): pl.pallas_call(functools.partial(cross_kernel, slots, steps, cross_digits...  80.1 us
    pallas_call x1, Pallas kernels, local(): pl.pallas_call(functools.partial(ffn_kernel, slots, steps, digits[:chunk_...  66.3 us
    pallas_call x1, Pallas kernels, local(): pl.pallas_call(functools.partial(forward_kernel, slots, steps), grid=(ste...  42.7 us
    pallas_call x1, Pallas kernels, local(): pl.pallas_call(functools.partial(self_kernel, slots, steps, digits, z_dig...  42.6 us

profile of v3, /device:TPU:0, one launch (start us, length us, event | category | flops | bytes accessed | tf_op | source)
XLA Modules:
  0.0 239.8 jit_solution(7610854342541949135)
XLA Ops:
  0.6 1.3 copy.32.self_bias
  1.9 42.7 %shard_map.280 = (bf16[864,768]{1,0:T(8,128)(2,1)}, bf16[864,768]{1,0:T(8,128)(2,1)}, bf16[12,80,2304]{2,1,0:T(8,128)(2,1)}, bf16[12,6,160,80]{3,2,1,0:T(8,128)(...) custom-call(s32[1,24]{1,0:T(1,128)} %lengths.3, ...), custom_call_target="tpu_custom_call" | custom-call | flops 12230590464 | bytes 40000000 | tf_op jit(solution)/shard_map/pallas_call | solution.py:930
  44.6 66.3 %shard_map.281 = (bf16[36,24,768]{2,1,0:T(8,128)(2,1)}, f32[864,768]{1,0:T(8,128)}, f32[1,3072]{1,0:T(1,128)}, f32[3,768]{1,0:T(4,128)}, bf16[768,768]{1,0:T(8,1...) custom-call(s32[1,24]{1,0:T(1,128)} %lengths.3, s32[1,24]{1,0:T(1,128)} %flags.1, ...), custom_call_target="tpu_custom_call" | custom-call | flops 36691771392 | bytes 40000000 | tf_op jit(solution)/shard_map/pallas_call | solution.py:949
  110.9 42.6 %shard_map.282 = (f32[864,768]{1,0:T(8,128)}, bf16[768,768]{1,0:T(8,128)(2,1)}, bf16[192,3072]{1,0:T(8,128)(2,1)}, bf16[192,3200]{1,0:T(8,128)(2,1)}, bf16[192,3200]{1,0:T(8,128)(2,1)}) custom-call(f32[864,768]{1,0:T(8,128)} %get-tuple-element.64.grad_attended, f32[864,768]{1,0:T(8,128)} %get-tuple-element.62.normed2, f32[864,1]{1,0:T(8,128)} %get-tuple-element.65.scale2, ...), custom_call_target="tpu_custom_call" | custom-call | flops 18345885696 | bytes 40000000 | tf_op jit(solution)/shard_map/pallas_call | solution.py:969
  153.6 80.1 %shard_map.283 = (bf16[36,24,768]{2,1,0:T(8,128)(2,1)}, f32[192,768]{1,0:T(8,128)}, f32[48,3072]{1,0:T(8,128)}, f32[48,3200]{1,0:T(8,128)}, f32[24,3200]{1,0:T(8,128)}) custom-call(f32[864,768]{1,0:T(8,128)} %get-tuple-element.77.grad_crossed, f32[864,768]{1,0:T(8,128)} %get-tuple-element.66.normed1, f32[864,1]{1,0:T(8,128)} %get-tuple-element.78.scale1, ...), custom_call_target="tpu_custom_call" | custom-call | flops 18345885696 | bytes 40000000 | tf_op jit(solution)/shard_map/pallas_call | solution.py:996
  233.7 4.6 %shard_map.284 = (bf16[36,24,768]{2,1,0:T(8,128)(2,1)}, bf16[36,24,768]{2,1,0:T(8,128)(2,1)}, f32[192,768]{1,0:T(8,128)}, f32[48,3072]{1,0:T(8,128)}, f32[48,230...) custom-call(bf16[36,24,768]{2,1,0:T(8,128)(2,1)} %get-tuple-element., ...), custom_call_target="tpu_custom_call" | custom-call | bytes 10000000 | tf_op jit(solution)/shard_map/pallas_call | solution.py:1037
  238.4 1.2 copy.33
